TPU v7x, 32 devices: a whole 2x2x4 slice. The times are simulated.
32 devices in a mesh: tile: 8 (over z, y), sec: 4 (over x, core).
Axes of the slice: x: 2, y: 2, z: 4, core: 2. Of those that a mesh axis runs over, the one named last changes fastest.
Arguments:
- voltage: float32 [1024, 512], P('tile', 'sec'), may hold values from -6 to 6
- conductance: float32 [1024, 512], P('tile', 'sec'), may hold values from 0.2 to 2
- reversal: float32 [1024, 512], P('tile', 'sec'), may hold values from -1 to 1
- drive: bfloat16 [8, 1024, 512], P(None, 'tile', 'sec'), may hold values from -6 to 6
- inv_cable: float32 [128, 128], replicated, may hold values from -1 to 1
- owner_map: int32 [1024], P('tile'), may hold values from 0 to 7, as said below
- peer_counts: int32 [8, 8], P('tile'), may hold values from 0 to 32, as said below
- pattern: int32 [4, 1024, 2], P('sec', 'tile'), may hold values from 0 to 31, all different within a row
- transfer: bfloat16 [4, 1024, 2, 128, 128], P('sec', 'tile'), may hold values from -0.03125 to 0.03125
Outputs:
- final_voltage: float32 [1024, 512], P('tile', 'sec')
- probe: float32 [8, 4096], P(None, ('tile', 'sec'))
Inputs may be any that keep to these rules, and one draw needn't show every extreme that they name: `owner_map`: every depth tile owns exactly 128 cells; the cells c with c // 128 = u include at most 32 cells of one owner, and exactly 32 of some owner. peer_counts[d, u] is the number of cells c with c // 128 = u and owner_map[c] = d. `pattern`: the 2 contact tiles of one slot and section differ.
All inputs are finite; a program needn't handle non-finite values.
Results may differ from a plain program's by a relative error of at most 0.0029.
Values may be sent and summed in bfloat16 or wider, within the bound.
No kernel may reach another device: no remote copies, remote signals or barrier semaphores. Data moves between devices by JAX's collectives and lax.ppermute only.
A program may use at most 64 MiB of HBM per device.

v0:
```python
import jax
import jax.numpy as jnp
from jax import lax
from jax.sharding import PartitionSpec as P

CONTACTS = 4096


TIME_STEP = 0.25
AXIAL = 2.0


def padded_2(block, sides, width):
    for axis, dim in sides:
        count = lax.axis_size(axis)
        forward = [(i, i + 1) for i in range(count - 1)]
        backward = [(target, source) for source, target in forward]
        low = lax.ppermute(
            lax.slice_in_dim(block, block.shape[dim] - width, None, axis=dim), axis, forward
        )
        high = lax.ppermute(lax.slice_in_dim(block, 0, width, axis=dim), axis, backward)
        block = jnp.concatenate([low, block, high], axis=dim)
    return block


def cable_update(voltage_now, conductance, reversal, drive_now, inv_cable):
    padded = padded_2(voltage_now.astype(jnp.bfloat16), (("sec", 1),), 1).astype(voltage_now.dtype)
    columns = jnp.arange(voltage_now.shape[1], dtype=jnp.int32)
    first_col = (columns == 0).astype(jnp.float32)
    last_col = (columns == voltage_now.shape[1] - 1).astype(jnp.float32)
    boundary = first_col * (padded[:, :-2] - voltage_now) + last_col * (padded[:, 2:] - voltage_now)
    driven = drive_now.astype(jnp.float32)
    right_side = voltage_now * (1.0 - TIME_STEP * conductance) + TIME_STEP * (
        conductance * reversal + driven + AXIAL * boundary
    )
    voltage_next = jnp.einsum("ci,ji->cj", right_side, inv_cable, precision=lax.Precision.HIGHEST)
    current = (conductance * (voltage_next - reversal) - driven).astype(jnp.bfloat16)
    return (voltage_next, current)


def on_device(
    voltage, conductance, reversal, drive, inv_cable, owner_map, peer_counts, pattern, transfer
):
    cell_count = voltage.shape[0]
    seg_width = voltage.shape[1]
    step_count = drive.shape[0]
    tile_count = lax.axis_size("tile")
    section_count = lax.axis_size("sec")
    capacity = 2 * cell_count // tile_count
    owners = jnp.arange(tile_count, dtype=jnp.int32)
    member = (owner_map[:, None] == owners[None, :]).astype(jnp.int32)
    rank_within = jnp.sum(jnp.cumsum(member, axis=0) * member, axis=1) - 1
    placed = owner_map * capacity + rank_within
    source_row = (
        jnp.full((tile_count * capacity,), cell_count, jnp.int32)
        .at[placed]
        .set(jnp.arange(cell_count, dtype=jnp.int32))
    )
    blank_row = jnp.zeros((1, seg_width), jnp.bfloat16)

    def advance_send(voltage_now, drive_now):
        voltage_next, current = cable_update(
            voltage_now, conductance, reversal, drive_now, inv_cable
        )
        outgoing = jnp.take(jnp.concatenate([current, blank_row], axis=0), source_row, axis=0)
        outgoing = outgoing.reshape(tile_count, capacity, seg_width)
        arrived = lax.all_to_all(outgoing, "tile", split_axis=0, concat_axis=0, tiled=True)
        return (voltage_next, arrived)

    final_voltage, arrived = lax.scan(advance_send, voltage, drive)
    received = arrived.reshape(step_count, tile_count * capacity, seg_width)
    counts = peer_counts[0]
    end_rows = jnp.cumsum(counts)
    starts = end_rows - counts
    slot_ids = jnp.arange(cell_count, dtype=jnp.int32)
    source = jnp.sum((end_rows[None, :] <= slot_ids[:, None]).astype(jnp.int32), axis=1)
    offset = jnp.sum(jnp.where(source[:, None] == owners[None, :], starts[None, :], 0), axis=1)
    gather_rows = source * capacity + slot_ids - offset
    ordered = jnp.take(received, gather_rows, axis=1)
    weights = transfer[0]
    layout = pattern[0]
    contact_width = weights.shape[3]
    tile_total = CONTACTS // contact_width
    tile_sums = jnp.einsum("tsi,skic->tskc", ordered, weights, preferred_element_type=jnp.float32)
    select = (layout[:, :, None] == jnp.arange(tile_total, dtype=jnp.int32)[None, None, :]).astype(
        jnp.float32
    )
    partial_sum = jnp.einsum("tskc,skq->tqc", tile_sums, select, precision=lax.Precision.HIGHEST)
    partial_sum = partial_sum.reshape(step_count, tile_total * contact_width)
    summed = lax.psum(partial_sum, ("tile", "sec"))
    share_width = summed.shape[1] // (tile_count * section_count)
    position = lax.axis_index("tile") * section_count + lax.axis_index("sec")
    probe_share = lax.dynamic_slice_in_dim(summed, position * share_width, share_width, 1)
    return (final_voltage, probe_share)


def solution(mesh):
    placed = (
        P("tile", "sec"),
        P("tile", "sec"),
        P("tile", "sec"),
        P(None, "tile", "sec"),
        P(),
        P("tile"),
        P("tile", None),
        P("sec", "tile", None),
        P("sec", "tile", None, None, None),
    )
    return jax.shard_map(
        on_device,
        mesh=mesh,
        in_specs=placed,
        out_specs=(P("tile", "sec"), P(None, ("tile", "sec"))),
        check_vma=False,
    )
```

profile of v0, /device:TPU:0, one launch (start us, length us, event | category | flops | bytes accessed | tf_op | source)
XLA Modules:
  0.0 317.4 jit_solution(17633135514962966802)
XLA Ops:
  14.1 163.4 %while.13 = (s32[]{:T(128)}, f32[128,128]{1,0:T(8,128)S(1)}, bf16[8,8,32,128]{3,2,1,0:T(8,128)(2,1)S(1)}, f32[128,128]{1,0:T(8,128)}, bf16[8,128,128]{2,1,0:T(8,...) while((s32[]{:T(128)}, f32[128,128]{1,0:T(8,128)S(1)}, ...), condition=%wide.region_4.5_spmd, body=%wide.region_3.4_spmd.sunk | while | flops 25629952 | bytes 1626603 | solution.py:70
  14.2 1.3 collective-permute-start
  15.5 3.0 collective-permute-start.1
  22.4 7.3 %all-to-all-start = ((bf16[8,32,128]{2,1,0:T(8,128)(2,1)}), bf16[8,32,128]{2,1,0:T(8,128)(2,1)S(1)}, u32[]{:S(2)}, u32[]{:S(2)}) async-start(bf16[8,32,128]{2,1,0:T(8,128)(2,1)} %broadcast_select_fusion.2), calls=%async_computation | async-start | bytes 131072 | tf_op jit(solution)/shard_map/while/body/eval_jaxpr/all_to_all | solution.py:67
  29.7 7.3 %all-to-all-done = bf16[8,32,128]{2,1,0:T(8,128)(2,1)S(1)} async-done(((bf16[8,32,128]{2,1,0:T(8,128)(2,1)}), bf16[8,32,128]{2,1,0:T(8,128)(2,1)S(1)}, u32[]{:S(2)}, u32[]{:S(2)}) %all-to-all-start) | async-done | bytes 65568 | tf_op jit(solution)/shard_map/while/body/eval_jaxpr/all_to_all | solution.py:67
  38.4 3.0 collective-permute-start.1
  45.3 3.4 %all-to-all-start = ((bf16[8,32,128]{2,1,0:T(8,128)(2,1)}), bf16[8,32,128]{2,1,0:T(8,128)(2,1)S(1)}, u32[]{:S(2)}, u32[]{:S(2)}) async-start(bf16[8,32,128]{2,1,0:T(8,128)(2,1)} %broadcast_select_fusion.2), calls=%async_computation | async-start | bytes 131072 | tf_op jit(solution)/shard_map/while/body/eval_jaxpr/all_to_all | solution.py:67
  48.6 6.8 %all-to-all-done = bf16[8,32,128]{2,1,0:T(8,128)(2,1)S(1)} async-done(((bf16[8,32,128]{2,1,0:T(8,128)(2,1)}), bf16[8,32,128]{2,1,0:T(8,128)(2,1)S(1)}, u32[]{:S(2)}, u32[]{:S(2)}) %all-to-all-start) | async-done | bytes 65568 | tf_op jit(solution)/shard_map/while/body/eval_jaxpr/all_to_all | solution.py:67
  56.9 4.2 %collective-permute-start.1 = (bf16[128,1]{1,0:T(8,128)(2,1)S(1)}, bf16[128,1]{1,0:T(8,128)(2,1)S(1)}, u32[]{:S(2)}, u32[]{:S(2)}) collective-permute-start(bf16[128,1]{1,0:T(8,128)(2,1)S(1)} %get-tuple-element.171), channel_id=1, source_target_pairs={{0,1},{1,2},{2,3},{4,5},{5,6},{6,7},{8,9},{9,10},{10,11},{12,13},{... | collective-permute-start | bytes 776 | tf_op jit(solution)/shard_map/while/body/eval_jaxpr/ppermute | solution.py:18
  65.0 3.4 %all-to-all-start = ((bf16[8,32,128]{2,1,0:T(8,128)(2,1)}), bf16[8,32,128]{2,1,0:T(8,128)(2,1)S(1)}, u32[]{:S(2)}, u32[]{:S(2)}) async-start(bf16[8,32,128]{2,1,0:T(8,128)(2,1)} %broadcast_select_fusion.2), calls=%async_computation | async-start | bytes 131072 | tf_op jit(solution)/shard_map/while/body/eval_jaxpr/all_to_all | solution.py:67
  68.3 6.8 %all-to-all-done = bf16[8,32,128]{2,1,0:T(8,128)(2,1)S(1)} async-done(((bf16[8,32,128]{2,1,0:T(8,128)(2,1)}), bf16[8,32,128]{2,1,0:T(8,128)(2,1)S(1)}, u32[]{:S(2)}, u32[]{:S(2)}) %all-to-all-start) | async-done | bytes 65568 | tf_op jit(solution)/shard_map/while/body/eval_jaxpr/all_to_all | solution.py:67
  76.6 5.0 %collective-permute-start.1 = (bf16[128,1]{1,0:T(8,128)(2,1)S(1)}, bf16[128,1]{1,0:T(8,128)(2,1)S(1)}, u32[]{:S(2)}, u32[]{:S(2)}) collective-permute-start(bf16[128,1]{1,0:T(8,128)(2,1)S(1)} %get-tuple-element.171), channel_id=1, source_target_pairs={{0,1},{1,2},{2,3},{4,5},{5,6},{6,7},{8,9},{9,10},{10,11},{12,13},{... | collective-permute-start | bytes 776 | tf_op jit(solution)/shard_map/while/body/eval_jaxpr/ppermute | solution.py:18
  85.4 3.4 %all-to-all-start = ((bf16[8,32,128]{2,1,0:T(8,128)(2,1)}), bf16[8,32,128]{2,1,0:T(8,128)(2,1)S(1)}, u32[]{:S(2)}, u32[]{:S(2)}) async-start(bf16[8,32,128]{2,1,0:T(8,128)(2,1)} %broadcast_select_fusion.2), calls=%async_computation | async-start | bytes 131072 | tf_op jit(solution)/shard_map/while/body/eval_jaxpr/all_to_all | solution.py:67
  88.8 6.8 %all-to-all-done = bf16[8,32,128]{2,1,0:T(8,128)(2,1)S(1)} async-done(((bf16[8,32,128]{2,1,0:T(8,128)(2,1)}), bf16[8,32,128]{2,1,0:T(8,128)(2,1)S(1)}, u32[]{:S(2)}, u32[]{:S(2)}) %all-to-all-start) | async-done | bytes 65568 | tf_op jit(solution)/shard_map/while/body/eval_jaxpr/all_to_all | solution.py:67
  95.8 1.3 collective-permute-start
  97.1 5.0 %collective-permute-start.1 = (bf16[128,1]{1,0:T(8,128)(2,1)S(1)}, bf16[128,1]{1,0:T(8,128)(2,1)S(1)}, u32[]{:S(2)}, u32[]{:S(2)}) collective-permute-start(bf16[128,1]{1,0:T(8,128)(2,1)S(1)} %get-tuple-element.171), channel_id=1, source_target_pairs={{0,1},{1,2},{2,3},{4,5},{5,6},{6,7},{8,9},{9,10},{10,11},{12,13},{... | collective-permute-start | bytes 776 | tf_op jit(solution)/shard_map/while/body/eval_jaxpr/ppermute | solution.py:18
  105.9 3.4 %all-to-all-start = ((bf16[8,32,128]{2,1,0:T(8,128)(2,1)}), bf16[8,32,128]{2,1,0:T(8,128)(2,1)S(1)}, u32[]{:S(2)}, u32[]{:S(2)}) async-start(bf16[8,32,128]{2,1,0:T(8,128)(2,1)} %broadcast_select_fusion.2), calls=%async_computation | async-start | bytes 131072 | tf_op jit(solution)/shard_map/while/body/eval_jaxpr/all_to_all | solution.py:67
  109.3 6.8 %all-to-all-done = bf16[8,32,128]{2,1,0:T(8,128)(2,1)S(1)} async-done(((bf16[8,32,128]{2,1,0:T(8,128)(2,1)}), bf16[8,32,128]{2,1,0:T(8,128)(2,1)S(1)}, u32[]{:S(2)}, u32[]{:S(2)}) %all-to-all-start) | async-done | bytes 65568 | tf_op jit(solution)/shard_map/while/body/eval_jaxpr/all_to_all | solution.py:67
  116.2 1.3 collective-permute-start
  117.5 5.0 %collective-permute-start.1 = (bf16[128,1]{1,0:T(8,128)(2,1)S(1)}, bf16[128,1]{1,0:T(8,128)(2,1)S(1)}, u32[]{:S(2)}, u32[]{:S(2)}) collective-permute-start(bf16[128,1]{1,0:T(8,128)(2,1)S(1)} %get-tuple-element.171), channel_id=1, source_target_pairs={{0,1},{1,2},{2,3},{4,5},{5,6},{6,7},{8,9},{9,10},{10,11},{12,13},{... | collective-permute-start | bytes 776 | tf_op jit(solution)/shard_map/while/body/eval_jaxpr/ppermute | solution.py:18
  126.4 3.4 %all-to-all-start = ((bf16[8,32,128]{2,1,0:T(8,128)(2,1)}), bf16[8,32,128]{2,1,0:T(8,128)(2,1)S(1)}, u32[]{:S(2)}, u32[]{:S(2)}) async-start(bf16[8,32,128]{2,1,0:T(8,128)(2,1)} %broadcast_select_fusion.2), calls=%async_computation | async-start | bytes 131072 | tf_op jit(solution)/shard_map/while/body/eval_jaxpr/all_to_all | solution.py:67
  129.7 6.8 %all-to-all-done = bf16[8,32,128]{2,1,0:T(8,128)(2,1)S(1)} async-done(((bf16[8,32,128]{2,1,0:T(8,128)(2,1)}), bf16[8,32,128]{2,1,0:T(8,128)(2,1)S(1)}, u32[]{:S(2)}, u32[]{:S(2)}) %all-to-all-start) | async-done | bytes 65568 | tf_op jit(solution)/shard_map/while/body/eval_jaxpr/all_to_all | solution.py:67
  136.7 1.3 collective-permute-start
  138.0 5.0 %collective-permute-start.1 = (bf16[128,1]{1,0:T(8,128)(2,1)S(1)}, bf16[128,1]{1,0:T(8,128)(2,1)S(1)}, u32[]{:S(2)}, u32[]{:S(2)}) collective-permute-start(bf16[128,1]{1,0:T(8,128)(2,1)S(1)} %get-tuple-element.171), channel_id=1, source_target_pairs={{0,1},{1,2},{2,3},{4,5},{5,6},{6,7},{8,9},{9,10},{10,11},{12,13},{... | collective-permute-start | bytes 776 | tf_op jit(solution)/shard_map/while/body/eval_jaxpr/ppermute | solution.py:18
  146.8 3.4 %all-to-all-start = ((bf16[8,32,128]{2,1,0:T(8,128)(2,1)}), bf16[8,32,128]{2,1,0:T(8,128)(2,1)S(1)}, u32[]{:S(2)}, u32[]{:S(2)}) async-start(bf16[8,32,128]{2,1,0:T(8,128)(2,1)} %broadcast_select_fusion.2), calls=%async_computation | async-start | bytes 131072 | tf_op jit(solution)/shard_map/while/body/eval_jaxpr/all_to_all | solution.py:67
  150.2 6.8 %all-to-all-done = bf16[8,32,128]{2,1,0:T(8,128)(2,1)S(1)} async-done(((bf16[8,32,128]{2,1,0:T(8,128)(2,1)}), bf16[8,32,128]{2,1,0:T(8,128)(2,1)S(1)}, u32[]{:S(2)}, u32[]{:S(2)}) %all-to-all-start) | async-done | bytes 65568 | tf_op jit(solution)/shard_map/while/body/eval_jaxpr/all_to_all | solution.py:67
  157.2 1.3 collective-permute-start
  158.5 5.0 %collective-permute-start.1 = (bf16[128,1]{1,0:T(8,128)(2,1)S(1)}, bf16[128,1]{1,0:T(8,128)(2,1)S(1)}, u32[]{:S(2)}, u32[]{:S(2)}) collective-permute-start(bf16[128,1]{1,0:T(8,128)(2,1)S(1)} %get-tuple-element.171), channel_id=1, source_target_pairs={{0,1},{1,2},{2,3},{4,5},{5,6},{6,7},{8,9},{9,10},{10,11},{12,13},{... | collective-permute-start | bytes 776 | tf_op jit(solution)/shard_map/while/body/eval_jaxpr/ppermute | solution.py:18
  167.3 3.4 %all-to-all-start = ((bf16[8,32,128]{2,1,0:T(8,128)(2,1)}), bf16[8,32,128]{2,1,0:T(8,128)(2,1)S(1)}, u32[]{:S(2)}, u32[]{:S(2)}) async-start(bf16[8,32,128]{2,1,0:T(8,128)(2,1)} %broadcast_select_fusion.2), calls=%async_computation | async-start | bytes 131072 | tf_op jit(solution)/shard_map/while/body/eval_jaxpr/all_to_all | solution.py:67
  170.7 6.8 %all-to-all-done = bf16[8,32,128]{2,1,0:T(8,128)(2,1)S(1)} async-done(((bf16[8,32,128]{2,1,0:T(8,128)(2,1)}), bf16[8,32,128]{2,1,0:T(8,128)(2,1)S(1)}, u32[]{:S(2)}, u32[]{:S(2)}) %all-to-all-start) | async-done | bytes 65568 | tf_op jit(solution)/shard_map/while/body/eval_jaxpr/all_to_all | solution.py:67
  178.6 4.6 %fusion.28 = f32[8,128,2,128]{3,0,2,1:T(8,128)S(1)} fusion(bf16[1,128,2,128,128]{4,3,2,1,0:T(8,128)(2,1)} %param.19, bf16[128,8,128]{2,1,0:T(8,128)(2,1)S(1)} %gather_fusion.1, pred[128]{0:T(512)(128)(4,1)S(1)} %compare_and_fusion.1), kind=kOutput, calls=%fused_computation.41 | convolution fusion | flops 67239936 | bytes 9699456 | tf_op jit(solution)/shard_map/tsi,skic->tskc/dot_general | solution.py:84
  184.8 124.4 %all-reduce.3.cloned.1.call-done = f32[8,4096]{1,0:T(8,128)} async-done(((f32[8,4096]{1,0:T(8,128)}), f32[8,4096]{1,0:T(8,128)}) %all-reduce.3.cloned.1.call-update) | async-done | bytes 131088 | tf_op jit(solution)/shard_map/psum | solution.py:90
  (158 shorter events, 45.7 us)
Async XLA Ops:
  7.2 302.1 %all-reduce.3.cloned.1.call-start = ((), (), s32[]{:S(2)}) async-start(), calls=%async_computation.1 | async-start | bytes 262144 | tf_op jit(solution)/shard_map/psum | solution.py:90
  14.2 4.4 %collective-permute-start = (bf16[128,1]{1,0:T(8,128)(2,1)S(1)}, bf16[128,1]{1,0:T(8,128)(2,1)S(1)}, u32[]{:S(2)}, u32[]{:S(2)}) collective-permute-start(bf16[128,1]{1,0:T(8,128)(2,1)S(1)} %get-tuple-element.170), channel_id=1, source_target_pairs={{1,0},{2,1},{3,2},{5,4},{6,5},{7,6},{9,8},{10,9},{11,10},{13,12},{... | collective-permute-start | bytes 776 | tf_op jit(solution)/shard_map/while/body/eval_jaxpr/ppermute | solution.py:21
  15.5 3.9 %collective-permute-start.1 = (bf16[128,1]{1,0:T(8,128)(2,1)S(1)}, bf16[128,1]{1,0:T(8,128)(2,1)S(1)}, u32[]{:S(2)}, u32[]{:S(2)}) collective-permute-start(bf16[128,1]{1,0:T(8,128)(2,1)S(1)} %get-tuple-element.171), channel_id=1, source_target_pairs={{0,1},{1,2},{2,3},{4,5},{5,6},{6,7},{8,9},{9,10},{10,11},{12,13},{... | collective-permute-start | bytes 776 | tf_op jit(solution)/shard_map/while/body/eval_jaxpr/ppermute | solution.py:18
  22.4 14.6 %all-to-all-start = ((bf16[8,32,128]{2,1,0:T(8,128)(2,1)}), bf16[8,32,128]{2,1,0:T(8,128)(2,1)S(1)}, u32[]{:S(2)}, u32[]{:S(2)}) async-start(bf16[8,32,128]{2,1,0:T(8,128)(2,1)} %broadcast_select_fusion.2), calls=%async_computation | async-start | bytes 131072 | tf_op jit(solution)/shard_map/while/body/eval_jaxpr/all_to_all | solution.py:67
  37.1 4.4 %collective-permute-start = (bf16[128,1]{1,0:T(8,128)(2,1)S(1)}, bf16[128,1]{1,0:T(8,128)(2,1)S(1)}, u32[]{:S(2)}, u32[]{:S(2)}) collective-permute-start(bf16[128,1]{1,0:T(8,128)(2,1)S(1)} %get-tuple-element.170), channel_id=1, source_target_pairs={{1,0},{2,1},{3,2},{5,4},{6,5},{7,6},{9,8},{10,9},{11,10},{13,12},{... | collective-permute-start | bytes 776 | tf_op jit(solution)/shard_map/while/body/eval_jaxpr/ppermute | solution.py:21
  38.4 3.9 %collective-permute-start.1 = (bf16[128,1]{1,0:T(8,128)(2,1)S(1)}, bf16[128,1]{1,0:T(8,128)(2,1)S(1)}, u32[]{:S(2)}, u32[]{:S(2)}) collective-permute-start(bf16[128,1]{1,0:T(8,128)(2,1)S(1)} %get-tuple-element.171), channel_id=1, source_target_pairs={{0,1},{1,2},{2,3},{4,5},{5,6},{6,7},{8,9},{9,10},{10,11},{12,13},{... | collective-permute-start | bytes 776 | tf_op jit(solution)/shard_map/while/body/eval_jaxpr/ppermute | solution.py:18
  45.3 10.2 %all-to-all-start = ((bf16[8,32,128]{2,1,0:T(8,128)(2,1)}), bf16[8,32,128]{2,1,0:T(8,128)(2,1)S(1)}, u32[]{:S(2)}, u32[]{:S(2)}) async-start(bf16[8,32,128]{2,1,0:T(8,128)(2,1)} %broadcast_select_fusion.2), calls=%async_computation | async-start | bytes 131072 | tf_op jit(solution)/shard_map/while/body/eval_jaxpr/all_to_all | solution.py:67
  55.6 5.6 %collective-permute-start = (bf16[128,1]{1,0:T(8,128)(2,1)S(1)}, bf16[128,1]{1,0:T(8,128)(2,1)S(1)}, u32[]{:S(2)}, u32[]{:S(2)}) collective-permute-start(bf16[128,1]{1,0:T(8,128)(2,1)S(1)} %get-tuple-element.170), channel_id=1, source_target_pairs={{1,0},{2,1},{3,2},{5,4},{6,5},{7,6},{9,8},{10,9},{11,10},{13,12},{... | collective-permute-start | bytes 776 | tf_op jit(solution)/shard_map/while/body/eval_jaxpr/ppermute | solution.py:21
  56.9 5.1 %collective-permute-start.1 = (bf16[128,1]{1,0:T(8,128)(2,1)S(1)}, bf16[128,1]{1,0:T(8,128)(2,1)S(1)}, u32[]{:S(2)}, u32[]{:S(2)}) collective-permute-start(bf16[128,1]{1,0:T(8,128)(2,1)S(1)} %get-tuple-element.171), channel_id=1, source_target_pairs={{0,1},{1,2},{2,3},{4,5},{5,6},{6,7},{8,9},{9,10},{10,11},{12,13},{... | collective-permute-start | bytes 776 | tf_op jit(solution)/shard_map/while/body/eval_jaxpr/ppermute | solution.py:18
  65.0 10.2 %all-to-all-start = ((bf16[8,32,128]{2,1,0:T(8,128)(2,1)}), bf16[8,32,128]{2,1,0:T(8,128)(2,1)S(1)}, u32[]{:S(2)}, u32[]{:S(2)}) async-start(bf16[8,32,128]{2,1,0:T(8,128)(2,1)} %broadcast_select_fusion.2), calls=%async_computation | async-start | bytes 131072 | tf_op jit(solution)/shard_map/while/body/eval_jaxpr/all_to_all | solution.py:67
  75.3 6.4 %collective-permute-start = (bf16[128,1]{1,0:T(8,128)(2,1)S(1)}, bf16[128,1]{1,0:T(8,128)(2,1)S(1)}, u32[]{:S(2)}, u32[]{:S(2)}) collective-permute-start(bf16[128,1]{1,0:T(8,128)(2,1)S(1)} %get-tuple-element.170), channel_id=1, source_target_pairs={{1,0},{2,1},{3,2},{5,4},{6,5},{7,6},{9,8},{10,9},{11,10},{13,12},{... | collective-permute-start | bytes 776 | tf_op jit(solution)/shard_map/while/body/eval_jaxpr/ppermute | solution.py:21
  76.6 5.9 %collective-permute-start.1 = (bf16[128,1]{1,0:T(8,128)(2,1)S(1)}, bf16[128,1]{1,0:T(8,128)(2,1)S(1)}, u32[]{:S(2)}, u32[]{:S(2)}) collective-permute-start(bf16[128,1]{1,0:T(8,128)(2,1)S(1)} %get-tuple-element.171), channel_id=1, source_target_pairs={{0,1},{1,2},{2,3},{4,5},{5,6},{6,7},{8,9},{9,10},{10,11},{12,13},{... | collective-permute-start | bytes 776 | tf_op jit(solution)/shard_map/while/body/eval_jaxpr/ppermute | solution.py:18
  85.4 10.2 %all-to-all-start = ((bf16[8,32,128]{2,1,0:T(8,128)(2,1)}), bf16[8,32,128]{2,1,0:T(8,128)(2,1)S(1)}, u32[]{:S(2)}, u32[]{:S(2)}) async-start(bf16[8,32,128]{2,1,0:T(8,128)(2,1)} %broadcast_select_fusion.2), calls=%async_computation | async-start | bytes 131072 | tf_op jit(solution)/shard_map/while/body/eval_jaxpr/all_to_all | solution.py:67
  95.8 6.4 %collective-permute-start = (bf16[128,1]{1,0:T(8,128)(2,1)S(1)}, bf16[128,1]{1,0:T(8,128)(2,1)S(1)}, u32[]{:S(2)}, u32[]{:S(2)}) collective-permute-start(bf16[128,1]{1,0:T(8,128)(2,1)S(1)} %get-tuple-element.170), channel_id=1, source_target_pairs={{1,0},{2,1},{3,2},{5,4},{6,5},{7,6},{9,8},{10,9},{11,10},{13,12},{... | collective-permute-start | bytes 776 | tf_op jit(solution)/shard_map/while/body/eval_jaxpr/ppermute | solution.py:21
  97.1 5.9 %collective-permute-start.1 = (bf16[128,1]{1,0:T(8,128)(2,1)S(1)}, bf16[128,1]{1,0:T(8,128)(2,1)S(1)}, u32[]{:S(2)}, u32[]{:S(2)}) collective-permute-start(bf16[128,1]{1,0:T(8,128)(2,1)S(1)} %get-tuple-element.171), channel_id=1, source_target_pairs={{0,1},{1,2},{2,3},{4,5},{5,6},{6,7},{8,9},{9,10},{10,11},{12,13},{... | collective-permute-start | bytes 776 | tf_op jit(solution)/shard_map/while/body/eval_jaxpr/ppermute | solution.py:18
  105.9 10.2 %all-to-all-start = ((bf16[8,32,128]{2,1,0:T(8,128)(2,1)}), bf16[8,32,128]{2,1,0:T(8,128)(2,1)S(1)}, u32[]{:S(2)}, u32[]{:S(2)}) async-start(bf16[8,32,128]{2,1,0:T(8,128)(2,1)} %broadcast_select_fusion.2), calls=%async_computation | async-start | bytes 131072 | tf_op jit(solution)/shard_map/while/body/eval_jaxpr/all_to_all | solution.py:67
  116.2 6.4 %collective-permute-start = (bf16[128,1]{1,0:T(8,128)(2,1)S(1)}, bf16[128,1]{1,0:T(8,128)(2,1)S(1)}, u32[]{:S(2)}, u32[]{:S(2)}) collective-permute-start(bf16[128,1]{1,0:T(8,128)(2,1)S(1)} %get-tuple-element.170), channel_id=1, source_target_pairs={{1,0},{2,1},{3,2},{5,4},{6,5},{7,6},{9,8},{10,9},{11,10},{13,12},{... | collective-permute-start | bytes 776 | tf_op jit(solution)/shard_map/while/body/eval_jaxpr/ppermute | solution.py:21
  117.5 5.9 %collective-permute-start.1 = (bf16[128,1]{1,0:T(8,128)(2,1)S(1)}, bf16[128,1]{1,0:T(8,128)(2,1)S(1)}, u32[]{:S(2)}, u32[]{:S(2)}) collective-permute-start(bf16[128,1]{1,0:T(8,128)(2,1)S(1)} %get-tuple-element.171), channel_id=1, source_target_pairs={{0,1},{1,2},{2,3},{4,5},{5,6},{6,7},{8,9},{9,10},{10,11},{12,13},{... | collective-permute-start | bytes 776 | tf_op jit(solution)/shard_map/while/body/eval_jaxpr/ppermute | solution.py:18
  126.4 10.2 %all-to-all-start = ((bf16[8,32,128]{2,1,0:T(8,128)(2,1)}), bf16[8,32,128]{2,1,0:T(8,128)(2,1)S(1)}, u32[]{:S(2)}, u32[]{:S(2)}) async-start(bf16[8,32,128]{2,1,0:T(8,128)(2,1)} %broadcast_select_fusion.2), calls=%async_computation | async-start | bytes 131072 | tf_op jit(solution)/shard_map/while/body/eval_jaxpr/all_to_all | solution.py:67
  136.7 6.4 %collective-permute-start = (bf16[128,1]{1,0:T(8,128)(2,1)S(1)}, bf16[128,1]{1,0:T(8,128)(2,1)S(1)}, u32[]{:S(2)}, u32[]{:S(2)}) collective-permute-start(bf16[128,1]{1,0:T(8,128)(2,1)S(1)} %get-tuple-element.170), channel_id=1, source_target_pairs={{1,0},{2,1},{3,2},{5,4},{6,5},{7,6},{9,8},{10,9},{11,10},{13,12},{... | collective-permute-start | bytes 776 | tf_op jit(solution)/shard_map/while/body/eval_jaxpr/ppermute | solution.py:21
  138.0 5.9 %collective-permute-start.1 = (bf16[128,1]{1,0:T(8,128)(2,1)S(1)}, bf16[128,1]{1,0:T(8,128)(2,1)S(1)}, u32[]{:S(2)}, u32[]{:S(2)}) collective-permute-start(bf16[128,1]{1,0:T(8,128)(2,1)S(1)} %get-tuple-element.171), channel_id=1, source_target_pairs={{0,1},{1,2},{2,3},{4,5},{5,6},{6,7},{8,9},{9,10},{10,11},{12,13},{... | collective-permute-start | bytes 776 | tf_op jit(solution)/shard_map/while/body/eval_jaxpr/ppermute | solution.py:18
  146.8 10.2 %all-to-all-start = ((bf16[8,32,128]{2,1,0:T(8,128)(2,1)}), bf16[8,32,128]{2,1,0:T(8,128)(2,1)S(1)}, u32[]{:S(2)}, u32[]{:S(2)}) async-start(bf16[8,32,128]{2,1,0:T(8,128)(2,1)} %broadcast_select_fusion.2), calls=%async_computation | async-start | bytes 131072 | tf_op jit(solution)/shard_map/while/body/eval_jaxpr/all_to_all | solution.py:67
  157.2 6.4 %collective-permute-start = (bf16[128,1]{1,0:T(8,128)(2,1)S(1)}, bf16[128,1]{1,0:T(8,128)(2,1)S(1)}, u32[]{:S(2)}, u32[]{:S(2)}) collective-permute-start(bf16[128,1]{1,0:T(8,128)(2,1)S(1)} %get-tuple-element.170), channel_id=1, source_target_pairs={{1,0},{2,1},{3,2},{5,4},{6,5},{7,6},{9,8},{10,9},{11,10},{13,12},{... | collective-permute-start | bytes 776 | tf_op jit(solution)/shard_map/while/body/eval_jaxpr/ppermute | solution.py:21
  158.5 5.9 %collective-permute-start.1 = (bf16[128,1]{1,0:T(8,128)(2,1)S(1)}, bf16[128,1]{1,0:T(8,128)(2,1)S(1)}, u32[]{:S(2)}, u32[]{:S(2)}) collective-permute-start(bf16[128,1]{1,0:T(8,128)(2,1)S(1)} %get-tuple-element.171), channel_id=1, source_target_pairs={{0,1},{1,2},{2,3},{4,5},{5,6},{6,7},{8,9},{9,10},{10,11},{12,13},{... | collective-permute-start | bytes 776 | tf_op jit(solution)/shard_map/while/body/eval_jaxpr/ppermute | solution.py:18
  167.3 10.2 %all-to-all-start = ((bf16[8,32,128]{2,1,0:T(8,128)(2,1)}), bf16[8,32,128]{2,1,0:T(8,128)(2,1)S(1)}, u32[]{:S(2)}, u32[]{:S(2)}) async-start(bf16[8,32,128]{2,1,0:T(8,128)(2,1)} %broadcast_select_fusion.2), calls=%async_computation | async-start | bytes 131072 | tf_op jit(solution)/shard_map/while/body/eval_jaxpr/all_to_all | solution.py:67
  177.5 133.0 %copy-start = (f32[128,128]{1,0:T(8,128)}, f32[128,128]{1,0:T(8,128)S(1)}, u32[]{:S(2)}) copy-start(f32[128,128]{1,0:T(8,128)S(1)} %get-tuple-element.81) | copy-start | bytes 196612
  177.6 5.7 %copy-start.1 = (s32[1,128,2]{1,2,0:T(2,128)S(1)}, s32[1,128,2]{1,2,0:T(2,128)}, u32[]{:S(2)}) copy-start(s32[1,128,2]{1,2,0:T(2,128)} %param.18) | copy-start | bytes 3076
Sparse Core Ops, SparseCore 0:
  184.9 124.2 all-reduce.2
where the time goes:
time: 319 us; the launch traced here: 317 us
  waiting for transfers between devices  185 us (58%)
  starting transfers between devices  76.4 us (24%)
  matrix products  15.6 us (5%)
  between operations  14.1 us (4%)
  local copies, waits for them, and re-layouts  13.2 us (4%)
  other arithmetic  11.9 us (4%)
    psum x1, waiting for transfers between devices, on_device(): summed = lax.psum(partial_sum, ('tile', 'sec'))  124 us
    all_to_all x8, waiting for transfers between devices, advance_send(): lax.all_to_all(outgoing, 'tile', split_axis=0, concat_axis=0, tiled=True)  55.2 us
    ppermute x8, starting transfers between devices, padded_2(): lax.ppermute(lax.slice_in_dim(block, block.shape[dim] - width, None, axis...  35.4 us
    all_to_all x8, starting transfers between devices, advance_send(): lax.all_to_all(outgoing, 'tile', split_axis=0, concat_axis=0, tiled=True)  30.7 us
    ppermute x8, starting transfers between devices, padded_2(): lax.ppermute(lax.slice_in_dim(block, 0, width, axis=dim), axis, backward)  10.3 us
    dot_general x8, matrix products, cable_update(): jnp.einsum('ci,ji->cj', right_side, inv_cable, precision=lax.Precision.HI...  10.2 us
    gather x8, local copies, waits for them, and re-layouts, advance_send(): jnp.take(jnp.concatenate([current, blank_row], axis=0), source_row, axis=0)  6.84 us
  transfers between devices with their start and end apart: 25, of which 17 were waited for; matrix products, arithmetic and copies ran while one was open for 0% of the time, Pallas kernels for 0%

commit v1 on v0

v1 whole, which is shorter than its diff:
```python
import functools

import jax
import jax.numpy as jnp
from jax import lax
from jax.experimental import pallas as pl
from jax.experimental.pallas import tpu as pltpu
from jax.sharding import PartitionSpec as P

CONTACTS = 4096
TIME_STEP = 0.25
AXIAL = 2.0
END_ROWS = 48
BF = jnp.bfloat16
F32 = jnp.float32


def split_hi_lo(x):
    hi = x.astype(BF)
    return hi, (x - hi.astype(F32)).astype(BF)


def local_kernel(v_ref, g_ref, e_ref, drive_ref, cable_ref, vloc_ref, resp_ref, ends_ref):
    cells, width = v_ref.shape
    steps = drive_ref.shape[0]
    cond = g_ref[...]
    lane = lax.broadcasted_iota(jnp.int32, (cells, width), 1)
    at_end = jnp.where((lane == 0) | (lane == width - 1), TIME_STEP * AXIAL, 0.0).astype(F32)
    keep = 1.0 - TIME_STEP * cond - at_end
    source = TIME_STEP * cond * e_ref[...]
    cable = cable_ref[...].T
    cable_hi, cable_lo = split_hi_lo(cable)
    half = jnp.concatenate([cable_hi, cable_lo], axis=1)
    weights = jnp.concatenate([half, half], axis=0)
    pick_row = lax.broadcasted_iota(jnp.int32, (16, width), 0)
    pick_lane = lax.broadcasted_iota(jnp.int32, (16, width), 1)
    pick = jnp.where(
        ((pick_row == 0) & (pick_lane == 0)) | ((pick_row == 1) & (pick_lane == width - 1)),
        1.0,
        0.0,
    ).astype(BF)

    def solve(rhs):
        hi, lo = split_hi_lo(rhs)
        both = jnp.dot(jnp.concatenate([hi, lo], axis=1), weights, preferred_element_type=F32)
        return both[:, :width] + both[:, width:]

    def ends_of(x):
        return lax.dot_general(
            pick, x.astype(BF), (((1,), (1,)), ((), ())), preferred_element_type=F32
        )[0:2]

    voltage = v_ref[...]
    lag_left = jnp.broadcast_to(TIME_STEP * AXIAL * cable[0:1, :], (cells, width))
    lag_right = jnp.broadcast_to(TIME_STEP * AXIAL * cable[width - 1 : width, :], (cells, width))
    keep2 = jnp.concatenate([keep, keep], axis=0)
    resp = jnp.concatenate([lag_left, lag_right], axis=0)
    v_ends, l_ends, r_ends = [ends_of(voltage)], [], []
    both_ends = ends_of(resp)
    l_ends.append(both_ends[:, :cells])
    r_ends.append(both_ends[:, cells:])
    for k in range(steps):
        rhs = voltage * keep + source + TIME_STEP * drive_ref[k].astype(F32)
        if k < steps - 1:
            out = solve(jnp.concatenate([rhs, resp * keep2], axis=0))
            voltage, resp = out[:cells], out[cells:]
            resp_ref[k] = resp
            v_ends.append(ends_of(voltage))
            if k < steps - 2:
                both_ends = ends_of(resp)
                l_ends.append(both_ends[:, :cells])
                r_ends.append(both_ends[:, cells:])
        else:
            voltage = solve(rhs)
        vloc_ref[k] = voltage
    rows = v_ends + l_ends + r_ends
    rows.append(jnp.zeros((END_ROWS - 2 * len(rows), cells), F32))
    ends_ref[...] = jnp.concatenate(rows, axis=0).astype(BF)


def couple_kernel(
    tiles,
    sec_ref,
    ends_ref,
    vloc_ref,
    resp_ref,
    g_ref,
    e_ref,
    drive_ref,
    cable_ref,
    owner_ref,
    final_ref,
    out_ref,
    ends32,
    incoming,
    leak,
):
    steps, cells, width = drive_ref.shape
    sections = ends_ref.shape[0]
    ends32[...] = ends_ref[...].astype(F32)

    def rows(q):
        return ends32[:, q, :]

    base_l, base_r = 2 * steps, 4 * steps - 2
    left_a = [None] + [rows(base_l + 2 * l) for l in range(steps - 1)]
    left_b = [None] + [rows(base_l + 2 * l + 1) for l in range(steps - 1)]
    right_a = [None] + [rows(base_r + 2 * l) for l in range(steps - 1)]
    right_b = [None] + [rows(base_r + 2 * l + 1) for l in range(steps - 1)]
    zero = jnp.zeros((1, cells), F32)
    from_left, from_right = [], []
    for k in range(steps):
        first, last = rows(2 * k), rows(2 * k + 1)
        for j in range(k):
            first = first + (left_a[k - j] * from_left[j] + right_a[k - j] * from_right[j])
            last = last + (left_b[k - j] * from_left[j] + right_b[k - j] * from_right[j])
        from_left.append(jnp.concatenate([zero, last[:-1]], axis=0))
        from_right.append(jnp.concatenate([first[1:], zero], axis=0))
    mine = lax.broadcasted_iota(jnp.int32, (sections, cells), 0) == sec_ref[0]
    for j in range(steps):
        incoming[pl.ds(2 * j, 1), :] = jnp.sum(
            jnp.where(mine, from_left[j], 0.0), axis=0, keepdims=True
        )
        incoming[pl.ds(2 * j + 1, 1), :] = jnp.sum(
            jnp.where(mine, from_right[j], 0.0), axis=0, keepdims=True
        )
    by_cell = incoming[...].T

    cable = cable_ref[...].T
    block = 8
    lag_left = jnp.broadcast_to(TIME_STEP * AXIAL * cable[0:1, :], (block, width))
    lag_right = jnp.broadcast_to(TIME_STEP * AXIAL * cable[width - 1 : width, :], (block, width))
    for c in range(0, cells, block):
        span = slice(c, c + block)
        unit = [
            jnp.broadcast_to(by_cell[span, q : q + 1], (block, width)) for q in range(2 * steps)
        ]
        lefts = [None, lag_left] + [resp_ref[l, span, :] for l in range(steps - 1)]
        rights = [None, lag_right] + [
            resp_ref[l, cells + c : cells + c + block, :] for l in range(steps - 1)
        ]
        cond, rev = g_ref[span, :], e_ref[span, :]
        for k in range(1, steps + 1):
            total = vloc_ref[k - 1, span, :]
            for j in range(k):
                total = total + (unit[2 * j] * lefts[k - j] + unit[2 * j + 1] * rights[k - j])
            leak[k - 1, span, :] = cond * (total - rev)
        final_ref[span, :] = total

    capacity = out_ref.shape[0] // tiles
    owner = owner_ref[...]
    member = owner == lax.broadcasted_iota(jnp.int32, (tiles, cells), 0)
    before = lax.broadcasted_iota(jnp.int32, (cells, cells), 0) < lax.broadcasted_iota(
        jnp.int32, (cells, cells), 1
    )
    rank = jnp.dot(
        jnp.where(member, 1.0, 0.0).astype(BF),
        jnp.where(before, 1.0, 0.0).astype(BF),
        preferred_element_type=F32,
    )
    rank = jnp.sum(jnp.where(member, rank, 0.0), axis=0, keepdims=True).astype(jnp.int32)
    target = owner * capacity + rank
    spread = lax.broadcasted_iota(jnp.int32, (out_ref.shape[0], cells), 0) == target
    spread = jnp.where(spread, 1.0, 0.0).astype(BF)
    for k in range(steps):
        current = (leak[k] - drive_ref[k].astype(F32)).astype(BF)
        out_ref[:, k * width : (k + 1) * width] = jnp.dot(
            spread, current, preferred_element_type=F32
        ).astype(BF)


def readout_kernel(
    tiles, steps, counts_ref, pattern_ref, rows_ref, transfer_ref, out_ref, slots
):
    block, kinds, width, contacts = transfer_ref.shape
    step = pl.program_id(0)
    row_count = rows_ref.shape[0]
    capacity = row_count // tiles
    slot_count = block * pl.num_programs(0)

    @pl.when(step == 0)
    def _():
        row = lax.broadcasted_iota(jnp.int32, (1, row_count), 1)
        slot_of = jnp.full((1, row_count), -1, jnp.int32)
        start = jnp.int32(0)
        for u in range(tiles):
            count = counts_ref[0, u]
            place = row - u * capacity
            slot_of = jnp.where((place >= 0) & (place < count), place + start, slot_of)
            start = start + count
        order = lax.broadcasted_iota(jnp.int32, (slot_count, row_count), 0) == slot_of
        order = jnp.where(order, 1.0, 0.0).astype(BF)
        for k in range(steps):
            slots[pl.ds(k, slot_count, stride=steps), :] = jnp.dot(
                order, rows_ref[:, k * width : (k + 1) * width], preferred_element_type=F32
            )
        out_ref[...] = jnp.zeros_like(out_ref)

    for s in range(block):
        slot = step * block + s
        current = slots[pl.ds(pl.multiple_of(slot * steps, steps), steps), :].astype(BF)
        for t in range(kinds):
            q = pattern_ref[t, slot]
            out_ref[q] += jnp.dot(current, transfer_ref[s, t], preferred_element_type=F32)


def on_device(
    voltage, conductance, reversal, drive, inv_cable, owner_map, peer_counts, pattern, transfer
):
    cells, width = voltage.shape
    steps = drive.shape[0]
    tiles = lax.axis_size("tile")
    sections = lax.axis_size("sec")
    capacity = 2 * cells // tiles
    row_count = tiles * capacity
    vmem = pl.BlockSpec(memory_space=pltpu.VMEM)
    smem = pl.BlockSpec(memory_space=pltpu.SMEM)
    big = pltpu.CompilerParams(vmem_limit_bytes=32 * 1024 * 1024)

    vloc, resp, ends = pl.pallas_call(
        local_kernel,
        out_shape=(
            jax.ShapeDtypeStruct((steps, cells, width), F32),
            jax.ShapeDtypeStruct((steps - 1, 2 * cells, width), F32),
            jax.ShapeDtypeStruct((END_ROWS, cells), BF),
        ),
        in_specs=[vmem] * 5,
        out_specs=(vmem,) * 3,
        compiler_params=big,
        name="local_steps",
    )(voltage, conductance, reversal, drive, inv_cable)

    all_ends = lax.all_gather(ends, "sec", axis=0, tiled=False)
    final_voltage, outgoing = pl.pallas_call(
        functools.partial(couple_kernel, tiles),
        out_shape=(
            jax.ShapeDtypeStruct((cells, width), F32),
            jax.ShapeDtypeStruct((row_count, steps * width), BF),
        ),
        in_specs=[smem] + [vmem] * 8,
        out_specs=(vmem,) * 2,
        scratch_shapes=[
            pltpu.VMEM((sections, END_ROWS, cells), F32),
            pltpu.VMEM((2 * steps, cells), F32),
            pltpu.VMEM((steps, cells, width), F32),
        ],
        compiler_params=big,
        name="couple_sections",
    )(
        lax.axis_index("sec").reshape(1),
        all_ends,
        vloc,
        resp,
        conductance,
        reversal,
        drive,
        inv_cable,
        owner_map.reshape(1, cells),
    )

    arrived = lax.all_to_all(outgoing, "tile", split_axis=0, concat_axis=0, tiled=True)

    weights = transfer[0]
    slot_count, kinds, _, contact_width = weights.shape
    contact_tiles = CONTACTS // contact_width
    block = 16
    partial_sum = pl.pallas_call(
        functools.partial(readout_kernel, tiles, steps),
        out_shape=jax.ShapeDtypeStruct((contact_tiles, steps, contact_width), F32),
        grid=(slot_count // block,),
        in_specs=[
            smem,
            smem,
            pl.BlockSpec((row_count, steps * width), lambda i: (0, 0)),
            pl.BlockSpec((block, kinds, width, contact_width), lambda i: (i, 0, 0, 0)),
        ],
        out_specs=pl.BlockSpec((contact_tiles, steps, contact_width), lambda i: (0, 0, 0)),
        scratch_shapes=[pltpu.VMEM((slot_count * steps, width), F32)],
        compiler_params=big,
        name="readout",
    )(peer_counts, pattern[0].T, arrived, weights)

    devices = tiles * sections
    share = CONTACTS // devices
    parts = contact_width // share
    if parts > 1:
        partial_sum = partial_sum.reshape(contact_tiles, steps, parts, share)
        partial_sum = partial_sum.transpose(0, 2, 1, 3).reshape(devices, steps, share)
    shares = lax.all_to_all(partial_sum, ("tile", "sec"), split_axis=0, concat_axis=0, tiled=True)
    return final_voltage, jnp.sum(shares, axis=0)


def solution(mesh):
    placed = (
        P("tile", "sec"),
        P("tile", "sec"),
        P("tile", "sec"),
        P(None, "tile", "sec"),
        P(),
        P("tile"),
        P("tile", None),
        P("sec", "tile", None),
        P("sec", "tile", None, None, None),
    )
    return jax.shard_map(
        on_device,
        mesh=mesh,
        in_specs=placed,
        out_specs=(P("tile", "sec"), P(None, ("tile", "sec"))),
        check_vma=False,
    )
```

time: 319 us -> 60.7 us (0.19)
  waiting for transfers between devices: 185 us -> 0 us
  starting transfers between devices: 76.4 us -> 0 us
  blocking collectives: 0 us -> 39 us
  matrix products: 15.6 us -> 0 us
  between operations: 14.1 us -> 0.67 us
  other arithmetic: 11.9 us -> 0.63 us
  Pallas kernels: 0 us -> 7.54 us
    psum x1 -> x0, waiting for transfers between devices: 124 us -> none  [on_device(): summed = lax.psum(partial_sum, ('tile', 'sec'))]
    all_to_all x8 -> x0, waiting for transfers between devices: 55.2 us -> none  [advance_send(): lax.all_to_all(outgoing, 'tile', split_axis=0, concat_axis=0, tiled=True)]
    ppermute x16 -> x0, starting transfers between devices: 45.6 us -> none  [the longest x8 35.4 us: padded_2(): lax.ppermute(lax.slice_in_dim(block, block.shape[dim] - width, None, axis...]
    all_to_all x0 -> x2, blocking collectives: none -> 32.8 us  [the longest x1 21.1 us: on_device(): lax.all_to_all(outgoing, 'tile', split_axis=0, concat_axis=0, tiled=True)]
    all_to_all x8 -> x0, starting transfers between devices: 30.7 us -> none  [advance_send(): lax.all_to_all(outgoing, 'tile', split_axis=0, concat_axis=0, tiled=True)]
    dot_general x10 -> x0, matrix products: 15.6 us -> none  [the longest x8 10.2 us: cable_update(): jnp.einsum('ci,ji->cj', right_side, inv_cable, precision=lax.Precision.HI...]
    unnamed x6 -> x24, local copies, waits for them, and re-layouts: 1.59 us -> 12.3 us
    pallas_call x0 -> x3, Pallas kernels: none -> 7.54 us  [the longest x1 4.05 us: on_device(): pl.pallas_call(functools.partial(readout_kernel, tiles, steps), out_shape...]
  transfers between devices with their start and end apart: 25 -> 0, of which waited for: 17 -> 0; matrix products, arithmetic and copies ran while one was open for 0% -> 0% of each run, Pallas kernels for 0% -> 0%
where the time goes in v1:
time: 60.7 us; the launch traced here: 60.1 us
  blocking collectives  39 us (64%)
  local copies, waits for them, and re-layouts  12.3 us (20%)
  Pallas kernels  7.54 us (12%)
  between operations  0.67 us (1%)
  other arithmetic  0.63 us (1%)
    all_to_all x1, blocking collectives, on_device(): lax.all_to_all(outgoing, 'tile', split_axis=0, concat_axis=0, tiled=True)  21.1 us
    unnamed x24, local copies, waits for them, and re-layouts  12.3 us
    all_to_all x1, blocking collectives, on_device(): lax.all_to_all(partial_sum, ('tile', 'sec'), split_axis=0, concat_axis=0,...  11.7 us
    all_gather x1, blocking collectives, on_device(): all_ends = lax.all_gather(ends, 'sec', axis=0, tiled=False)  6.18 us
    pallas_call x1, Pallas kernels, on_device(): pl.pallas_call(functools.partial(readout_kernel, tiles, steps), out_shape...  4.05 us
    pallas_call x1, Pallas kernels, on_device(): pl.pallas_call(local_kernel, out_shape=(jax.ShapeDtypeStruct((steps, cell...  1.98 us
    pallas_call x1, Pallas kernels, on_device(): pl.pallas_call(functools.partial(couple_kernel, tiles), out_shape=(jax.Sh...  1.51 us

profile of v1, /device:TPU:0, one launch (start us, length us, event | category | flops | bytes accessed | tf_op | source)
XLA Modules:
  0.0 60.1 jit_solution(1131568494547019828)
XLA Ops:
  0.6 0.0 copy-start.1
  0.6 0.9 %copy-done.1 = bf16[8,128,128]{2,1,0:T(8,128)(2,1)S(1)} copy-done((bf16[8,128,128]{2,1,0:T(8,128)(2,1)S(1)}, bf16[8,128,128]{2,1,0:T(8,128)(2,1)}, u32[]{:S(2)}) %copy-start.1) | copy-done | bytes 262168
  1.6 0.0 copy-start.3
  1.6 0.8 %copy-done.3 = f32[128,128]{1,0:T(8,128)S(1)} copy-done((f32[128,128]{1,0:T(8,128)S(1)}, f32[128,128]{1,0:T(8,128)}, u32[]{:S(2)}) %copy-start.3) | copy-done | bytes 65560
  2.4 0.0 copy-start.5
  2.4 0.8 %copy-done.5 = f32[128,128]{1,0:T(8,128)S(1)} copy-done((f32[128,128]{1,0:T(8,128)S(1)}, f32[128,128]{1,0:T(8,128)}, u32[]{:S(2)}) %copy-start.5) | copy-done | bytes 65560
  3.3 0.0 copy-start.7
  3.3 0.8 %copy-done.7 = f32[128,128]{1,0:T(8,128)S(1)} copy-done((f32[128,128]{1,0:T(8,128)S(1)}, f32[128,128]{1,0:T(8,128)}, u32[]{:S(2)}) %copy-start.7) | copy-done | bytes 65560
  4.1 0.0 copy-start.8
  4.1 0.8 %copy-done.8 = f32[128,128]{1,0:T(8,128)S(1)} copy-done((f32[128,128]{1,0:T(8,128)S(1)}, f32[128,128]{1,0:T(8,128)}, u32[]{:S(2)}) %copy-start.8) | copy-done | bytes 65560
  4.9 2.0 %local_steps.1 = (f32[8,128,128]{2,1,0:T(8,128)S(1)}, f32[7,256,128]{2,1,0:T(8,128)S(1)}, bf16[48,128]{1,0:T(8,128)(2,1)S(1)}) custom-call(f32[128,128]{1,0:T(8,128)S(1)} %copy-done.8, f32[128,128]{1,0:T(8,128)S(1)} %copy-done.3, f32[128,128]{1,0:T(8,128)S(1)} %copy-done.5, bf16[8,128,128]{2,1,0:T(8,128)(2,1)S(1)} %copy-done.1, f32[128,128]{1,0:T(8,128)S(1)} %copy-done.7), custom_call_target="tpu_custom_call" | custom-call | tf_op jit(solution)/shard_map/local_steps/pallas_call | solution.py:220
  6.9 6.2 %all-gather = bf16[192,128]{1,0:T(8,128)(2,1)S(1)} all-gather(bf16[48,128]{1,0:T(8,128)(2,1)S(1)} %get-tuple-element.7), channel_id=2, replica_groups=mesh['tile'=8,'sec'=4] {'sec'}, dimensions={0}, use_global_device_ids=true | all-gather | bytes 61440 | tf_op jit(solution)/shard_map/all_gather | solution.py:233
  13.1 0.0 copy-start.2
  13.1 0.9 %copy-done.2 = bf16[8,128,128]{2,1,0:T(8,128)(2,1)S(1)} copy-done((bf16[8,128,128]{2,1,0:T(8,128)(2,1)S(1)}, bf16[8,128,128]{2,1,0:T(8,128)(2,1)}, u32[]{:S(2)}) %copy-start.2) | copy-done | bytes 262168
  14.1 0.0 copy-start.4
  14.1 0.8 %copy-done.4 = f32[128,128]{1,0:T(8,128)S(1)} copy-done((f32[128,128]{1,0:T(8,128)S(1)}, f32[128,128]{1,0:T(8,128)}, u32[]{:S(2)}) %copy-start.4) | copy-done | bytes 65560
  14.9 0.0 copy-start.6
  14.9 0.8 %copy-done.6 = f32[128,128]{1,0:T(8,128)S(1)} copy-done((f32[128,128]{1,0:T(8,128)S(1)}, f32[128,128]{1,0:T(8,128)}, u32[]{:S(2)}) %copy-start.6) | copy-done | bytes 65560
  15.7 0.0 copy-start.10
  15.7 0.7 %copy-done.10 = s32[128]{0:T(128)S(1)} copy-done((s32[128]{0:T(128)S(1)}, s32[128]{0:T(128)}, u32[]{:S(2)}) %copy-start.10) | copy-done | bytes 536
  16.4 1.5 %couple_sections.1 = (f32[128,128]{1,0:T(8,128)}, bf16[256,1024]{1,0:T(8,128)(2,1)S(1)}) custom-call(s32[1]{0:T(128)} %bitcast.sec_ref, bf16[4,48,128]{2,1,0:T(8,128)(2,1)S(1)} %bitcast.12, f32[8,128,128]{2,1,0:T(8,128)S(1)} %get-tuple-element.8.vloc_ref, f32[7,256,128]{2,1,0:T(8,128)S(1)} %get-tuple-element.9.resp_ref, f32[128,128]{1,0:T(8,128)S(1)} %copy-done.4, ...), custom_call_target="tpu_custom_call" | custom-call | tf_op jit(solution)/shard_map/couple_sections/pallas_call | solution.py:234
  17.9 21.1 %all_to_all.16 = bf16[8,32,1024]{2,1,0:T(8,128)(2,1)S(1)} all-to-all(bf16[8,32,1024]{2,1,0:T(8,128)(2,1)S(1)} %bitcast.11), channel_id=1, replica_groups=mesh['tile'=8,'sec'=4] {'tile'}, dimensions={0} | all-to-all | bytes 1048576 | tf_op jit(solution)/shard_map/all_to_all | solution.py:261
  39.0 0.0 copy-start
  39.0 3.4 %copy-done = bf16[1,128,2,128,128]{4,3,2,1,0:T(8,128)(2,1)S(1)} copy-done((bf16[1,128,2,128,128]{4,3,2,1,0:T(8,128)(2,1)S(1)}, bf16[1,128,2,128,128]{4,3,2,1,0:T(8,128)(2,1)}, u32[]{:S(2)}) %copy-start) | copy-done | bytes 8388632
  42.4 0.0 copy-start.9
  42.4 0.7 %copy-done.9 = s32[1,128,2]{1,2,0:T(2,128)S(1)} copy-done((s32[1,128,2]{1,2,0:T(2,128)S(1)}, s32[1,128,2]{1,2,0:T(2,128)}, u32[]{:S(2)}) %copy-start.9) | copy-done | bytes 1048
  43.1 0.0 copy-start.11
  43.1 0.7 %copy-done.11 = s32[1,8]{1,0:T(1,128)S(1)} copy-done((s32[1,8]{1,0:T(1,128)S(1)}, s32[1,8]{1,0:T(1,128)}, u32[]{:S(2)}) %copy-start.11) | copy-done | bytes 56
  43.7 4.1 %readout.1 = f32[32,8,128]{2,1,0:T(8,128)S(1)} custom-call(s32[1,8]{1,0:T(1,128)S(1)} %copy-done.11, s32[2,128]{1,0:T(2,128)S(1)} %bitcast.13, bf16[256,1024]{1,0:T(8,128)(2,1)S(1)} %bitcast.10, bf16[128,2,128,128]{3,2,1,0:T(8,128)(2,1)S(1)} %bitcast.9), custom_call_target="tpu_custom_call" | custom-call | tf_op jit(solution)/shard_map/readout/pallas_call | solution.py:267
  47.8 11.7 %all_to_all.17 = f32[32,8,128]{2,1,0:T(8,128)S(1)} all-to-all(f32[32,8,128]{2,1,0:T(8,128)S(1)} %readout.1), channel_id=1, replica_groups=mesh['tile'=8,'sec'=4] {'tile','sec'}, dimensions={0} | all-to-all | bytes 262144 | tf_op jit(solution)/shard_map/all_to_all | solution.py:289
  59.5 0.6 %reduce_sum.9 = f32[8,128]{1,0:T(8,128)} reduce(f32[32,8,128]{2,1,0:T(8,128)S(1)} %all_to_all.17, f32[]{:T(128)} %constant.1.clone.1), dimensions={0}, to_apply=%region_0.0 | reduce | flops 31744 | bytes 135172 | tf_op jit(solution)/shard_map/reduce_sum | solution.py:290
Async XLA Ops:
  0.6 1.0 %copy-start.1 = (bf16[8,128,128]{2,1,0:T(8,128)(2,1)S(1)}, bf16[8,128,128]{2,1,0:T(8,128)(2,1)}, u32[]{:S(2)}) copy-start(bf16[8,128,128]{2,1,0:T(8,128)(2,1)} %drive_ref.3) | copy-start | bytes 786436
  1.6 0.8 %copy-start.3 = (f32[128,128]{1,0:T(8,128)S(1)}, f32[128,128]{1,0:T(8,128)}, u32[]{:S(2)}) copy-start(f32[128,128]{1,0:T(8,128)} %g_ref.3) | copy-start | bytes 196612
  2.4 0.8 %copy-start.5 = (f32[128,128]{1,0:T(8,128)S(1)}, f32[128,128]{1,0:T(8,128)}, u32[]{:S(2)}) copy-start(f32[128,128]{1,0:T(8,128)} %e_ref.3) | copy-start | bytes 196612
  3.3 0.8 %copy-start.7 = (f32[128,128]{1,0:T(8,128)S(1)}, f32[128,128]{1,0:T(8,128)}, u32[]{:S(2)}) copy-start(f32[128,128]{1,0:T(8,128)} %cable_ref.3) | copy-start | bytes 196612
  4.1 0.8 %copy-start.8 = (f32[128,128]{1,0:T(8,128)S(1)}, f32[128,128]{1,0:T(8,128)}, u32[]{:S(2)}) copy-start(f32[128,128]{1,0:T(8,128)} %v_ref.1) | copy-start | bytes 196612
  13.1 0.9 %copy-start.2 = (bf16[8,128,128]{2,1,0:T(8,128)(2,1)S(1)}, bf16[8,128,128]{2,1,0:T(8,128)(2,1)}, u32[]{:S(2)}) copy-start(bf16[8,128,128]{2,1,0:T(8,128)(2,1)} %drive_ref.3) | copy-start | bytes 786436
  14.1 0.8 %copy-start.4 = (f32[128,128]{1,0:T(8,128)S(1)}, f32[128,128]{1,0:T(8,128)}, u32[]{:S(2)}) copy-start(f32[128,128]{1,0:T(8,128)} %g_ref.3) | copy-start | bytes 196612
  14.9 0.8 %copy-start.6 = (f32[128,128]{1,0:T(8,128)S(1)}, f32[128,128]{1,0:T(8,128)}, u32[]{:S(2)}) copy-start(f32[128,128]{1,0:T(8,128)} %e_ref.3) | copy-start | bytes 196612
  15.7 0.7 %copy-start.10 = (s32[128]{0:T(128)S(1)}, s32[128]{0:T(128)}, u32[]{:S(2)}) copy-start(s32[128]{0:T(128)} %param.14) | copy-start | bytes 1540
  39.0 3.4 %copy-start = (bf16[1,128,2,128,128]{4,3,2,1,0:T(8,128)(2,1)S(1)}, bf16[1,128,2,128,128]{4,3,2,1,0:T(8,128)(2,1)}, u32[]{:S(2)}) copy-start(bf16[1,128,2,128,128]{4,3,2,1,0:T(8,128)(2,1)} %param.17) | copy-start | bytes 25165828
  42.4 0.7 %copy-start.9 = (s32[1,128,2]{1,2,0:T(2,128)S(1)}, s32[1,128,2]{1,2,0:T(2,128)}, u32[]{:S(2)}) copy-start(s32[1,128,2]{1,2,0:T(2,128)} %param.16) | copy-start | bytes 3076
  43.1 0.7 %copy-start.11 = (s32[1,8]{1,0:T(1,128)S(1)}, s32[1,8]{1,0:T(1,128)}, u32[]{:S(2)}) copy-start(s32[1,8]{1,0:T(1,128)} %counts_ref.1) | copy-start | bytes 100

commit v2 on v1

v2 whole, which is shorter than its diff:
```python
import functools

import jax
import jax.numpy as jnp
from jax import lax
from jax.experimental import pallas as pl
from jax.experimental.pallas import tpu as pltpu
from jax.sharding import PartitionSpec as P

CONTACTS = 4096
TIME_STEP = 0.25
AXIAL = 2.0
END_ROWS = 48
PAIRED = True
BF = jnp.bfloat16
F32 = jnp.float32
PARAMS = pltpu.CompilerParams(vmem_limit_bytes=24 * 1024 * 1024)


def split_hi_lo(x):
    hi = x.astype(BF)
    return hi, (x - hi.astype(F32)).astype(BF)


def one_hot(condition):
    return jnp.where(condition, 1.0, 0.0).astype(BF)


def iota(shape, dim):
    return lax.broadcasted_iota(jnp.int32, shape, dim)


def local_kernel(
    tiles,
    paired,
    me_ref,
    v_hbm,
    g_hbm,
    e_hbm,
    drive_hbm,
    cable_hbm,
    owner_hbm,
    counts_hbm,
    pattern_hbm,
    vloc_ref,
    resp_ref,
    ends_ref,
    g_ref,
    e_ref,
    drive_ref,
    lags_ref,
    spread_ref,
    order_ref,
    pattern_ref,
    v_ref,
    cable_ref,
    owner_ref,
    counts_ref,
    sems,
):
    pairs = [
        (g_hbm, g_ref),
        (v_hbm, v_ref),
        (e_hbm, e_ref),
        (cable_hbm, cable_ref),
        (drive_hbm, drive_ref),
        (owner_hbm, owner_ref),
        (counts_hbm, counts_ref),
        (pattern_hbm, pattern_ref),
    ]
    copies = [pltpu.make_async_copy(src, dst, sems.at[i]) for i, (src, dst) in enumerate(pairs)]
    for copy in copies:
        copy.start()
    for copy in copies[:5]:
        copy.wait()

    cells, width = v_ref.shape
    steps = drive_ref.shape[0]
    cond = g_ref[...]
    lane = iota((cells, width), 1)
    at_end = jnp.where((lane == 0) | (lane == width - 1), TIME_STEP * AXIAL, 0.0).astype(F32)
    keep = 1.0 - TIME_STEP * cond - at_end
    source = TIME_STEP * cond * e_ref[...]
    cable = cable_ref[...].T
    cable_hi, cable_lo = split_hi_lo(cable)
    half = jnp.concatenate([cable_hi, cable_lo], axis=1)
    weights = jnp.concatenate([half, half], axis=0)
    pick_row, pick_lane = iota((16, width), 0), iota((16, width), 1)
    pick = one_hot(
        ((pick_row == 0) & (pick_lane == 0)) | ((pick_row == 1) & (pick_lane == width - 1))
    )

    def solve(rhs):
        hi, lo = split_hi_lo(rhs)
        both = jnp.dot(jnp.concatenate([hi, lo], axis=1), weights, preferred_element_type=F32)
        return both[:, :width] + both[:, width:]

    def ends_of(x):
        return lax.dot_general(
            pick, x.astype(BF), (((1,), (1,)), ((), ())), preferred_element_type=F32
        )[0:2]

    voltage = v_ref[...]
    lag_left = TIME_STEP * AXIAL * cable[0:1, :]
    lag_right = TIME_STEP * AXIAL * cable[width - 1 : width, :]
    lags_ref[0:1, :] = lag_left
    lags_ref[1:2, :] = lag_right
    keep2 = jnp.concatenate([keep, keep], axis=0)
    resp = jnp.concatenate(
        [jnp.broadcast_to(lag_left, (cells, width)), jnp.broadcast_to(lag_right, (cells, width))],
        axis=0,
    )
    v_ends, l_ends, r_ends = [ends_of(voltage)], [], []
    both_ends = ends_of(resp)
    l_ends.append(both_ends[:, :cells])
    r_ends.append(both_ends[:, cells:])
    for k in range(steps):
        rhs = voltage * keep + source + TIME_STEP * drive_ref[k].astype(F32)
        if k < steps - 1:
            out = solve(jnp.concatenate([rhs, resp * keep2], axis=0))
            voltage, resp = out[:cells], out[cells:]
            resp_ref[k] = resp
            v_ends.append(ends_of(voltage))
            if k < steps - 2:
                both_ends = ends_of(resp)
                l_ends.append(both_ends[:, :cells])
                r_ends.append(both_ends[:, cells:])
        else:
            voltage = solve(rhs)
        vloc_ref[k] = voltage
    rows = v_ends + l_ends + r_ends
    rows.append(jnp.zeros((END_ROWS - 2 * len(rows), cells), F32))
    ends_ref[...] = jnp.concatenate(rows, axis=0).astype(BF)

    for copy in copies[5:7]:
        copy.wait()
    me = me_ref[0]
    row_count = spread_ref.shape[0]
    capacity = row_count // tiles
    owner = owner_ref[...]
    member = owner == iota((tiles, cells), 0)
    before = iota((cells, cells), 0) < iota((cells, cells), 1)
    rank = jnp.dot(one_hot(member), one_hot(before), preferred_element_type=F32)
    rank = jnp.sum(jnp.where(member, rank, 0.0), axis=0, keepdims=True).astype(jnp.int32)
    to = owner ^ me if paired else owner
    spread_ref[...] = one_hot(iota((row_count, cells), 0) == to * capacity + rank)

    counts = [counts_ref[0, u] for u in range(tiles)]
    row = iota((1, row_count), 1)
    slot_of = jnp.full((1, row_count), -1, jnp.int32)
    start = jnp.int32(0)
    for b in range(tiles):
        if paired:
            sender = b ^ me
            count = counts_ref[0, sender]
            start = sum(jnp.where(u < sender, counts[u], 0) for u in range(tiles))
        else:
            count = counts[b]
            start = start + (counts[b - 1] if b else 0)
        place = row - b * capacity
        slot_of = jnp.where((place >= 0) & (place < count), place + start, slot_of)
    order_ref[...] = one_hot(iota(order_ref.shape, 0) == slot_of)
    for copy in copies[7:]:
        copy.wait()


def couple_kernel(sections, block_count, *refs):
    sec_ref, *refs = refs
    ends_refs, refs = refs[:sections], refs[sections:]
    vloc_ref, resp_ref, g_ref, e_ref, drive_ref, lags_ref, spread_ref, *refs = refs
    final_hbm, *refs = refs
    out_refs, refs = refs[:block_count], refs[block_count:]
    ends32, incoming, leak, final_ref, sem = refs
    steps, cells, width = drive_ref.shape
    mine = sec_ref[0]
    for p in range(sections):
        ends32[mine ^ p] = ends_refs[p][...].astype(F32)

    def rows(q):
        return ends32[:, q, :]

    base_l, base_r = 2 * steps, 4 * steps - 2
    left_a = [None] + [rows(base_l + 2 * l) for l in range(steps - 1)]
    left_b = [None] + [rows(base_l + 2 * l + 1) for l in range(steps - 1)]
    right_a = [None] + [rows(base_r + 2 * l) for l in range(steps - 1)]
    right_b = [None] + [rows(base_r + 2 * l + 1) for l in range(steps - 1)]
    zero = jnp.zeros((1, cells), F32)
    from_left, from_right = [], []
    for k in range(steps):
        first, last = rows(2 * k), rows(2 * k + 1)
        for j in range(k):
            first = first + (left_a[k - j] * from_left[j] + right_a[k - j] * from_right[j])
            last = last + (left_b[k - j] * from_left[j] + right_b[k - j] * from_right[j])
        from_left.append(jnp.concatenate([zero, last[:-1]], axis=0))
        from_right.append(jnp.concatenate([first[1:], zero], axis=0))
    own = iota((sections, cells), 0) == mine
    for j in range(steps):
        incoming[pl.ds(2 * j, 1), :] = jnp.sum(
            jnp.where(own, from_left[j], 0.0), axis=0, keepdims=True
        )
        incoming[pl.ds(2 * j + 1, 1), :] = jnp.sum(
            jnp.where(own, from_right[j], 0.0), axis=0, keepdims=True
        )
    by_cell = incoming[...].T

    block = 8
    lag_left = jnp.broadcast_to(lags_ref[0:1, :], (block, width))
    lag_right = jnp.broadcast_to(lags_ref[1:2, :], (block, width))
    for c in range(0, cells, block):
        span = slice(c, c + block)
        unit = [
            jnp.broadcast_to(by_cell[span, q : q + 1], (block, width)) for q in range(2 * steps)
        ]
        lefts = [None, lag_left] + [resp_ref[l, span, :] for l in range(steps - 1)]
        rights = [None, lag_right] + [
            resp_ref[l, cells + c : cells + c + block, :] for l in range(steps - 1)
        ]
        cond, rev = g_ref[span, :], e_ref[span, :]
        for k in range(1, steps + 1):
            total = vloc_ref[k - 1, span, :]
            for j in range(k):
                total = total + (unit[2 * j] * lefts[k - j] + unit[2 * j + 1] * rights[k - j])
            leak[k - 1, span, :] = cond * (total - rev)
        final_ref[span, :] = total
    give = pltpu.make_async_copy(final_ref, final_hbm, sem)
    give.start()

    capacity = out_refs[0].shape[0]
    for k in range(steps):
        current = (leak[k] - drive_ref[k].astype(F32)).astype(BF)
        placed = jnp.dot(spread_ref[...], current, preferred_element_type=F32).astype(BF)
        for b in range(block_count):
            out_refs[b][:, k * width : (k + 1) * width] = placed[b * capacity : (b + 1) * capacity]
    give.wait()


def fetch_kernel(after_ref, transfer_hbm, transfer_ref, sems):
    del after_ref
    parts = sems.shape[0]
    size = transfer_ref.shape[0] // parts
    copies = []
    for p in range(parts):
        span = pl.ds(p * size, size)
        copies.append(
            pltpu.make_async_copy(transfer_hbm.at[span], transfer_ref.at[span], sems.at[p])
        )
    for copy in copies:
        copy.start()
    for copy in copies:
        copy.wait()


def readout_kernel(steps, pattern_ref, order_ref, *refs):
    *block_refs, transfer_ref, out_ref, slots, sums = refs
    slot_count = order_ref.shape[0]
    kinds, width, contacts = transfer_ref.shape[1:]
    for k in range(steps):
        span = slice(k * width, (k + 1) * width)
        rows = jnp.concatenate([ref[:, span] for ref in block_refs], axis=0)
        slots[pl.ds(k, slot_count, stride=steps), :] = jnp.dot(
            order_ref[...], rows, preferred_element_type=F32
        )
    sums[...] = jnp.zeros_like(sums)
    ways = sums.shape[0]
    turn = 0
    for s in range(slot_count):
        current = slots[s * steps : (s + 1) * steps, :].astype(BF)
        tile = jnp.concatenate([transfer_ref[s, t] for t in range(kinds)], axis=1)
        reach = jnp.dot(current, tile, preferred_element_type=F32)
        for t in range(kinds):
            sums[turn % ways, pattern_ref[t, s]] += reach[:, t * contacts : (t + 1) * contacts]
            turn += 1
    out_ref[...] = sum(sums[w] for w in range(ways))


def in_hbm(x):
    return pltpu.with_memory_space_constraint(x, pltpu.HBM)


def exchange(blocks, axis):
    count = lax.axis_size(axis)
    arrived = [blocks[0]]
    for p in range(1, count):
        arrived.append(lax.ppermute(blocks[p], axis, [(i, i ^ p) for i in range(count)]))
    return arrived


def on_device(
    voltage, conductance, reversal, drive, inv_cable, owner_map, peer_counts, pattern, transfer
):
    cells, width = voltage.shape
    steps = drive.shape[0]
    tiles = lax.axis_size("tile")
    sections = lax.axis_size("sec")
    capacity = 2 * cells // tiles
    row_count = tiles * capacity
    weights = transfer[0]
    slot_count, kinds, _, contact_width = weights.shape
    paired = PAIRED and tiles == 8
    vmem = pl.BlockSpec(memory_space=pltpu.VMEM)
    smem = pl.BlockSpec(memory_space=pltpu.SMEM)
    hbm = pl.BlockSpec(memory_space=pltpu.HBM)

    vloc, resp, ends, cond, rev, driven, lags, spread, order, layout = pl.pallas_call(
        functools.partial(local_kernel, tiles, paired),
        out_shape=(
            jax.ShapeDtypeStruct((steps, cells, width), F32),
            jax.ShapeDtypeStruct((steps - 1, 2 * cells, width), F32),
            jax.ShapeDtypeStruct((END_ROWS, cells), BF),
            jax.ShapeDtypeStruct((cells, width), F32),
            jax.ShapeDtypeStruct((cells, width), F32),
            jax.ShapeDtypeStruct((steps, cells, width), BF),
            jax.ShapeDtypeStruct((2, width), F32),
            jax.ShapeDtypeStruct((row_count, cells), BF),
            jax.ShapeDtypeStruct((slot_count, row_count), BF),
            jax.ShapeDtypeStruct((kinds, slot_count), jnp.int32),
        ),
        in_specs=[smem] + [hbm] * 8,
        out_specs=(vmem,) * 10,
        scratch_shapes=[
            pltpu.VMEM((cells, width), F32),
            pltpu.VMEM((width, width), F32),
            pltpu.VMEM((1, cells), jnp.int32),
            pltpu.SMEM((1, tiles), jnp.int32),
            pltpu.SemaphoreType.DMA((8,)),
        ],
        compiler_params=PARAMS,
        name="local_steps",
    )(
        lax.axis_index("tile").reshape(1),
        in_hbm(voltage),
        in_hbm(conductance),
        in_hbm(reversal),
        in_hbm(drive),
        in_hbm(inv_cable),
        in_hbm(owner_map.reshape(1, cells)),
        in_hbm(peer_counts),
        in_hbm(pattern[0].T),
    )

    all_ends = exchange([ends] * sections, "sec")
    block_count = tiles if paired else 1
    final_voltage, *outgoing = pl.pallas_call(
        functools.partial(couple_kernel, sections, block_count),
        out_shape=(
            jax.ShapeDtypeStruct((cells, width), F32),
        )
        + (jax.ShapeDtypeStruct((row_count // block_count, steps * width), BF),) * block_count,
        in_specs=[smem] + [vmem] * (sections + 7),
        out_specs=(hbm,) + (vmem,) * block_count,
        scratch_shapes=[
            pltpu.VMEM((sections, END_ROWS, cells), F32),
            pltpu.VMEM((2 * steps, cells), F32),
            pltpu.VMEM((steps, cells, width), F32),
            pltpu.VMEM((cells, width), F32),
            pltpu.SemaphoreType.DMA,
        ],
        compiler_params=PARAMS,
        name="couple_sections",
    )(
        lax.axis_index("sec").reshape(1),
        *all_ends,
        vloc,
        resp,
        cond,
        rev,
        driven,
        lags,
        spread,
    )

    if paired:
        arrived = exchange(outgoing, "tile")
    else:
        arrived = [lax.all_to_all(outgoing[0], "tile", split_axis=0, concat_axis=0, tiled=True)]

    tiles_here = pl.pallas_call(
        fetch_kernel,
        out_shape=jax.ShapeDtypeStruct(weights.shape, BF),
        in_specs=[vmem, hbm],
        out_specs=vmem,
        scratch_shapes=[pltpu.SemaphoreType.DMA((4,))],
        compiler_params=PARAMS,
        name="fetch_tiles",
    )(outgoing[0], in_hbm(weights))

    contact_tiles = CONTACTS // contact_width
    partial_sum = pl.pallas_call(
        functools.partial(readout_kernel, steps),
        out_shape=jax.ShapeDtypeStruct((contact_tiles, steps, contact_width), F32),
        in_specs=[smem] + [vmem] * (len(arrived) + 2),
        out_specs=vmem,
        scratch_shapes=[
            pltpu.VMEM((slot_count * steps, width), F32),
            pltpu.VMEM((4, contact_tiles, steps, contact_width), F32),
        ],
        compiler_params=PARAMS,
        name="readout",
    )(layout, order, *arrived, tiles_here)

    devices = tiles * sections
    share = CONTACTS // devices
    parts = contact_width // share
    if parts > 1:
        partial_sum = partial_sum.reshape(contact_tiles, steps, parts, share)
        partial_sum = partial_sum.transpose(0, 2, 1, 3).reshape(devices, steps, share)
    shares = lax.all_to_all(partial_sum, ("tile", "sec"), split_axis=0, concat_axis=0, tiled=True)
    return final_voltage, jnp.sum(shares, axis=0)


def solution(mesh):
    placed = (
        P("tile", "sec"),
        P("tile", "sec"),
        P("tile", "sec"),
        P(None, "tile", "sec"),
        P(),
        P("tile"),
        P("tile", None),
        P("sec", "tile", None),
        P("sec", "tile", None, None, None),
    )
    return jax.shard_map(
        on_device,
        mesh=mesh,
        in_specs=placed,
        out_specs=(P("tile", "sec"), P(None, ("tile", "sec"))),
        check_vma=False,
    )
```

time: 60.7 us -> 43.7 us (0.72)
  blocking collectives: 39 us -> 10.9 us
  starting transfers between devices: 0 us -> 14.3 us
  local copies, waits for them, and re-layouts: 12.3 us -> 0 us
  waiting for transfers between devices: 0 us -> 6.4 us
  Pallas kernels: 7.54 us -> 10.5 us
    all_to_all x1 -> x0, blocking collectives: 21.1 us -> none  [on_device(): lax.all_to_all(outgoing, 'tile', split_axis=0, concat_axis=0, tiled=True)]
    ppermute x0 -> x10, starting transfers between devices: none -> 14.3 us  [exchange(): lax.ppermute(blocks[p], axis, [(i, i ^ p) for i in range(count)])]
    unnamed x24 -> x0, local copies, waits for them, and re-layouts: 12.3 us -> none
    ppermute x0 -> x10, waiting for transfers between devices: none -> 6.4 us  [exchange(): lax.ppermute(blocks[p], axis, [(i, i ^ p) for i in range(count)])]
    all_gather x1 -> x0, blocking collectives: 6.18 us -> none  [on_device(): all_ends = lax.all_gather(ends, 'sec', axis=0, tiled=False)]
    pallas_call x3 -> x4, Pallas kernels: 7.54 us -> 10.5 us  [the longest x1 3.5 us: on_device(): pl.pallas_call(fetch_kernel, out_shape=jax.ShapeDtypeStruct(weights.shape...]
    all_to_all x1, blocking collectives: 11.7 us -> 10.9 us  [on_device(): lax.all_to_all(partial_sum, ('tile', 'sec'), split_axis=0, concat_axis=0,...]
  transfers between devices with their start and end apart: 0 -> 10, of which waited for: 0 -> 4; matrix products, arithmetic and copies ran while one was open for 0% -> 0% of each run, Pallas kernels for 0% -> 8%
where the time goes in v2:
time: 43.7 us; the launch traced here: 43.5 us
  starting transfers between devices  14.3 us (33%)
  blocking collectives  10.9 us (25%)
  Pallas kernels  10.5 us (24%)
  waiting for transfers between devices  6.4 us (15%)
  between operations  0.69 us (2%)
  other arithmetic  0.63 us (1%)
    ppermute x10, starting transfers between devices, exchange(): lax.ppermute(blocks[p], axis, [(i, i ^ p) for i in range(count)])  14.3 us
    all_to_all x1, blocking collectives, on_device(): lax.all_to_all(partial_sum, ('tile', 'sec'), split_axis=0, concat_axis=0,...  10.9 us
    ppermute x10, waiting for transfers between devices, exchange(): lax.ppermute(blocks[p], axis, [(i, i ^ p) for i in range(count)])  6.4 us
    pallas_call x1, Pallas kernels, on_device(): pl.pallas_call(fetch_kernel, out_shape=jax.ShapeDtypeStruct(weights.shape...  3.5 us
    pallas_call x1, Pallas kernels, on_device(): pl.pallas_call(functools.partial(local_kernel, tiles, paired), out_shape=...  3.32 us
    pallas_call x1, Pallas kernels, on_device(): pl.pallas_call(functools.partial(readout_kernel, steps), out_shape=jax.Sh...  2.26 us
    pallas_call x1, Pallas kernels, on_device(): pl.pallas_call(functools.partial(couple_kernel, sections, block_count), o...  1.43 us
  transfers between devices with their start and end apart: 10, of which 4 were waited for; matrix products, arithmetic and copies ran while one was open for 0% of the time, Pallas kernels for 8%

profile of v2, /device:TPU:0, one launch (start us, length us, event | category | flops | bytes accessed | tf_op | source)
XLA Modules:
  0.0 43.5 jit_solution(14522575467773165421)
XLA Ops:
  0.6 3.3 %local_steps.1 = (f32[8,128,128]{2,1,0:T(8,128)S(1)}, f32[7,256,128]{2,1,0:T(8,128)S(1)}, bf16[48,128]{1,0:T(8,128)(2,1)S(1)}, f32[128,128]{1,0:T(8,128)S(1)}, f...) custom-call(s32[1]{0:T(128)} %bitcast.1.me_ref, ...), custom_call_target="tpu_custom_call" | custom-call | tf_op jit(solution)/shard_map/local_steps/pallas_call | solution.py:304
  4.0 2.4 %collective-permute-start.2 = (bf16[48,128]{1,0:T(8,128)(2,1)S(1)}, bf16[48,128]{1,0:T(8,128)(2,1)S(1)}, u32[]{:S(2)}, u32[]{:S(2)}) collective-permute-start(bf16[48,128]{1,0:T(8,128)(2,1)S(1)} %get-tuple-element.21.refs_1_), channel_id=1, source_target_pairs={{0,3},{1,2},{2,1},{3,0},{4,7},{5,6},{6,5},{7,4},{8,11},{9,10},{10,... | collective-permute-start | bytes 36872 | tf_op jit(solution)/shard_map/ppermute | solution.py:284
  6.4 0.6 %collective-permute-start.1 = (bf16[48,128]{1,0:T(8,128)(2,1)S(1)}, bf16[48,128]{1,0:T(8,128)(2,1)S(1)}, u32[]{:S(2)}, u32[]{:S(2)}) collective-permute-start(bf16[48,128]{1,0:T(8,128)(2,1)S(1)} %get-tuple-element.21.refs_1_), channel_id=1, source_target_pairs={{0,2},{1,3},{2,0},{3,1},{4,6},{5,7},{6,4},{7,5},{8,10},{9,11},{10,... | collective-permute-start | bytes 36872 | tf_op jit(solution)/shard_map/ppermute | solution.py:284
  7.1 0.0 collective-permute-start
  7.1 0.7 %collective-permute-done.2.refs_4_ = bf16[48,128]{1,0:T(8,128)(2,1)S(1)} collective-permute-done((bf16[48,128]{1,0:T(8,128)(2,1)S(1)}, bf16[48,128]{1,0:T(8,128)(2,1)S(1)}, u32[]{:S(2)}, u32[]{:S(2)}) %collective-permute-start.2) | collective-permute-done | bytes 12320 | tf_op jit(solution)/shard_map/ppermute | solution.py:284
  7.8 2.3 %collective-permute-done.1.refs_3_ = bf16[48,128]{1,0:T(8,128)(2,1)S(1)} collective-permute-done((bf16[48,128]{1,0:T(8,128)(2,1)S(1)}, bf16[48,128]{1,0:T(8,128)(2,1)S(1)}, u32[]{:S(2)}, u32[]{:S(2)}) %collective-permute-start.1) | collective-permute-done | bytes 12320 | tf_op jit(solution)/shard_map/ppermute | solution.py:284
  10.1 0.0 collective-permute-done.refs_2_
  10.1 1.4 %couple_sections.1 = (f32[128,128]{1,0:T(8,128)}, bf16[32,1024]{1,0:T(8,128)(2,1)S(1)}, bf16[32,1024]{1,0:T(8,128)(2,1)S(1)}, bf16[32,1024]{1,0:T(8,128)(2,1)S(1...) custom-call(s32[1]{0:T(128)} %bitcast.refs_0_, ...), custom_call_target="tpu_custom_call" | custom-call | tf_op jit(solution)/shard_map/couple_sections/pallas_call | solution.py:343
  11.6 1.6 %collective-permute-start.3 = (bf16[32,1024]{1,0:T(8,128)(2,1)S(1)}, bf16[32,1024]{1,0:T(8,128)(2,1)S(1)}, u32[]{:S(2)}, u32[]{:S(2)}) collective-permute-start(bf16[32,1024]{1,0:T(8,128)(2,1)S(1)} %get-tuple-element.33), channel_id=1, source_target_pairs={{0,4},{4,0},{8,12},{12,8},{16,20},{20,16},{24,28},{28,24},{1,5},{5... | collective-permute-start | bytes 196616 | tf_op jit(solution)/shard_map/ppermute | solution.py:284
  13.1 1.6 %collective-permute-start.4 = (bf16[32,1024]{1,0:T(8,128)(2,1)S(1)}, bf16[32,1024]{1,0:T(8,128)(2,1)S(1)}, u32[]{:S(2)}, u32[]{:S(2)}) collective-permute-start(bf16[32,1024]{1,0:T(8,128)(2,1)S(1)} %get-tuple-element.34), channel_id=1, source_target_pairs={{0,8},{4,12},{8,0},{12,4},{16,24},{20,28},{24,16},{28,20},{1,9},{5... | collective-permute-start | bytes 196616 | tf_op jit(solution)/shard_map/ppermute | solution.py:284
  14.7 0.4 collective-permute-start.5
  15.1 2.6 %collective-permute-start.6 = (bf16[32,1024]{1,0:T(8,128)(2,1)S(1)}, bf16[32,1024]{1,0:T(8,128)(2,1)S(1)}, u32[]{:S(2)}, u32[]{:S(2)}) collective-permute-start(bf16[32,1024]{1,0:T(8,128)(2,1)S(1)} %get-tuple-element.36), channel_id=1, source_target_pairs={{0,16},{4,20},{8,24},{12,28},{16,0},{20,4},{24,8},{28,12},{1,17},{... | collective-permute-start | bytes 196616 | tf_op jit(solution)/shard_map/ppermute | solution.py:284
  17.7 1.3 %collective-permute-start.7 = (bf16[32,1024]{1,0:T(8,128)(2,1)S(1)}, bf16[32,1024]{1,0:T(8,128)(2,1)S(1)}, u32[]{:S(2)}, u32[]{:S(2)}) collective-permute-start(bf16[32,1024]{1,0:T(8,128)(2,1)S(1)} %get-tuple-element.37), channel_id=1, source_target_pairs={{0,20},{4,16},{8,28},{12,24},{16,4},{20,0},{24,12},{28,8},{1,21},{... | collective-permute-start | bytes 196616 | tf_op jit(solution)/shard_map/ppermute | solution.py:284
  19.0 0.0 collective-permute-done.3.refs_1_
  19.0 3.6 %collective-permute-start.8 = (bf16[32,1024]{1,0:T(8,128)(2,1)S(1)}, bf16[32,1024]{1,0:T(8,128)(2,1)S(1)}, u32[]{:S(2)}, u32[]{:S(2)}) collective-permute-start(bf16[32,1024]{1,0:T(8,128)(2,1)S(1)} %get-tuple-element.38), channel_id=1, source_target_pairs={{0,24},{4,28},{8,16},{12,20},{16,8},{20,12},{24,0},{28,4},{1,25},{... | collective-permute-start | bytes 196616 | tf_op jit(solution)/shard_map/ppermute | solution.py:284
  22.6 0.0 collective-permute-done.4.refs_2_
  22.6 0.2 collective-permute-start.9
  22.8 3.5 %fetch_tiles.1.refs_8_ = bf16[128,2,128,128]{3,2,1,0:T(8,128)(2,1)S(1)} custom-call(bf16[32,1024]{1,0:T(8,128)(2,1)S(1)} %get-tuple-element.32.after_ref.refs_0_, bf16[128,2,128,128]{3,2,1,0:T(8,128)(2,1)} %bitcast.7), custom_call_target="tpu_custom_call" | custom-call | tf_op jit(solution)/shard_map/fetch_tiles/pallas_call | solution.py:377
  26.3 0.0 collective-permute-done.5.refs_3_
  26.3 0.0 collective-permute-done.6.refs_4_
  26.3 1.5 %collective-permute-done.7.refs_5_ = bf16[32,1024]{1,0:T(8,128)(2,1)S(1)} collective-permute-done((bf16[32,1024]{1,0:T(8,128)(2,1)S(1)}, bf16[32,1024]{1,0:T(8,128)(2,1)S(1)}, u32[]{:S(2)}, u32[]{:S(2)}) %collective-permute-start.7) | collective-permute-done | bytes 65568 | tf_op jit(solution)/shard_map/ppermute | solution.py:284
  27.8 0.0 collective-permute-done.8.refs_6_
  27.8 1.9 %collective-permute-done.9.refs_7_ = bf16[32,1024]{1,0:T(8,128)(2,1)S(1)} collective-permute-done((bf16[32,1024]{1,0:T(8,128)(2,1)S(1)}, bf16[32,1024]{1,0:T(8,128)(2,1)S(1)}, u32[]{:S(2)}, u32[]{:S(2)}) %collective-permute-start.9) | collective-permute-done | bytes 65568 | tf_op jit(solution)/shard_map/ppermute | solution.py:284
  29.7 2.3 %readout.1 = f32[32,8,128]{2,1,0:T(8,128)S(1)} custom-call(s32[2,128]{1,0:T(2,128)S(1)} %get-tuple-element.30.pattern_ref, bf16[128,256]{1,0:T(8,128)(2,1)S(1)} %get-tuple-element.31.order_ref, bf16[32,1024]{1,0:T(8,128)(2,1)S(1)} %get-tuple-element.32.after_ref.refs_0_, bf16[32,1024]{1,0:T(8,128)(2,1)S(1)} %collective-permute-done.3.refs_1_, ...), custom_call_target="tpu_custom_call" | custom-call | tf_op jit(solution)/shard_map/readout/pallas_call | solution.py:388
  31.9 10.9 %all_to_all.5 = f32[32,8,128]{2,1,0:T(8,128)S(1)} all-to-all(f32[32,8,128]{2,1,0:T(8,128)S(1)} %readout.1), channel_id=1, replica_groups=mesh['tile'=8,'sec'=4] {'tile','sec'}, dimensions={0} | all-to-all | bytes 262144 | tf_op jit(solution)/shard_map/all_to_all | solution.py:407
  42.9 0.6 %reduce_sum.9 = f32[8,128]{1,0:T(8,128)} reduce(f32[32,8,128]{2,1,0:T(8,128)S(1)} %all_to_all.5, f32[]{:T(128)} %constant.10.clone.1), dimensions={0}, to_apply=%region_0.0 | reduce | flops 31744 | bytes 135172 | tf_op jit(solution)/shard_map/reduce_sum | solution.py:408
Async XLA Ops:
  4.0 3.8 %collective-permute-start.2 = (bf16[48,128]{1,0:T(8,128)(2,1)S(1)}, bf16[48,128]{1,0:T(8,128)(2,1)S(1)}, u32[]{:S(2)}, u32[]{:S(2)}) collective-permute-start(bf16[48,128]{1,0:T(8,128)(2,1)S(1)} %get-tuple-element.21.refs_1_), channel_id=1, source_target_pairs={{0,3},{1,2},{2,1},{3,0},{4,7},{5,6},{6,5},{7,4},{8,11},{9,10},{10,... | collective-permute-start | bytes 36872 | tf_op jit(solution)/shard_map/ppermute | solution.py:284
  6.4 3.7 %collective-permute-start.1 = (bf16[48,128]{1,0:T(8,128)(2,1)S(1)}, bf16[48,128]{1,0:T(8,128)(2,1)S(1)}, u32[]{:S(2)}, u32[]{:S(2)}) collective-permute-start(bf16[48,128]{1,0:T(8,128)(2,1)S(1)} %get-tuple-element.21.refs_1_), channel_id=1, source_target_pairs={{0,2},{1,3},{2,0},{3,1},{4,6},{5,7},{6,4},{7,5},{8,10},{9,11},{10,... | collective-permute-start | bytes 36872 | tf_op jit(solution)/shard_map/ppermute | solution.py:284
  7.1 3.1 %collective-permute-start = (bf16[48,128]{1,0:T(8,128)(2,1)S(1)}, bf16[48,128]{1,0:T(8,128)(2,1)S(1)}, u32[]{:S(2)}, u32[]{:S(2)}) collective-permute-start(bf16[48,128]{1,0:T(8,128)(2,1)S(1)} %get-tuple-element.21.refs_1_), channel_id=1, source_target_pairs={{0,1},{1,0},{2,3},{3,2},{4,5},{5,4},{6,7},{7,6},{8,9},{9,8},{10,11... | collective-permute-start | bytes 36872 | tf_op jit(solution)/shard_map/ppermute | solution.py:284
  11.6 7.4 %collective-permute-start.3 = (bf16[32,1024]{1,0:T(8,128)(2,1)S(1)}, bf16[32,1024]{1,0:T(8,128)(2,1)S(1)}, u32[]{:S(2)}, u32[]{:S(2)}) collective-permute-start(bf16[32,1024]{1,0:T(8,128)(2,1)S(1)} %get-tuple-element.33), channel_id=1, source_target_pairs={{0,4},{4,0},{8,12},{12,8},{16,20},{20,16},{24,28},{28,24},{1,5},{5... | collective-permute-start | bytes 196616 | tf_op jit(solution)/shard_map/ppermute | solution.py:284
  13.1 9.5 %collective-permute-start.4 = (bf16[32,1024]{1,0:T(8,128)(2,1)S(1)}, bf16[32,1024]{1,0:T(8,128)(2,1)S(1)}, u32[]{:S(2)}, u32[]{:S(2)}) collective-permute-start(bf16[32,1024]{1,0:T(8,128)(2,1)S(1)} %get-tuple-element.34), channel_id=1, source_target_pairs={{0,8},{4,12},{8,0},{12,4},{16,24},{20,28},{24,16},{28,20},{1,9},{5... | collective-permute-start | bytes 196616 | tf_op jit(solution)/shard_map/ppermute | solution.py:284
  14.7 11.6 %collective-permute-start.5 = (bf16[32,1024]{1,0:T(8,128)(2,1)S(1)}, bf16[32,1024]{1,0:T(8,128)(2,1)S(1)}, u32[]{:S(2)}, u32[]{:S(2)}) collective-permute-start(bf16[32,1024]{1,0:T(8,128)(2,1)S(1)} %get-tuple-element.35), channel_id=1, source_target_pairs={{0,12},{4,8},{8,4},{12,0},{16,28},{20,24},{24,20},{28,16},{1,13},{... | collective-permute-start | bytes 196616 | tf_op jit(solution)/shard_map/ppermute | solution.py:284
  15.1 11.2 %collective-permute-start.6 = (bf16[32,1024]{1,0:T(8,128)(2,1)S(1)}, bf16[32,1024]{1,0:T(8,128)(2,1)S(1)}, u32[]{:S(2)}, u32[]{:S(2)}) collective-permute-start(bf16[32,1024]{1,0:T(8,128)(2,1)S(1)} %get-tuple-element.36), channel_id=1, source_target_pairs={{0,16},{4,20},{8,24},{12,28},{16,0},{20,4},{24,8},{28,12},{1,17},{... | collective-permute-start | bytes 196616 | tf_op jit(solution)/shard_map/ppermute | solution.py:284
  17.7 10.1 %collective-permute-start.7 = (bf16[32,1024]{1,0:T(8,128)(2,1)S(1)}, bf16[32,1024]{1,0:T(8,128)(2,1)S(1)}, u32[]{:S(2)}, u32[]{:S(2)}) collective-permute-start(bf16[32,1024]{1,0:T(8,128)(2,1)S(1)} %get-tuple-element.37), channel_id=1, source_target_pairs={{0,20},{4,16},{8,28},{12,24},{16,4},{20,0},{24,12},{28,8},{1,21},{... | collective-permute-start | bytes 196616 | tf_op jit(solution)/shard_map/ppermute | solution.py:284
  19.0 8.8 %collective-permute-start.8 = (bf16[32,1024]{1,0:T(8,128)(2,1)S(1)}, bf16[32,1024]{1,0:T(8,128)(2,1)S(1)}, u32[]{:S(2)}, u32[]{:S(2)}) collective-permute-start(bf16[32,1024]{1,0:T(8,128)(2,1)S(1)} %get-tuple-element.38), channel_id=1, source_target_pairs={{0,24},{4,28},{8,16},{12,20},{16,8},{20,12},{24,0},{28,4},{1,25},{... | collective-permute-start | bytes 196616 | tf_op jit(solution)/shard_map/ppermute | solution.py:284
  22.6 7.1 %collective-permute-start.9 = (bf16[32,1024]{1,0:T(8,128)(2,1)S(1)}, bf16[32,1024]{1,0:T(8,128)(2,1)S(1)}, u32[]{:S(2)}, u32[]{:S(2)}) collective-permute-start(bf16[32,1024]{1,0:T(8,128)(2,1)S(1)} %get-tuple-element.39), channel_id=1, source_target_pairs={{0,28},{4,24},{8,20},{12,16},{16,12},{20,8},{24,4},{28,0},{1,29},{... | collective-permute-start | bytes 196616 | tf_op jit(solution)/shard_map/ppermute | solution.py:284

commit v3 on v2

--- a/solution.py
+++ b/solution.py
@@ -12,6 +12,7 @@
 AXIAL = 2.0
 END_ROWS = 48
 PAIRED = True
+SEQUENCE = (0, 6, 1, 7, 2, 5, 3, 4)
 BF = jnp.bfloat16
 F32 = jnp.float32
 PARAMS = pltpu.CompilerParams(vmem_limit_bytes=24 * 1024 * 1024)
@@ -33,7 +34,6 @@
 def local_kernel(
     tiles,
     paired,
-    me_ref,
     v_hbm,
     g_hbm,
     e_hbm,
@@ -42,6 +42,7 @@
     owner_hbm,
     counts_hbm,
     pattern_hbm,
+    transfer_hbm,
     vloc_ref,
     resp_ref,
     ends_ref,
@@ -52,6 +53,7 @@
     spread_ref,
     order_ref,
     pattern_ref,
+    transfer_ref,
     v_ref,
     cable_ref,
     owner_ref,
@@ -67,6 +69,7 @@
         (owner_hbm, owner_ref),
         (counts_hbm, counts_ref),
         (pattern_hbm, pattern_ref),
+        (transfer_hbm, transfer_ref),
     ]
     copies = [pltpu.make_async_copy(src, dst, sems.at[i]) for i, (src, dst) in enumerate(pairs)]
     for copy in copies:
@@ -134,7 +137,7 @@
 
     for copy in copies[5:7]:
         copy.wait()
-    me = me_ref[0]
+    me = lax.axis_index("tile")
     row_count = spread_ref.shape[0]
     capacity = row_count // tiles
     owner = owner_ref[...]
@@ -165,14 +168,13 @@
 
 
 def couple_kernel(sections, block_count, *refs):
-    sec_ref, *refs = refs
     ends_refs, refs = refs[:sections], refs[sections:]
     vloc_ref, resp_ref, g_ref, e_ref, drive_ref, lags_ref, spread_ref, *refs = refs
     final_hbm, *refs = refs
     out_refs, refs = refs[:block_count], refs[block_count:]
     ends32, incoming, leak, final_ref, sem = refs
     steps, cells, width = drive_ref.shape
-    mine = sec_ref[0]
+    mine = lax.axis_index("sec")
     for p in range(sections):
         ends32[mine ^ p] = ends_refs[p][...].astype(F32)
 
@@ -234,24 +236,9 @@
     give.wait()
 
 
-def fetch_kernel(after_ref, transfer_hbm, transfer_ref, sems):
-    del after_ref
-    parts = sems.shape[0]
-    size = transfer_ref.shape[0] // parts
-    copies = []
-    for p in range(parts):
-        span = pl.ds(p * size, size)
-        copies.append(
-            pltpu.make_async_copy(transfer_hbm.at[span], transfer_ref.at[span], sems.at[p])
-        )
-    for copy in copies:
-        copy.start()
-    for copy in copies:
-        copy.wait()
-
-
-def readout_kernel(steps, pattern_ref, order_ref, *refs):
+def readout_kernel(steps, sequence, pattern_ref, order_ref, *refs):
     *block_refs, transfer_ref, out_ref, slots, sums = refs
+    block_refs = [block_refs[sequence.index(p)] for p in range(len(block_refs))]
     slot_count = order_ref.shape[0]
     kinds, width, contacts = transfer_ref.shape[1:]
     for k in range(steps):
@@ -301,7 +288,7 @@
     smem = pl.BlockSpec(memory_space=pltpu.SMEM)
     hbm = pl.BlockSpec(memory_space=pltpu.HBM)
 
-    vloc, resp, ends, cond, rev, driven, lags, spread, order, layout = pl.pallas_call(
+    vloc, resp, ends, cond, rev, driven, lags, spread, order, layout, tiles_here = pl.pallas_call(
         functools.partial(local_kernel, tiles, paired),
         out_shape=(
             jax.ShapeDtypeStruct((steps, cells, width), F32),
@@ -314,20 +301,20 @@
             jax.ShapeDtypeStruct((row_count, cells), BF),
             jax.ShapeDtypeStruct((slot_count, row_count), BF),
             jax.ShapeDtypeStruct((kinds, slot_count), jnp.int32),
+            jax.ShapeDtypeStruct(weights.shape, BF),
         ),
-        in_specs=[smem] + [hbm] * 8,
-        out_specs=(vmem,) * 10,
+        in_specs=[hbm] * 9,
+        out_specs=(vmem,) * 11,
         scratch_shapes=[
             pltpu.VMEM((cells, width), F32),
             pltpu.VMEM((width, width), F32),
             pltpu.VMEM((1, cells), jnp.int32),
             pltpu.SMEM((1, tiles), jnp.int32),
-            pltpu.SemaphoreType.DMA((8,)),
+            pltpu.SemaphoreType.DMA((9,)),
         ],
         compiler_params=PARAMS,
         name="local_steps",
     )(
-        lax.axis_index("tile").reshape(1),
         in_hbm(voltage),
         in_hbm(conductance),
         in_hbm(reversal),
@@ -336,6 +323,7 @@
         in_hbm(owner_map.reshape(1, cells)),
         in_hbm(peer_counts),
         in_hbm(pattern[0].T),
+        in_hbm(weights),
     )
 
     all_ends = exchange([ends] * sections, "sec")
@@ -346,7 +334,7 @@
             jax.ShapeDtypeStruct((cells, width), F32),
         )
         + (jax.ShapeDtypeStruct((row_count // block_count, steps * width), BF),) * block_count,
-        in_specs=[smem] + [vmem] * (sections + 7),
+        in_specs=[vmem] * (sections + 7),
         out_specs=(hbm,) + (vmem,) * block_count,
         scratch_shapes=[
             pltpu.VMEM((sections, END_ROWS, cells), F32),
@@ -358,7 +346,6 @@
         compiler_params=PARAMS,
         name="couple_sections",
     )(
-        lax.axis_index("sec").reshape(1),
         *all_ends,
         vloc,
         resp,
@@ -374,19 +361,11 @@
     else:
         arrived = [lax.all_to_all(outgoing[0], "tile", split_axis=0, concat_axis=0, tiled=True)]
 
-    tiles_here = pl.pallas_call(
-        fetch_kernel,
-        out_shape=jax.ShapeDtypeStruct(weights.shape, BF),
-        in_specs=[vmem, hbm],
-        out_specs=vmem,
-        scratch_shapes=[pltpu.SemaphoreType.DMA((4,))],
-        compiler_params=PARAMS,
-        name="fetch_tiles",
-    )(outgoing[0], in_hbm(weights))
-
+    sequence = SEQUENCE if paired else (0,)
+    arrived = [arrived[p] for p in sequence]
     contact_tiles = CONTACTS // contact_width
     partial_sum = pl.pallas_call(
-        functools.partial(readout_kernel, steps),
+        functools.partial(readout_kernel, steps, sequence),
         out_shape=jax.ShapeDtypeStruct((contact_tiles, steps, contact_width), F32),
         in_specs=[smem] + [vmem] * (len(arrived) + 2),
         out_specs=vmem,

time: 43.7 us -> 42.2 us (0.966)
  Pallas kernels: 10.5 us -> 7.46 us
  starting transfers between devices: 14.3 us -> 15.1 us
  blocking collectives: 10.9 us -> 11.5 us
    pallas_call x2 -> x1, Pallas kernels: 5.76 us -> 2.26 us  [on_device(): pl.pallas_call(functools.partial(readout_kernel, steps, sequence), out_sh...]
    ppermute x10, starting transfers between devices: 14.3 us -> 15.1 us  [exchange(): lax.ppermute(blocks[p], axis, [(i, i ^ p) for i in range(count)])]
    all_to_all x1, blocking collectives: 10.9 us -> 11.5 us  [on_device(): lax.all_to_all(partial_sum, ('tile', 'sec'), split_axis=0, concat_axis=0,...]
  transfers between devices with their start and end apart: 10 -> 10, of which waited for: 4 -> 6; matrix products, arithmetic and copies ran while one was open for 0% -> 0% of each run, Pallas kernels for 8% -> 0%
where the time goes in v3:
time: 42.2 us; the launch traced here: 42.1 us
  starting transfers between devices  15.1 us (36%)
  blocking collectives  11.5 us (27%)
  Pallas kernels  7.46 us (18%)
  waiting for transfers between devices  6.74 us (16%)
  between operations  0.67 us (2%)
  other arithmetic  0.63 us (1%)
    ppermute x10, starting transfers between devices, exchange(): lax.ppermute(blocks[p], axis, [(i, i ^ p) for i in range(count)])  15.1 us
    all_to_all x1, blocking collectives, on_device(): lax.all_to_all(partial_sum, ('tile', 'sec'), split_axis=0, concat_axis=0,...  11.5 us
    ppermute x10, waiting for transfers between devices, exchange(): lax.ppermute(blocks[p], axis, [(i, i ^ p) for i in range(count)])  6.74 us
    pallas_call x1, Pallas kernels, on_device(): pl.pallas_call(functools.partial(local_kernel, tiles, paired), out_shape=...  3.73 us
    pallas_call x1, Pallas kernels, on_device(): pl.pallas_call(functools.partial(readout_kernel, steps, sequence), out_sh...  2.26 us
    pallas_call x1, Pallas kernels, on_device(): pl.pallas_call(functools.partial(couple_kernel, sections, block_count), o...  1.47 us
  transfers between devices with their start and end apart: 10, of which 6 were waited for; matrix products, arithmetic and copies ran while one was open for 0% of the time, Pallas kernels for 0%

profile of v3, /device:TPU:0, one launch (start us, length us, event | category | flops | bytes accessed | tf_op | source)
XLA Modules:
  0.0 42.1 jit_solution(14735056820165457579)
XLA Ops:
  0.6 3.7 %local_steps.1 = (f32[8,128,128]{2,1,0:T(8,128)S(1)}, f32[7,256,128]{2,1,0:T(8,128)S(1)}, bf16[48,128]{1,0:T(8,128)(2,1)S(1)}, f32[128,128]{1,0:T(8,128)S(1)}, f...) custom-call(f32[128,128]{1,0:T(8,128)} %v_hbm.1, ...), custom_call_target="tpu_custom_call" | custom-call | tf_op jit(solution)/shard_map/local_steps/pallas_call | solution.py:291
  4.4 2.4 %collective-permute-start.2 = (bf16[48,128]{1,0:T(8,128)(2,1)S(1)}, bf16[48,128]{1,0:T(8,128)(2,1)S(1)}, u32[]{:S(2)}, u32[]{:S(2)}) collective-permute-start(bf16[48,128]{1,0:T(8,128)(2,1)S(1)} %get-tuple-element.22.refs_0_), channel_id=1, source_target_pairs={{0,3},{1,2},{2,1},{3,0},{4,7},{5,6},{6,5},{7,4},{8,11},{9,10},{10,... | collective-permute-start | bytes 36872 | tf_op jit(solution)/shard_map/ppermute | solution.py:271
  6.8 0.6 %collective-permute-start.1 = (bf16[48,128]{1,0:T(8,128)(2,1)S(1)}, bf16[48,128]{1,0:T(8,128)(2,1)S(1)}, u32[]{:S(2)}, u32[]{:S(2)}) collective-permute-start(bf16[48,128]{1,0:T(8,128)(2,1)S(1)} %get-tuple-element.22.refs_0_), channel_id=1, source_target_pairs={{0,2},{1,3},{2,0},{3,1},{4,6},{5,7},{6,4},{7,5},{8,10},{9,11},{10,... | collective-permute-start | bytes 36872 | tf_op jit(solution)/shard_map/ppermute | solution.py:271
  7.5 0.0 collective-permute-start
  7.5 0.7 %collective-permute-done.2.refs_3_ = bf16[48,128]{1,0:T(8,128)(2,1)S(1)} collective-permute-done((bf16[48,128]{1,0:T(8,128)(2,1)S(1)}, bf16[48,128]{1,0:T(8,128)(2,1)S(1)}, u32[]{:S(2)}, u32[]{:S(2)}) %collective-permute-start.2) | collective-permute-done | bytes 12320 | tf_op jit(solution)/shard_map/ppermute | solution.py:271
  8.2 2.3 %collective-permute-done.1.refs_2_ = bf16[48,128]{1,0:T(8,128)(2,1)S(1)} collective-permute-done((bf16[48,128]{1,0:T(8,128)(2,1)S(1)}, bf16[48,128]{1,0:T(8,128)(2,1)S(1)}, u32[]{:S(2)}, u32[]{:S(2)}) %collective-permute-start.1) | collective-permute-done | bytes 12320 | tf_op jit(solution)/shard_map/ppermute | solution.py:271
  10.5 0.0 collective-permute-done.refs_1_
  10.5 1.5 %couple_sections.1 = (f32[128,128]{1,0:T(8,128)}, bf16[32,1024]{1,0:T(8,128)(2,1)S(1)}, bf16[32,1024]{1,0:T(8,128)(2,1)S(1)}, bf16[32,1024]{1,0:T(8,128)(2,1)S(1...) custom-call(bf16[48,128]{1,0:T(8,128)(2,1)S(1)} %get-tuple-element.2, ...), custom_call_target="tpu_custom_call" | custom-call | tf_op jit(solution)/shard_map/couple_sections/pallas_call | solution.py:331
  12.0 3.7 %collective-permute-start.3 = (bf16[32,1024]{1,0:T(8,128)(2,1)S(1)}, bf16[32,1024]{1,0:T(8,128)(2,1)S(1)}, u32[]{:S(2)}, u32[]{:S(2)}) collective-permute-start(bf16[32,1024]{1,0:T(8,128)(2,1)S(1)} %get-tuple-element.34), channel_id=1, source_target_pairs={{0,24},{4,28},{8,16},{12,20},{16,8},{20,12},{24,0},{28,4},{1,25},{... | collective-permute-start | bytes 196616 | tf_op jit(solution)/shard_map/ppermute | solution.py:271
  15.7 1.5 %collective-permute-start.4 = (bf16[32,1024]{1,0:T(8,128)(2,1)S(1)}, bf16[32,1024]{1,0:T(8,128)(2,1)S(1)}, u32[]{:S(2)}, u32[]{:S(2)}) collective-permute-start(bf16[32,1024]{1,0:T(8,128)(2,1)S(1)} %get-tuple-element.35), channel_id=1, source_target_pairs={{0,4},{4,0},{8,12},{12,8},{16,20},{20,16},{24,28},{28,24},{1,5},{5... | collective-permute-start | bytes 196616 | tf_op jit(solution)/shard_map/ppermute | solution.py:271
  17.2 0.2 collective-permute-start.5
  17.3 0.0 collective-permute-start.6
  17.4 5.1 %collective-permute-start.7 = (bf16[32,1024]{1,0:T(8,128)(2,1)S(1)}, bf16[32,1024]{1,0:T(8,128)(2,1)S(1)}, u32[]{:S(2)}, u32[]{:S(2)}) collective-permute-start(bf16[32,1024]{1,0:T(8,128)(2,1)S(1)} %get-tuple-element.38), channel_id=1, source_target_pairs={{0,20},{4,16},{8,28},{12,24},{16,4},{20,0},{24,12},{28,8},{1,21},{... | collective-permute-start | bytes 196616 | tf_op jit(solution)/shard_map/ppermute | solution.py:271
  22.5 0.0 collective-permute-done.3.refs_1_
  22.5 0.0 collective-permute-start.8
  22.5 0.0 collective-permute-done.4.refs_2_
  22.5 1.5 %collective-permute-start.9 = (bf16[32,1024]{1,0:T(8,128)(2,1)S(1)}, bf16[32,1024]{1,0:T(8,128)(2,1)S(1)}, u32[]{:S(2)}, u32[]{:S(2)}) collective-permute-start(bf16[32,1024]{1,0:T(8,128)(2,1)S(1)} %get-tuple-element.40), channel_id=1, source_target_pairs={{0,16},{4,20},{8,24},{12,28},{16,0},{20,4},{24,8},{28,12},{1,17},{... | collective-permute-start | bytes 196616 | tf_op jit(solution)/shard_map/ppermute | solution.py:271
  24.0 1.0 %collective-permute-done.5.refs_3_ = bf16[32,1024]{1,0:T(8,128)(2,1)S(1)} collective-permute-done((bf16[32,1024]{1,0:T(8,128)(2,1)S(1)}, bf16[32,1024]{1,0:T(8,128)(2,1)S(1)}, u32[]{:S(2)}, u32[]{:S(2)}) %collective-permute-start.5) | collective-permute-done | bytes 65568 | tf_op jit(solution)/shard_map/ppermute | solution.py:271
  25.0 0.0 collective-permute-done.6.refs_4_
  25.0 0.4 %collective-permute-done.7.refs_5_ = bf16[32,1024]{1,0:T(8,128)(2,1)S(1)} collective-permute-done((bf16[32,1024]{1,0:T(8,128)(2,1)S(1)}, bf16[32,1024]{1,0:T(8,128)(2,1)S(1)}, u32[]{:S(2)}, u32[]{:S(2)}) %collective-permute-start.7) | collective-permute-done | bytes 65568 | tf_op jit(solution)/shard_map/ppermute | solution.py:271
  25.4 2.2 %collective-permute-done.8.refs_6_ = bf16[32,1024]{1,0:T(8,128)(2,1)S(1)} collective-permute-done((bf16[32,1024]{1,0:T(8,128)(2,1)S(1)}, bf16[32,1024]{1,0:T(8,128)(2,1)S(1)}, u32[]{:S(2)}, u32[]{:S(2)}) %collective-permute-start.8) | collective-permute-done | bytes 65568 | tf_op jit(solution)/shard_map/ppermute | solution.py:271
  27.6 0.1 collective-permute-done.9.refs_7_
  27.7 2.3 %readout.1 = f32[32,8,128]{2,1,0:T(8,128)S(1)} custom-call(s32[2,128]{1,0:T(2,128)S(1)} %get-tuple-element.31.pattern_ref, bf16[128,256]{1,0:T(8,128)(2,1)S(1)} %get-tuple-element.32.order_ref, bf16[32,1024]{1,0:T(8,128)(2,1)S(1)} %get-tuple-element.33.refs_0_, bf16[32,1024]{1,0:T(8,128)(2,1)S(1)} %collective-permute-done.3.refs_1_, ...), custom_call_target="tpu_custom_call" | custom-call | tf_op jit(solution)/shard_map/readout/pallas_call | solution.py:367
  30.0 11.5 %all_to_all.5 = f32[32,8,128]{2,1,0:T(8,128)S(1)} all-to-all(f32[32,8,128]{2,1,0:T(8,128)S(1)} %readout.1), channel_id=1, replica_groups=mesh['tile'=8,'sec'=4] {'tile','sec'}, dimensions={0} | all-to-all | bytes 262144 | tf_op jit(solution)/shard_map/all_to_all | solution.py:386
  41.5 0.6 %reduce_sum.9 = f32[8,128]{1,0:T(8,128)} reduce(f32[32,8,128]{2,1,0:T(8,128)S(1)} %all_to_all.5, f32[]{:T(128)} %constant.0.clone.1), dimensions={0}, to_apply=%region_0.0 | reduce | flops 31744 | bytes 135172 | tf_op jit(solution)/shard_map/reduce_sum | solution.py:387
Async XLA Ops:
  4.4 3.8 %collective-permute-start.2 = (bf16[48,128]{1,0:T(8,128)(2,1)S(1)}, bf16[48,128]{1,0:T(8,128)(2,1)S(1)}, u32[]{:S(2)}, u32[]{:S(2)}) collective-permute-start(bf16[48,128]{1,0:T(8,128)(2,1)S(1)} %get-tuple-element.22.refs_0_), channel_id=1, source_target_pairs={{0,3},{1,2},{2,1},{3,0},{4,7},{5,6},{6,5},{7,4},{8,11},{9,10},{10,... | collective-permute-start | bytes 36872 | tf_op jit(solution)/shard_map/ppermute | solution.py:271
  6.8 3.7 %collective-permute-start.1 = (bf16[48,128]{1,0:T(8,128)(2,1)S(1)}, bf16[48,128]{1,0:T(8,128)(2,1)S(1)}, u32[]{:S(2)}, u32[]{:S(2)}) collective-permute-start(bf16[48,128]{1,0:T(8,128)(2,1)S(1)} %get-tuple-element.22.refs_0_), channel_id=1, source_target_pairs={{0,2},{1,3},{2,0},{3,1},{4,6},{5,7},{6,4},{7,5},{8,10},{9,11},{10,... | collective-permute-start | bytes 36872 | tf_op jit(solution)/shard_map/ppermute | solution.py:271
  7.5 3.1 %collective-permute-start = (bf16[48,128]{1,0:T(8,128)(2,1)S(1)}, bf16[48,128]{1,0:T(8,128)(2,1)S(1)}, u32[]{:S(2)}, u32[]{:S(2)}) collective-permute-start(bf16[48,128]{1,0:T(8,128)(2,1)S(1)} %get-tuple-element.22.refs_0_), channel_id=1, source_target_pairs={{0,1},{1,0},{2,3},{3,2},{4,5},{5,4},{6,7},{7,6},{8,9},{9,8},{10,11... | collective-permute-start | bytes 36872 | tf_op jit(solution)/shard_map/ppermute | solution.py:271
  12.0 10.5 %collective-permute-start.3 = (bf16[32,1024]{1,0:T(8,128)(2,1)S(1)}, bf16[32,1024]{1,0:T(8,128)(2,1)S(1)}, u32[]{:S(2)}, u32[]{:S(2)}) collective-permute-start(bf16[32,1024]{1,0:T(8,128)(2,1)S(1)} %get-tuple-element.34), channel_id=1, source_target_pairs={{0,24},{4,28},{8,16},{12,20},{16,8},{20,12},{24,0},{28,4},{1,25},{... | collective-permute-start | bytes 196616 | tf_op jit(solution)/shard_map/ppermute | solution.py:271
  15.7 6.8 %collective-permute-start.4 = (bf16[32,1024]{1,0:T(8,128)(2,1)S(1)}, bf16[32,1024]{1,0:T(8,128)(2,1)S(1)}, u32[]{:S(2)}, u32[]{:S(2)}) collective-permute-start(bf16[32,1024]{1,0:T(8,128)(2,1)S(1)} %get-tuple-element.35), channel_id=1, source_target_pairs={{0,4},{4,0},{8,12},{12,8},{16,20},{20,16},{24,28},{28,24},{1,5},{5... | collective-permute-start | bytes 196616 | tf_op jit(solution)/shard_map/ppermute | solution.py:271
  17.2 7.8 %collective-permute-start.5 = (bf16[32,1024]{1,0:T(8,128)(2,1)S(1)}, bf16[32,1024]{1,0:T(8,128)(2,1)S(1)}, u32[]{:S(2)}, u32[]{:S(2)}) collective-permute-start(bf16[32,1024]{1,0:T(8,128)(2,1)S(1)} %get-tuple-element.36), channel_id=1, source_target_pairs={{0,28},{4,24},{8,20},{12,16},{16,12},{20,8},{24,4},{28,0},{1,29},{... | collective-permute-start | bytes 196616 | tf_op jit(solution)/shard_map/ppermute | solution.py:271
  17.3 7.7 %collective-permute-start.6 = (bf16[32,1024]{1,0:T(8,128)(2,1)S(1)}, bf16[32,1024]{1,0:T(8,128)(2,1)S(1)}, u32[]{:S(2)}, u32[]{:S(2)}) collective-permute-start(bf16[32,1024]{1,0:T(8,128)(2,1)S(1)} %get-tuple-element.37), channel_id=1, source_target_pairs={{0,8},{4,12},{8,0},{12,4},{16,24},{20,28},{24,16},{28,20},{1,9},{5... | collective-permute-start | bytes 196616 | tf_op jit(solution)/shard_map/ppermute | solution.py:271
  17.4 8.1 %collective-permute-start.7 = (bf16[32,1024]{1,0:T(8,128)(2,1)S(1)}, bf16[32,1024]{1,0:T(8,128)(2,1)S(1)}, u32[]{:S(2)}, u32[]{:S(2)}) collective-permute-start(bf16[32,1024]{1,0:T(8,128)(2,1)S(1)} %get-tuple-element.38), channel_id=1, source_target_pairs={{0,20},{4,16},{8,28},{12,24},{16,4},{20,0},{24,12},{28,8},{1,21},{... | collective-permute-start | bytes 196616 | tf_op jit(solution)/shard_map/ppermute | solution.py:271
  22.5 5.2 %collective-permute-start.8 = (bf16[32,1024]{1,0:T(8,128)(2,1)S(1)}, bf16[32,1024]{1,0:T(8,128)(2,1)S(1)}, u32[]{:S(2)}, u32[]{:S(2)}) collective-permute-start(bf16[32,1024]{1,0:T(8,128)(2,1)S(1)} %get-tuple-element.39), channel_id=1, source_target_pairs={{0,12},{4,8},{8,4},{12,0},{16,28},{20,24},{24,20},{28,16},{1,13},{... | collective-permute-start | bytes 196616 | tf_op jit(solution)/shard_map/ppermute | solution.py:271
  22.5 5.2 %collective-permute-start.9 = (bf16[32,1024]{1,0:T(8,128)(2,1)S(1)}, bf16[32,1024]{1,0:T(8,128)(2,1)S(1)}, u32[]{:S(2)}, u32[]{:S(2)}) collective-permute-start(bf16[32,1024]{1,0:T(8,128)(2,1)S(1)} %get-tuple-element.40), channel_id=1, source_target_pairs={{0,16},{4,20},{8,24},{12,28},{16,0},{20,4},{24,8},{28,12},{1,17},{... | collective-permute-start | bytes 196616 | tf_op jit(solution)/shard_map/ppermute | solution.py:271

commit v4 on v3

v4 whole, which is shorter than its diff:
```python
import functools

import jax
import jax.numpy as jnp
from jax import lax
from jax.experimental import pallas as pl
from jax.experimental.pallas import tpu as pltpu
from jax.sharding import PartitionSpec as P

CONTACTS = 4096
TIME_STEP = 0.25
AXIAL = 2.0
END_ROWS = 48
PAIRED = True
PARTS = (48, 16, 64)
SEQUENCE = (0, 6, 1, 7, 2, 5, 3, 4)
BF = jnp.bfloat16
F32 = jnp.float32
PARAMS = pltpu.CompilerParams(vmem_limit_bytes=24 * 1024 * 1024)


def split_hi_lo(x):
    hi = x.astype(BF)
    return hi, (x - hi.astype(F32)).astype(BF)


def one_hot(condition):
    return jnp.where(condition, 1.0, 0.0).astype(BF)


def iota(shape, dim):
    return lax.broadcasted_iota(jnp.int32, shape, dim)


def hi_lo_weights(cable):
    cable_hi, cable_lo = split_hi_lo(cable)
    half = jnp.concatenate([cable_hi, cable_lo], axis=1)
    return jnp.concatenate([half, half], axis=0)


def solve(rhs, weights):
    width = rhs.shape[1]
    hi, lo = split_hi_lo(rhs)
    both = jnp.dot(jnp.concatenate([hi, lo], axis=1), weights, preferred_element_type=F32)
    return both[:, :width] + both[:, width:]


def keep_and_source(cond, rev):
    lane = iota(cond.shape, 1)
    at_end = (lane == 0) | (lane == cond.shape[1] - 1)
    keep = 1.0 - TIME_STEP * cond - jnp.where(at_end, TIME_STEP * AXIAL, 0.0).astype(F32)
    return keep, TIME_STEP * cond * rev


def start_all(pairs, sems):
    copies = [pltpu.make_async_copy(src, dst, sems.at[i]) for i, (src, dst) in enumerate(pairs)]
    for copy in copies:
        copy.start()
    return copies


def local_kernel(
    v_hbm,
    g_hbm,
    e_hbm,
    drive_hbm,
    cable_hbm,
    transfer_hbm,
    vloc_ref,
    resp_ref,
    ends_ref,
    g_ref,
    e_ref,
    drive_ref,
    turned_ref,
    early_ref,
    v_ref,
    cable_ref,
    sems,
):
    copies = start_all(
        [
            (g_hbm, g_ref),
            (v_hbm, v_ref),
            (cable_hbm, cable_ref),
            (e_hbm, e_ref),
            (drive_hbm, drive_ref),
            (transfer_hbm.at[pl.ds(0, PARTS[0])], early_ref),
        ],
        sems,
    )
    for copy in copies[:5]:
        copy.wait()
    cells, width = v_ref.shape
    steps = drive_ref.shape[0]
    keep, source = keep_and_source(g_ref[...], e_ref[...])
    cable = cable_ref[...].T
    turned_ref[...] = cable
    weights = hi_lo_weights(cable)
    lane = iota((cells, width), 1)

    def with_ends(table, x, row):
        return jnp.where((lane >= row) & (lane < row + 2), pltpu.roll(x, row + 1, 1), table)

    voltage = v_ref[...]
    left = jnp.broadcast_to(TIME_STEP * AXIAL * cable[0:1, :], (cells, width))
    right = jnp.broadcast_to(TIME_STEP * AXIAL * cable[width - 1 : width, :], (cells, width))
    left_row, right_row = 2 * steps, 4 * steps
    table = with_ends(jnp.zeros((cells, width), F32), voltage, 0)
    table = with_ends(with_ends(table, left, left_row), right, right_row)
    for k in range(steps - 1):
        rhs = voltage * keep + source + TIME_STEP * drive_ref[k].astype(F32)
        voltage = solve(rhs, weights)
        left = solve(left * keep, weights)
        right = solve(right * keep, weights)
        vloc_ref[k] = voltage
        resp_ref[k, :cells] = left
        resp_ref[k, cells:] = right
        table = with_ends(table, voltage, 2 * (k + 1))
        if k < steps - 2:
            table = with_ends(table, left, left_row + 2 * (k + 1))
            table = with_ends(table, right, right_row + 2 * (k + 1))
    ends_ref[...] = table.T[:END_ROWS].astype(BF)
    copies[5].wait()


def prepare_kernel(
    tiles,
    paired,
    vloc_ref,
    g_ref,
    e_ref,
    drive_ref,
    turned_ref,
    owner_hbm,
    counts_hbm,
    pattern_hbm,
    transfer_hbm,
    vlast_ref,
    spread_ref,
    order_ref,
    pattern_ref,
    middle_ref,
    owner_ref,
    counts_ref,
    sems,
):
    copies = start_all(
        [
            (owner_hbm, owner_ref),
            (counts_hbm, counts_ref),
            (pattern_hbm, pattern_ref),
            (transfer_hbm.at[pl.ds(PARTS[0], PARTS[1])], middle_ref),
        ],
        sems,
    )
    steps, cells, _ = drive_ref.shape
    keep, source = keep_and_source(g_ref[...], e_ref[...])
    rhs = vloc_ref[steps - 2] * keep + source + TIME_STEP * drive_ref[steps - 1].astype(F32)
    vlast_ref[...] = solve(rhs, hi_lo_weights(turned_ref[...]))

    for copy in copies[:2]:
        copy.wait()
    me = lax.axis_index("tile")
    row_count = spread_ref.shape[0]
    capacity = row_count // tiles
    owner = owner_ref[...]
    member = owner == iota((tiles, cells), 0)
    before = iota((cells, cells), 0) < iota((cells, cells), 1)
    rank = jnp.dot(one_hot(member), one_hot(before), preferred_element_type=F32)
    rank = jnp.sum(jnp.where(member, rank, 0.0), axis=0, keepdims=True).astype(jnp.int32)
    to = owner ^ me if paired else owner
    spread_ref[...] = one_hot(iota((row_count, cells), 0) == to * capacity + rank)

    counts = [counts_ref[0, u] for u in range(tiles)]
    row = iota((1, row_count), 1)
    slot_of = jnp.full((1, row_count), -1, jnp.int32)
    start = jnp.int32(0)
    for b in range(tiles):
        if paired:
            sender = b ^ me
            count = counts_ref[0, sender]
            start = sum(jnp.where(u < sender, counts[u], 0) for u in range(tiles))
        else:
            count = counts[b]
            start = start + (counts[b - 1] if b else 0)
        place = row - b * capacity
        slot_of = jnp.where((place >= 0) & (place < count), place + start, slot_of)
    order_ref[...] = one_hot(iota(order_ref.shape, 0) == slot_of)
    for copy in copies[2:]:
        copy.wait()


def couple_kernel(sections, block_count, *refs):
    ends_refs, refs = refs[:sections], refs[sections:]
    vloc_ref, vlast_ref, resp_ref, g_ref, e_ref, drive_ref, turned_ref, spread_ref, *refs = refs
    final_hbm, *refs = refs
    out_refs, refs = refs[:block_count], refs[block_count:]
    ends32, incoming, leak, final_ref, sem = refs
    steps, cells, width = drive_ref.shape
    mine = lax.axis_index("sec")
    for p in range(sections):
        ends32[mine ^ p] = ends_refs[p][...].astype(F32)

    def rows(q):
        return ends32[:, q, :]

    def lagged(row):
        return [None] + [rows(row + 2 * l) for l in range(steps - 1)]

    left_b, left_a = lagged(2 * steps), lagged(2 * steps + 1)
    right_b, right_a = lagged(4 * steps), lagged(4 * steps + 1)
    zero = jnp.zeros((1, cells), F32)
    from_left, from_right = [], []
    for k in range(steps):
        last, first = rows(2 * k), rows(2 * k + 1)
        for j in range(k):
            first = first + (left_a[k - j] * from_left[j] + right_a[k - j] * from_right[j])
            last = last + (left_b[k - j] * from_left[j] + right_b[k - j] * from_right[j])
        from_left.append(jnp.concatenate([zero, last[:-1]], axis=0))
        from_right.append(jnp.concatenate([first[1:], zero], axis=0))
    own = iota((sections, cells), 0) == mine
    for j in range(steps):
        incoming[pl.ds(2 * j, 1), :] = jnp.sum(
            jnp.where(own, from_left[j], 0.0), axis=0, keepdims=True
        )
        incoming[pl.ds(2 * j + 1, 1), :] = jnp.sum(
            jnp.where(own, from_right[j], 0.0), axis=0, keepdims=True
        )
    by_cell = incoming[...].T

    block = 8
    lag_left = jnp.broadcast_to(TIME_STEP * AXIAL * turned_ref[0:1, :], (block, width))
    lag_right = jnp.broadcast_to(
        TIME_STEP * AXIAL * turned_ref[width - 1 : width, :], (block, width)
    )
    for c in range(0, cells, block):
        span = slice(c, c + block)
        unit = [
            jnp.broadcast_to(by_cell[span, q : q + 1], (block, width)) for q in range(2 * steps)
        ]
        lefts = [None, lag_left] + [resp_ref[l, span, :] for l in range(steps - 1)]
        rights = [None, lag_right] + [
            resp_ref[l, cells + c : cells + c + block, :] for l in range(steps - 1)
        ]
        cond, rev = g_ref[span, :], e_ref[span, :]
        for k in range(1, steps + 1):
            total = vloc_ref[k - 1, span, :] if k < steps else vlast_ref[span, :]
            for j in range(k):
                total = total + (unit[2 * j] * lefts[k - j] + unit[2 * j + 1] * rights[k - j])
            leak[k - 1, span, :] = cond * (total - rev)
        final_ref[span, :] = total
    give = pltpu.make_async_copy(final_ref, final_hbm, sem)
    give.start()

    capacity = out_refs[0].shape[0]
    for k in range(steps):
        current = (leak[k] - drive_ref[k].astype(F32)).astype(BF)
        placed = jnp.dot(spread_ref[...], current, preferred_element_type=F32).astype(BF)
        for b in range(block_count):
            out_refs[b][:, k * width : (k + 1) * width] = placed[b * capacity : (b + 1) * capacity]
    give.wait()


def fetch_kernel(after_ref, transfer_hbm, late_ref, sem):
    del after_ref
    copy = pltpu.make_async_copy(
        transfer_hbm.at[pl.ds(PARTS[0] + PARTS[1], PARTS[2])], late_ref, sem
    )
    copy.start()
    copy.wait()


def readout_kernel(steps, sequence, pattern_ref, order_ref, *refs):
    *block_refs, early_ref, middle_ref, late_ref, out_ref, slots, sums = refs
    held = [(ref, at) for ref in (early_ref, middle_ref, late_ref) for at in range(ref.shape[0])]
    block_refs = [block_refs[sequence.index(p)] for p in range(len(block_refs))]
    slot_count = order_ref.shape[0]
    kinds, width, contacts = early_ref.shape[1:]
    for k in range(steps):
        span = slice(k * width, (k + 1) * width)
        rows = jnp.concatenate([ref[:, span] for ref in block_refs], axis=0)
        slots[pl.ds(k, slot_count, stride=steps), :] = jnp.dot(
            order_ref[...], rows, preferred_element_type=F32
        )
    sums[...] = jnp.zeros_like(sums)
    ways = sums.shape[0]
    turn = 0
    for s in range(slot_count):
        current = slots[s * steps : (s + 1) * steps, :].astype(BF)
        ref, at = held[s]
        tile = jnp.concatenate([ref[at, t] for t in range(kinds)], axis=1)
        reach = jnp.dot(current, tile, preferred_element_type=F32)
        for t in range(kinds):
            sums[turn % ways, pattern_ref[t, s]] += reach[:, t * contacts : (t + 1) * contacts]
            turn += 1
    out_ref[...] = sum(sums[w] for w in range(ways))


def in_hbm(x):
    return pltpu.with_memory_space_constraint(x, pltpu.HBM)


def exchange(blocks, axis):
    count = lax.axis_size(axis)
    arrived = [blocks[0]]
    for p in range(1, count):
        arrived.append(lax.ppermute(blocks[p], axis, [(i, i ^ p) for i in range(count)]))
    return arrived


def on_device(
    voltage, conductance, reversal, drive, inv_cable, owner_map, peer_counts, pattern, transfer
):
    cells, width = voltage.shape
    steps = drive.shape[0]
    tiles = lax.axis_size("tile")
    sections = lax.axis_size("sec")
    capacity = 2 * cells // tiles
    row_count = tiles * capacity
    weights = transfer[0]
    slot_count, kinds, _, contact_width = weights.shape
    paired = PAIRED and tiles == 8
    vmem = pl.BlockSpec(memory_space=pltpu.VMEM)
    smem = pl.BlockSpec(memory_space=pltpu.SMEM)
    hbm = pl.BlockSpec(memory_space=pltpu.HBM)

    vloc, resp, ends, cond, rev, driven, turned, early_tiles = pl.pallas_call(
        local_kernel,
        out_shape=(
            jax.ShapeDtypeStruct((steps - 1, cells, width), F32),
            jax.ShapeDtypeStruct((steps - 1, 2 * cells, width), F32),
            jax.ShapeDtypeStruct((END_ROWS, cells), BF),
            jax.ShapeDtypeStruct((cells, width), F32),
            jax.ShapeDtypeStruct((cells, width), F32),
            jax.ShapeDtypeStruct((steps, cells, width), BF),
            jax.ShapeDtypeStruct((width, width), F32),
            jax.ShapeDtypeStruct((PARTS[0],) + weights.shape[1:], BF),
        ),
        in_specs=[hbm] * 6,
        out_specs=(vmem,) * 8,
        scratch_shapes=[
            pltpu.VMEM((cells, width), F32),
            pltpu.VMEM((width, width), F32),
            pltpu.SemaphoreType.DMA((6,)),
        ],
        compiler_params=PARAMS,
        name="local_steps",
    )(
        in_hbm(voltage),
        in_hbm(conductance),
        in_hbm(reversal),
        in_hbm(drive),
        in_hbm(inv_cable),
        in_hbm(weights),
    )

    vlast, spread, order, layout, middle_tiles = pl.pallas_call(
        functools.partial(prepare_kernel, tiles, paired),
        out_shape=(
            jax.ShapeDtypeStruct((cells, width), F32),
            jax.ShapeDtypeStruct((row_count, cells), BF),
            jax.ShapeDtypeStruct((slot_count, row_count), BF),
            jax.ShapeDtypeStruct((kinds, slot_count), jnp.int32),
            jax.ShapeDtypeStruct((PARTS[1],) + weights.shape[1:], BF),
        ),
        in_specs=[vmem] * 5 + [hbm] * 4,
        out_specs=(vmem,) * 5,
        scratch_shapes=[
            pltpu.VMEM((1, cells), jnp.int32),
            pltpu.SMEM((1, tiles), jnp.int32),
            pltpu.SemaphoreType.DMA((4,)),
        ],
        compiler_params=PARAMS,
        name="prepare_rows",
    )(
        vloc,
        cond,
        rev,
        driven,
        turned,
        in_hbm(owner_map.reshape(1, cells)),
        in_hbm(peer_counts),
        in_hbm(pattern[0].T),
        in_hbm(weights),
    )

    all_ends = exchange([ends] * sections, "sec")
    block_count = tiles if paired else 1
    final_voltage, *outgoing = pl.pallas_call(
        functools.partial(couple_kernel, sections, block_count),
        out_shape=(
            jax.ShapeDtypeStruct((cells, width), F32),
        )
        + (jax.ShapeDtypeStruct((row_count // block_count, steps * width), BF),) * block_count,
        in_specs=[vmem] * (sections + 8),
        out_specs=(hbm,) + (vmem,) * block_count,
        scratch_shapes=[
            pltpu.VMEM((sections, END_ROWS, cells), F32),
            pltpu.VMEM((2 * steps, cells), F32),
            pltpu.VMEM((steps, cells, width), F32),
            pltpu.VMEM((cells, width), F32),
            pltpu.SemaphoreType.DMA,
        ],
        compiler_params=PARAMS,
        name="couple_sections",
    )(
        *all_ends,
        vloc,
        vlast,
        resp,
        cond,
        rev,
        driven,
        turned,
        spread,
    )

    if paired:
        arrived = exchange(outgoing, "tile")
    else:
        arrived = [lax.all_to_all(outgoing[0], "tile", split_axis=0, concat_axis=0, tiled=True)]

    late_tiles = pl.pallas_call(
        fetch_kernel,
        out_shape=jax.ShapeDtypeStruct((PARTS[2],) + weights.shape[1:], BF),
        in_specs=[vmem, hbm],
        out_specs=vmem,
        scratch_shapes=[pltpu.SemaphoreType.DMA],
        compiler_params=PARAMS,
        name="fetch_tiles",
    )(outgoing[0], in_hbm(weights))

    sequence = SEQUENCE if paired else (0,)
    arrived = [arrived[p] for p in sequence]
    contact_tiles = CONTACTS // contact_width
    partial_sum = pl.pallas_call(
        functools.partial(readout_kernel, steps, sequence),
        out_shape=jax.ShapeDtypeStruct((contact_tiles, steps, contact_width), F32),
        in_specs=[smem] + [vmem] * (len(arrived) + 4),
        out_specs=vmem,
        scratch_shapes=[
            pltpu.VMEM((slot_count * steps, width), F32),
            pltpu.VMEM((4, contact_tiles, steps, contact_width), F32),
        ],
        compiler_params=PARAMS,
        name="readout",
    )(layout, order, *arrived, early_tiles, middle_tiles, late_tiles)

    devices = tiles * sections
    share = CONTACTS // devices
    parts = contact_width // share
    if parts > 1:
        partial_sum = partial_sum.reshape(contact_tiles, steps, parts, share)
        partial_sum = partial_sum.transpose(0, 2, 1, 3).reshape(devices, steps, share)
    shares = lax.all_to_all(partial_sum, ("tile", "sec"), split_axis=0, concat_axis=0, tiled=True)
    return final_voltage, jnp.sum(shares, axis=0)


def solution(mesh):
    placed = (
        P("tile", "sec"),
        P("tile", "sec"),
        P("tile", "sec"),
        P(None, "tile", "sec"),
        P(),
        P("tile"),
        P("tile", None),
        P("sec", "tile", None),
        P("sec", "tile", None, None, None),
    )
    return jax.shard_map(
        on_device,
        mesh=mesh,
        in_specs=placed,
        out_specs=(P("tile", "sec"), P(None, ("tile", "sec"))),
        check_vma=False,
    )
```

time: 42.2 us -> 40.9 us (0.969)
  waiting for transfers between devices: 6.74 us -> 3.17 us
  Pallas kernels: 7.46 us -> 9.65 us
    ppermute x10, waiting for transfers between devices: 6.74 us -> 3.17 us  [exchange(): lax.ppermute(blocks[p], axis, [(i, i ^ p) for i in range(count)])]
    pallas_call x1 -> x3, Pallas kernels: 3.73 us -> 5.88 us  [the longest x1 2.36 us: on_device(): pl.pallas_call(local_kernel, out_shape=(jax.ShapeDtypeStruct((steps - 1,...]
  transfers between devices with their start and end apart: 10 -> 10, of which waited for: 6 -> 3; matrix products, arithmetic and copies ran while one was open for 0% -> 0% of each run, Pallas kernels for 0% -> 9%
where the time goes in v4:
time: 40.9 us; the launch traced here: 40.7 us
  starting transfers between devices  15.1 us (37%)
  blocking collectives  11.5 us (28%)
  Pallas kernels  9.65 us (24%)
  waiting for transfers between devices  3.17 us (8%)
  between operations  0.71 us (2%)
  other arithmetic  0.63 us (2%)
    ppermute x10, starting transfers between devices, exchange(): lax.ppermute(blocks[p], axis, [(i, i ^ p) for i in range(count)])  15.1 us
    all_to_all x1, blocking collectives, on_device(): lax.all_to_all(partial_sum, ('tile', 'sec'), split_axis=0, concat_axis=0,...  11.5 us
    ppermute x10, waiting for transfers between devices, exchange(): lax.ppermute(blocks[p], axis, [(i, i ^ p) for i in range(count)])  3.17 us
    pallas_call x1, Pallas kernels, on_device(): pl.pallas_call(local_kernel, out_shape=(jax.ShapeDtypeStruct((steps - 1,...  2.36 us
    pallas_call x1, Pallas kernels, on_device(): pl.pallas_call(functools.partial(readout_kernel, steps, sequence), out_sh...  2.27 us
    pallas_call x1, Pallas kernels, on_device(): pl.pallas_call(fetch_kernel, out_shape=jax.ShapeDtypeStruct((PARTS[2],) +...  2.2 us
    pallas_call x1, Pallas kernels, on_device(): pl.pallas_call(functools.partial(couple_kernel, sections, block_count), o...  1.5 us
    pallas_call x1, Pallas kernels, on_device(): pl.pallas_call(functools.partial(prepare_kernel, tiles, paired), out_shap...  1.33 us
  transfers between devices with their start and end apart: 10, of which 3 were waited for; matrix products, arithmetic and copies ran while one was open for 0% of the time, Pallas kernels for 9%

profile of v4, /device:TPU:0, one launch (start us, length us, event | category | flops | bytes accessed | tf_op | source)
XLA Modules:
  0.0 40.7 jit_solution(5343972516050012251)
XLA Ops:
  0.6 2.4 %local_steps.1 = (f32[7,128,128]{2,1,0:T(8,128)S(1)}, f32[7,256,128]{2,1,0:T(8,128)S(1)}, bf16[48,128]{1,0:T(8,128)(2,1)S(1)}, f32[128,128]{1,0:T(8,128)S(1)}, f...) custom-call(f32[128,128]{1,0:T(8,128)} %v_hbm.1, ...), custom_call_target="tpu_custom_call" | custom-call | tf_op jit(solution)/shard_map/local_steps/pallas_call | solution.py:328
  3.0 2.4 %collective-permute-start.2 = (bf16[48,128]{1,0:T(8,128)(2,1)S(1)}, bf16[48,128]{1,0:T(8,128)(2,1)S(1)}, u32[]{:S(2)}, u32[]{:S(2)}) collective-permute-start(bf16[48,128]{1,0:T(8,128)(2,1)S(1)} %get-tuple-element.24.refs_0_), channel_id=1, source_target_pairs={{0,3},{1,2},{2,1},{3,0},{4,7},{5,6},{6,5},{7,4},{8,11},{9,10},{10,... | collective-permute-start | bytes 36872 | tf_op jit(solution)/shard_map/ppermute | solution.py:308
  5.4 0.6 %collective-permute-start.1 = (bf16[48,128]{1,0:T(8,128)(2,1)S(1)}, bf16[48,128]{1,0:T(8,128)(2,1)S(1)}, u32[]{:S(2)}, u32[]{:S(2)}) collective-permute-start(bf16[48,128]{1,0:T(8,128)(2,1)S(1)} %get-tuple-element.24.refs_0_), channel_id=1, source_target_pairs={{0,2},{1,3},{2,0},{3,1},{4,6},{5,7},{6,4},{7,5},{8,10},{9,11},{10,... | collective-permute-start | bytes 36872 | tf_op jit(solution)/shard_map/ppermute | solution.py:308
  6.1 0.0 collective-permute-start
  6.1 1.3 %prepare_rows.1 = (f32[128,128]{1,0:T(8,128)S(1)}, bf16[256,128]{1,0:T(8,128)(2,1)S(1)}, bf16[128,256]{1,0:T(8,128)(2,1)S(1)}, s32[2,128]{1,0:T(2,128)S(1)}, bf16[16,2,128,128]{3,2,1,0:T(8,128)(2,1)S(1)}) custom-call(f32[7,128,128]{2,1,0:T(8,128)S(1)} %get-tuple-element.25.vloc_ref.refs_4_, f32[128,128]{1,0:T(8,128)S(1)} %get-tuple-element.26.g_ref.refs_7_, ...), custom_call_target="tpu_custom_call" | custom-call | tf_op jit(solution)/shard_map/prepare_rows/pallas_call | solution.py:358
  7.5 0.0 collective-permute-done.2.refs_3_
  7.5 1.7 %collective-permute-done.1.refs_2_ = bf16[48,128]{1,0:T(8,128)(2,1)S(1)} collective-permute-done((bf16[48,128]{1,0:T(8,128)(2,1)S(1)}, bf16[48,128]{1,0:T(8,128)(2,1)S(1)}, u32[]{:S(2)}, u32[]{:S(2)}) %collective-permute-start.1) | collective-permute-done | bytes 12320 | tf_op jit(solution)/shard_map/ppermute | solution.py:308
  9.1 0.0 collective-permute-done.refs_1_
  9.1 1.5 %couple_sections.1 = (f32[128,128]{1,0:T(8,128)}, bf16[32,1024]{1,0:T(8,128)(2,1)S(1)}, bf16[32,1024]{1,0:T(8,128)(2,1)S(1)}, bf16[32,1024]{1,0:T(8,128)(2,1)S(1...) custom-call(bf16[48,128]{1,0:T(8,128)(2,1)S(1)} %get-tuple-element.2, ...), custom_call_target="tpu_custom_call" | custom-call | tf_op jit(solution)/shard_map/couple_sections/pallas_call | solution.py:390
  10.6 3.7 %collective-permute-start.3 = (bf16[32,1024]{1,0:T(8,128)(2,1)S(1)}, bf16[32,1024]{1,0:T(8,128)(2,1)S(1)}, u32[]{:S(2)}, u32[]{:S(2)}) collective-permute-start(bf16[32,1024]{1,0:T(8,128)(2,1)S(1)} %get-tuple-element.37), channel_id=1, source_target_pairs={{0,24},{4,28},{8,16},{12,20},{16,8},{20,12},{24,0},{28,4},{1,25},{... | collective-permute-start | bytes 196616 | tf_op jit(solution)/shard_map/ppermute | solution.py:308
  14.3 1.5 %collective-permute-start.4 = (bf16[32,1024]{1,0:T(8,128)(2,1)S(1)}, bf16[32,1024]{1,0:T(8,128)(2,1)S(1)}, u32[]{:S(2)}, u32[]{:S(2)}) collective-permute-start(bf16[32,1024]{1,0:T(8,128)(2,1)S(1)} %get-tuple-element.38), channel_id=1, source_target_pairs={{0,4},{4,0},{8,12},{12,8},{16,20},{20,16},{24,28},{28,24},{1,5},{5... | collective-permute-start | bytes 196616 | tf_op jit(solution)/shard_map/ppermute | solution.py:308
  15.8 0.2 collective-permute-start.5
  16.0 0.0 collective-permute-start.6
  16.0 5.1 %collective-permute-start.7 = (bf16[32,1024]{1,0:T(8,128)(2,1)S(1)}, bf16[32,1024]{1,0:T(8,128)(2,1)S(1)}, u32[]{:S(2)}, u32[]{:S(2)}) collective-permute-start(bf16[32,1024]{1,0:T(8,128)(2,1)S(1)} %get-tuple-element.41), channel_id=1, source_target_pairs={{0,20},{4,16},{8,28},{12,24},{16,4},{20,0},{24,12},{28,8},{1,21},{... | collective-permute-start | bytes 196616 | tf_op jit(solution)/shard_map/ppermute | solution.py:308
  21.1 0.0 collective-permute-done.3.refs_1_
  21.1 0.0 collective-permute-start.8
  21.1 0.0 collective-permute-done.4.refs_2_
  21.1 1.5 %collective-permute-start.9 = (bf16[32,1024]{1,0:T(8,128)(2,1)S(1)}, bf16[32,1024]{1,0:T(8,128)(2,1)S(1)}, u32[]{:S(2)}, u32[]{:S(2)}) collective-permute-start(bf16[32,1024]{1,0:T(8,128)(2,1)S(1)} %get-tuple-element.43), channel_id=1, source_target_pairs={{0,16},{4,20},{8,24},{12,28},{16,0},{20,4},{24,8},{28,12},{1,17},{... | collective-permute-start | bytes 196616 | tf_op jit(solution)/shard_map/ppermute | solution.py:308
  22.7 2.2 %fetch_tiles.1.refs_10_ = bf16[64,2,128,128]{3,2,1,0:T(8,128)(2,1)S(1)} custom-call(bf16[32,1024]{1,0:T(8,128)(2,1)S(1)} %get-tuple-element.36.after_ref.refs_0_, bf16[128,2,128,128]{3,2,1,0:T(8,128)(2,1)} %bitcast.7), custom_call_target="tpu_custom_call" | custom-call | tf_op jit(solution)/shard_map/fetch_tiles/pallas_call | solution.py:424
  24.9 0.0 collective-permute-done.5.refs_3_
  24.9 0.0 collective-permute-done.6.refs_4_
  24.9 0.0 collective-permute-done.7.refs_5_
  24.9 1.4 %collective-permute-done.8.refs_6_ = bf16[32,1024]{1,0:T(8,128)(2,1)S(1)} collective-permute-done((bf16[32,1024]{1,0:T(8,128)(2,1)S(1)}, bf16[32,1024]{1,0:T(8,128)(2,1)S(1)}, u32[]{:S(2)}, u32[]{:S(2)}) %collective-permute-start.8) | collective-permute-done | bytes 65568 | tf_op jit(solution)/shard_map/ppermute | solution.py:308
  26.3 0.1 collective-permute-done.9.refs_7_
  26.4 2.3 %readout.1 = f32[32,8,128]{2,1,0:T(8,128)S(1)} custom-call(s32[2,128]{1,0:T(2,128)S(1)} %get-tuple-element.34.pattern_ref, bf16[128,256]{1,0:T(8,128)(2,1)S(1)} %get-tuple-element.35.order_ref, bf16[32,1024]{1,0:T(8,128)(2,1)S(1)} %get-tuple-element.36.after_ref.refs_0_, bf16[32,1024]{1,0:T(8,128)(2,1)S(1)} %collective-permute-done.3.refs_1_, ...), custom_call_target="tpu_custom_call" | custom-call | tf_op jit(solution)/shard_map/readout/pallas_call | solution.py:437
  28.6 11.5 %all_to_all.5 = f32[32,8,128]{2,1,0:T(8,128)S(1)} all-to-all(f32[32,8,128]{2,1,0:T(8,128)S(1)} %readout.1), channel_id=1, replica_groups=mesh['tile'=8,'sec'=4] {'tile','sec'}, dimensions={0} | all-to-all | bytes 262144 | tf_op jit(solution)/shard_map/all_to_all | solution.py:456
  40.1 0.6 %reduce_sum.9 = f32[8,128]{1,0:T(8,128)} reduce(f32[32,8,128]{2,1,0:T(8,128)S(1)} %all_to_all.5, f32[]{:T(128)} %constant.0.clone.1), dimensions={0}, to_apply=%region_0.0 | reduce | flops 31744 | bytes 135172 | tf_op jit(solution)/shard_map/reduce_sum | solution.py:457
Async XLA Ops:
  3.0 4.5 %collective-permute-start.2 = (bf16[48,128]{1,0:T(8,128)(2,1)S(1)}, bf16[48,128]{1,0:T(8,128)(2,1)S(1)}, u32[]{:S(2)}, u32[]{:S(2)}) collective-permute-start(bf16[48,128]{1,0:T(8,128)(2,1)S(1)} %get-tuple-element.24.refs_0_), channel_id=1, source_target_pairs={{0,3},{1,2},{2,1},{3,0},{4,7},{5,6},{6,5},{7,4},{8,11},{9,10},{10,... | collective-permute-start | bytes 36872 | tf_op jit(solution)/shard_map/ppermute | solution.py:308
  5.4 3.7 %collective-permute-start.1 = (bf16[48,128]{1,0:T(8,128)(2,1)S(1)}, bf16[48,128]{1,0:T(8,128)(2,1)S(1)}, u32[]{:S(2)}, u32[]{:S(2)}) collective-permute-start(bf16[48,128]{1,0:T(8,128)(2,1)S(1)} %get-tuple-element.24.refs_0_), channel_id=1, source_target_pairs={{0,2},{1,3},{2,0},{3,1},{4,6},{5,7},{6,4},{7,5},{8,10},{9,11},{10,... | collective-permute-start | bytes 36872 | tf_op jit(solution)/shard_map/ppermute | solution.py:308
  6.1 3.1 %collective-permute-start = (bf16[48,128]{1,0:T(8,128)(2,1)S(1)}, bf16[48,128]{1,0:T(8,128)(2,1)S(1)}, u32[]{:S(2)}, u32[]{:S(2)}) collective-permute-start(bf16[48,128]{1,0:T(8,128)(2,1)S(1)} %get-tuple-element.24.refs_0_), channel_id=1, source_target_pairs={{0,1},{1,0},{2,3},{3,2},{4,5},{5,4},{6,7},{7,6},{8,9},{9,8},{10,11... | collective-permute-start | bytes 36872 | tf_op jit(solution)/shard_map/ppermute | solution.py:308
  10.6 10.5 %collective-permute-start.3 = (bf16[32,1024]{1,0:T(8,128)(2,1)S(1)}, bf16[32,1024]{1,0:T(8,128)(2,1)S(1)}, u32[]{:S(2)}, u32[]{:S(2)}) collective-permute-start(bf16[32,1024]{1,0:T(8,128)(2,1)S(1)} %get-tuple-element.37), channel_id=1, source_target_pairs={{0,24},{4,28},{8,16},{12,20},{16,8},{20,12},{24,0},{28,4},{1,25},{... | collective-permute-start | bytes 196616 | tf_op jit(solution)/shard_map/ppermute | solution.py:308
  14.3 6.8 %collective-permute-start.4 = (bf16[32,1024]{1,0:T(8,128)(2,1)S(1)}, bf16[32,1024]{1,0:T(8,128)(2,1)S(1)}, u32[]{:S(2)}, u32[]{:S(2)}) collective-permute-start(bf16[32,1024]{1,0:T(8,128)(2,1)S(1)} %get-tuple-element.38), channel_id=1, source_target_pairs={{0,4},{4,0},{8,12},{12,8},{16,20},{20,16},{24,28},{28,24},{1,5},{5... | collective-permute-start | bytes 196616 | tf_op jit(solution)/shard_map/ppermute | solution.py:308
  15.8 9.0 %collective-permute-start.5 = (bf16[32,1024]{1,0:T(8,128)(2,1)S(1)}, bf16[32,1024]{1,0:T(8,128)(2,1)S(1)}, u32[]{:S(2)}, u32[]{:S(2)}) collective-permute-start(bf16[32,1024]{1,0:T(8,128)(2,1)S(1)} %get-tuple-element.39), channel_id=1, source_target_pairs={{0,28},{4,24},{8,20},{12,16},{16,12},{20,8},{24,4},{28,0},{1,29},{... | collective-permute-start | bytes 196616 | tf_op jit(solution)/shard_map/ppermute | solution.py:308
  16.0 8.9 %collective-permute-start.6 = (bf16[32,1024]{1,0:T(8,128)(2,1)S(1)}, bf16[32,1024]{1,0:T(8,128)(2,1)S(1)}, u32[]{:S(2)}, u32[]{:S(2)}) collective-permute-start(bf16[32,1024]{1,0:T(8,128)(2,1)S(1)} %get-tuple-element.40), channel_id=1, source_target_pairs={{0,8},{4,12},{8,0},{12,4},{16,24},{20,28},{24,16},{28,20},{1,9},{5... | collective-permute-start | bytes 196616 | tf_op jit(solution)/shard_map/ppermute | solution.py:308
  16.0 8.9 %collective-permute-start.7 = (bf16[32,1024]{1,0:T(8,128)(2,1)S(1)}, bf16[32,1024]{1,0:T(8,128)(2,1)S(1)}, u32[]{:S(2)}, u32[]{:S(2)}) collective-permute-start(bf16[32,1024]{1,0:T(8,128)(2,1)S(1)} %get-tuple-element.41), channel_id=1, source_target_pairs={{0,20},{4,16},{8,28},{12,24},{16,4},{20,0},{24,12},{28,8},{1,21},{... | collective-permute-start | bytes 196616 | tf_op jit(solution)/shard_map/ppermute | solution.py:308
  21.1 5.2 %collective-permute-start.8 = (bf16[32,1024]{1,0:T(8,128)(2,1)S(1)}, bf16[32,1024]{1,0:T(8,128)(2,1)S(1)}, u32[]{:S(2)}, u32[]{:S(2)}) collective-permute-start(bf16[32,1024]{1,0:T(8,128)(2,1)S(1)} %get-tuple-element.42), channel_id=1, source_target_pairs={{0,12},{4,8},{8,4},{12,0},{16,28},{20,24},{24,20},{28,16},{1,13},{... | collective-permute-start | bytes 196616 | tf_op jit(solution)/shard_map/ppermute | solution.py:308
  21.1 5.2 %collective-permute-start.9 = (bf16[32,1024]{1,0:T(8,128)(2,1)S(1)}, bf16[32,1024]{1,0:T(8,128)(2,1)S(1)}, u32[]{:S(2)}, u32[]{:S(2)}) collective-permute-start(bf16[32,1024]{1,0:T(8,128)(2,1)S(1)} %get-tuple-element.43), channel_id=1, source_target_pairs={{0,16},{4,20},{8,24},{12,28},{16,0},{20,4},{24,8},{28,12},{1,17},{... | collective-permute-start | bytes 196616 | tf_op jit(solution)/shard_map/ppermute | solution.py:308

commit v5 on v4

--- a/solution.py
+++ b/solution.py
@@ -139,10 +139,11 @@
     vlast_ref,
     spread_ref,
     order_ref,
-    pattern_ref,
+    select_ref,
     middle_ref,
     owner_ref,
     counts_ref,
+    pattern_ref,
     sems,
 ):
     copies = start_all(
@@ -187,8 +188,14 @@
         place = row - b * capacity
         slot_of = jnp.where((place >= 0) & (place < count), place + start, slot_of)
     order_ref[...] = one_hot(iota(order_ref.shape, 0) == slot_of)
-    for copy in copies[2:]:
-        copy.wait()
+    copies[2].wait()
+    contact_tiles = select_ref.shape[0]
+    kinds, slot_count = pattern_ref.shape
+    for t in range(kinds):
+        select_ref[:, t * slot_count : (t + 1) * slot_count] = one_hot(
+            iota((contact_tiles, slot_count), 0) == pattern_ref[t : t + 1, :]
+        )
+    copies[3].wait()
 
 
 def couple_kernel(sections, block_count, *refs):
@@ -254,11 +261,13 @@
     give.start()
 
     capacity = out_refs[0].shape[0]
-    for k in range(steps):
-        current = (leak[k] - drive_ref[k].astype(F32)).astype(BF)
-        placed = jnp.dot(spread_ref[...], current, preferred_element_type=F32).astype(BF)
+    for k in range(0, steps, 2):
+        current = [(leak[i] - drive_ref[i].astype(F32)).astype(BF) for i in (k, k + 1)]
+        placed = jnp.dot(
+            spread_ref[...], jnp.concatenate(current, axis=1), preferred_element_type=F32
+        ).astype(BF)
         for b in range(block_count):
-            out_refs[b][:, k * width : (k + 1) * width] = placed[b * capacity : (b + 1) * capacity]
+            out_refs[b][:, k * width : (k + 2) * width] = placed[b * capacity : (b + 1) * capacity]
     give.wait()
 
 
@@ -271,30 +280,31 @@
     copy.wait()
 
 
-def readout_kernel(steps, sequence, pattern_ref, order_ref, *refs):
-    *block_refs, early_ref, middle_ref, late_ref, out_ref, slots, sums = refs
+def readout_kernel(steps, sequence, select_ref, order_ref, *refs):
+    *block_refs, early_ref, middle_ref, late_ref, out_ref, slots, reach = refs
     held = [(ref, at) for ref in (early_ref, middle_ref, late_ref) for at in range(ref.shape[0])]
     block_refs = [block_refs[sequence.index(p)] for p in range(len(block_refs))]
     slot_count = order_ref.shape[0]
     kinds, width, contacts = early_ref.shape[1:]
+    for k in range(0, steps, 2):
+        span = slice(k * width, (k + 2) * width)
+        rows = jnp.concatenate([ref[:, span] for ref in block_refs], axis=0)
+        both = jnp.dot(order_ref[...], rows, preferred_element_type=F32)
+        for i in range(2):
+            slots[pl.ds(k + i, slot_count, stride=steps), :] = both[:, i * width : (i + 1) * width]
+    for s, (ref, at) in enumerate(held):
+        current = slots[s * steps : (s + 1) * steps, :].astype(BF)
+        tile = jnp.concatenate([ref[at, t] for t in range(kinds)], axis=1)
+        product = jnp.dot(current, tile, preferred_element_type=F32)
+        for t in range(kinds):
+            row = (t * slot_count + s) * steps
+            reach[row : row + steps, :] = product[:, t * contacts : (t + 1) * contacts]
     for k in range(steps):
-        span = slice(k * width, (k + 1) * width)
-        rows = jnp.concatenate([ref[:, span] for ref in block_refs], axis=0)
-        slots[pl.ds(k, slot_count, stride=steps), :] = jnp.dot(
-            order_ref[...], rows, preferred_element_type=F32
+        hi, lo = split_hi_lo(reach[pl.ds(k, kinds * slot_count, stride=steps), :])
+        both = jnp.dot(
+            select_ref[...], jnp.concatenate([hi, lo], axis=1), preferred_element_type=F32
         )
-    sums[...] = jnp.zeros_like(sums)
-    ways = sums.shape[0]
-    turn = 0
-    for s in range(slot_count):
-        current = slots[s * steps : (s + 1) * steps, :].astype(BF)
-        ref, at = held[s]
-        tile = jnp.concatenate([ref[at, t] for t in range(kinds)], axis=1)
-        reach = jnp.dot(current, tile, preferred_element_type=F32)
-        for t in range(kinds):
-            sums[turn % ways, pattern_ref[t, s]] += reach[:, t * contacts : (t + 1) * contacts]
-            turn += 1
-    out_ref[...] = sum(sums[w] for w in range(ways))
+        out_ref[:, k, :] = both[:, :contacts] + both[:, contacts:]
 
 
 def in_hbm(x):
@@ -320,9 +330,9 @@
     row_count = tiles * capacity
     weights = transfer[0]
     slot_count, kinds, _, contact_width = weights.shape
+    contact_tiles = CONTACTS // contact_width
     paired = PAIRED and tiles == 8
     vmem = pl.BlockSpec(memory_space=pltpu.VMEM)
-    smem = pl.BlockSpec(memory_space=pltpu.SMEM)
     hbm = pl.BlockSpec(memory_space=pltpu.HBM)
 
     vloc, resp, ends, cond, rev, driven, turned, early_tiles = pl.pallas_call(
@@ -355,13 +365,13 @@
         in_hbm(weights),
     )
 
-    vlast, spread, order, layout, middle_tiles = pl.pallas_call(
+    vlast, spread, order, select, middle_tiles = pl.pallas_call(
         functools.partial(prepare_kernel, tiles, paired),
         out_shape=(
             jax.ShapeDtypeStruct((cells, width), F32),
             jax.ShapeDtypeStruct((row_count, cells), BF),
             jax.ShapeDtypeStruct((slot_count, row_count), BF),
-            jax.ShapeDtypeStruct((kinds, slot_count), jnp.int32),
+            jax.ShapeDtypeStruct((contact_tiles, kinds * slot_count), BF),
             jax.ShapeDtypeStruct((PARTS[1],) + weights.shape[1:], BF),
         ),
         in_specs=[vmem] * 5 + [hbm] * 4,
@@ -369,6 +379,7 @@
         scratch_shapes=[
             pltpu.VMEM((1, cells), jnp.int32),
             pltpu.SMEM((1, tiles), jnp.int32),
+            pltpu.VMEM((kinds, slot_count), jnp.int32),
             pltpu.SemaphoreType.DMA((4,)),
         ],
         compiler_params=PARAMS,
@@ -433,19 +444,18 @@
 
     sequence = SEQUENCE if paired else (0,)
     arrived = [arrived[p] for p in sequence]
-    contact_tiles = CONTACTS // contact_width
     partial_sum = pl.pallas_call(
         functools.partial(readout_kernel, steps, sequence),
         out_shape=jax.ShapeDtypeStruct((contact_tiles, steps, contact_width), F32),
-        in_specs=[smem] + [vmem] * (len(arrived) + 4),
+        in_specs=[vmem] * (len(arrived) + 5),
         out_specs=vmem,
         scratch_shapes=[
             pltpu.VMEM((slot_count * steps, width), F32),
-            pltpu.VMEM((4, contact_tiles, steps, contact_width), F32),
+            pltpu.VMEM((kinds * slot_count * steps, contact_width), F32),
         ],
         compiler_params=PARAMS,
         name="readout",
-    )(layout, order, *arrived, early_tiles, middle_tiles, late_tiles)
+    )(select, order, *arrived, early_tiles, middle_tiles, late_tiles)
 
     devices = tiles * sections
     share = CONTACTS // devices

time: 40.9 us -> 40.3 us (0.985)
  Pallas kernels: 9.65 us -> 8.96 us
    pallas_call x1, Pallas kernels: 2.27 us -> 1.69 us  [on_device(): pl.pallas_call(functools.partial(readout_kernel, steps, sequence), out_sh...]
where the time goes in v5:
time: 40.3 us; the launch traced here: 40.1 us
  starting transfers between devices  15.1 us (37%)
  blocking collectives  11.5 us (29%)
  Pallas kernels  8.96 us (22%)
  waiting for transfers between devices  3.17 us (8%)
  between operations  0.71 us (2%)
  other arithmetic  0.63 us (2%)
    ppermute x10, starting transfers between devices, exchange(): lax.ppermute(blocks[p], axis, [(i, i ^ p) for i in range(count)])  15.1 us
    all_to_all x1, blocking collectives, on_device(): lax.all_to_all(partial_sum, ('tile', 'sec'), split_axis=0, concat_axis=0,...  11.5 us
    ppermute x10, waiting for transfers between devices, exchange(): lax.ppermute(blocks[p], axis, [(i, i ^ p) for i in range(count)])  3.17 us
    pallas_call x1, Pallas kernels, on_device(): pl.pallas_call(local_kernel, out_shape=(jax.ShapeDtypeStruct((steps - 1,...  2.36 us
    pallas_call x1, Pallas kernels, on_device(): pl.pallas_call(fetch_kernel, out_shape=jax.ShapeDtypeStruct((PARTS[2],) +...  2.2 us
    pallas_call x1, Pallas kernels, on_device(): pl.pallas_call(functools.partial(readout_kernel, steps, sequence), out_sh...  1.69 us
    pallas_call x1, Pallas kernels, on_device(): pl.pallas_call(functools.partial(couple_kernel, sections, block_count), o...  1.39 us
    pallas_call x1, Pallas kernels, on_device(): pl.pallas_call(functools.partial(prepare_kernel, tiles, paired), out_shap...  1.33 us
  transfers between devices with their start and end apart: 10, of which 3 were waited for; matrix products, arithmetic and copies ran while one was open for 0% of the time, Pallas kernels for 9%

profile of v5, /device:TPU:0, one launch (start us, length us, event | category | flops | bytes accessed | tf_op | source)
XLA Modules:
  0.0 40.1 jit_solution(6642061882490789537)
XLA Ops:
  0.6 2.4 %local_steps.1 = (f32[7,128,128]{2,1,0:T(8,128)S(1)}, f32[7,256,128]{2,1,0:T(8,128)S(1)}, bf16[48,128]{1,0:T(8,128)(2,1)S(1)}, f32[128,128]{1,0:T(8,128)S(1)}, f...) custom-call(f32[128,128]{1,0:T(8,128)} %v_hbm.1, ...), custom_call_target="tpu_custom_call" | custom-call | tf_op jit(solution)/shard_map/local_steps/pallas_call | solution.py:338
  3.0 2.4 %collective-permute-start.2 = (bf16[48,128]{1,0:T(8,128)(2,1)S(1)}, bf16[48,128]{1,0:T(8,128)(2,1)S(1)}, u32[]{:S(2)}, u32[]{:S(2)}) collective-permute-start(bf16[48,128]{1,0:T(8,128)(2,1)S(1)} %get-tuple-element.24.refs_0_), channel_id=1, source_target_pairs={{0,3},{1,2},{2,1},{3,0},{4,7},{5,6},{6,5},{7,4},{8,11},{9,10},{10,... | collective-permute-start | bytes 36872 | tf_op jit(solution)/shard_map/ppermute | solution.py:318
  5.4 0.6 %collective-permute-start.1 = (bf16[48,128]{1,0:T(8,128)(2,1)S(1)}, bf16[48,128]{1,0:T(8,128)(2,1)S(1)}, u32[]{:S(2)}, u32[]{:S(2)}) collective-permute-start(bf16[48,128]{1,0:T(8,128)(2,1)S(1)} %get-tuple-element.24.refs_0_), channel_id=1, source_target_pairs={{0,2},{1,3},{2,0},{3,1},{4,6},{5,7},{6,4},{7,5},{8,10},{9,11},{10,... | collective-permute-start | bytes 36872 | tf_op jit(solution)/shard_map/ppermute | solution.py:318
  6.1 0.0 collective-permute-start
  6.1 1.3 %prepare_rows.1 = (f32[128,128]{1,0:T(8,128)S(1)}, bf16[256,128]{1,0:T(8,128)(2,1)S(1)}, bf16[128,256]{1,0:T(8,128)(2,1)S(1)}, bf16[32,256]{1,0:T(8,128)(2,1)S(1)}, bf16[16,2,128,128]{3,2,1,0:T(8,128)(2,1)S(1)}) custom-call(f32[7,128,128]{2,1,0:T(8,128)S(1)} %get-tuple-element.25.vloc_ref.refs_4_, f32[128,128]{1,0:T(8,128)S(1)} %get-tuple-element.26.g_ref.refs_7_, ...), custom_call_target="tpu_custom_call" | custom-call | tf_op jit(solution)/shard_map/prepare_rows/pallas_call | solution.py:368
  7.5 0.0 collective-permute-done.2.refs_3_
  7.5 1.7 %collective-permute-done.1.refs_2_ = bf16[48,128]{1,0:T(8,128)(2,1)S(1)} collective-permute-done((bf16[48,128]{1,0:T(8,128)(2,1)S(1)}, bf16[48,128]{1,0:T(8,128)(2,1)S(1)}, u32[]{:S(2)}, u32[]{:S(2)}) %collective-permute-start.1) | collective-permute-done | bytes 12320 | tf_op jit(solution)/shard_map/ppermute | solution.py:318
  9.1 0.0 collective-permute-done.refs_1_
  9.1 1.4 %couple_sections.1 = (f32[128,128]{1,0:T(8,128)}, bf16[32,1024]{1,0:T(8,128)(2,1)S(1)}, bf16[32,1024]{1,0:T(8,128)(2,1)S(1)}, bf16[32,1024]{1,0:T(8,128)(2,1)S(1...) custom-call(bf16[48,128]{1,0:T(8,128)(2,1)S(1)} %get-tuple-element.2, ...), custom_call_target="tpu_custom_call" | custom-call | tf_op jit(solution)/shard_map/couple_sections/pallas_call | solution.py:401
  10.5 3.7 %collective-permute-start.3 = (bf16[32,1024]{1,0:T(8,128)(2,1)S(1)}, bf16[32,1024]{1,0:T(8,128)(2,1)S(1)}, u32[]{:S(2)}, u32[]{:S(2)}) collective-permute-start(bf16[32,1024]{1,0:T(8,128)(2,1)S(1)} %get-tuple-element.37), channel_id=1, source_target_pairs={{0,24},{4,28},{8,16},{12,20},{16,8},{20,12},{24,0},{28,4},{1,25},{... | collective-permute-start | bytes 196616 | tf_op jit(solution)/shard_map/ppermute | solution.py:318
  14.2 1.5 %collective-permute-start.4 = (bf16[32,1024]{1,0:T(8,128)(2,1)S(1)}, bf16[32,1024]{1,0:T(8,128)(2,1)S(1)}, u32[]{:S(2)}, u32[]{:S(2)}) collective-permute-start(bf16[32,1024]{1,0:T(8,128)(2,1)S(1)} %get-tuple-element.38), channel_id=1, source_target_pairs={{0,4},{4,0},{8,12},{12,8},{16,20},{20,16},{24,28},{28,24},{1,5},{5... | collective-permute-start | bytes 196616 | tf_op jit(solution)/shard_map/ppermute | solution.py:318
  15.7 0.2 collective-permute-start.5
  15.9 0.0 collective-permute-start.6
  15.9 5.1 %collective-permute-start.7 = (bf16[32,1024]{1,0:T(8,128)(2,1)S(1)}, bf16[32,1024]{1,0:T(8,128)(2,1)S(1)}, u32[]{:S(2)}, u32[]{:S(2)}) collective-permute-start(bf16[32,1024]{1,0:T(8,128)(2,1)S(1)} %get-tuple-element.41), channel_id=1, source_target_pairs={{0,20},{4,16},{8,28},{12,24},{16,4},{20,0},{24,12},{28,8},{1,21},{... | collective-permute-start | bytes 196616 | tf_op jit(solution)/shard_map/ppermute | solution.py:318
  21.0 0.0 collective-permute-done.3.refs_1_
  21.0 0.0 collective-permute-start.8
  21.0 0.0 collective-permute-done.4.refs_2_
  21.0 1.5 %collective-permute-start.9 = (bf16[32,1024]{1,0:T(8,128)(2,1)S(1)}, bf16[32,1024]{1,0:T(8,128)(2,1)S(1)}, u32[]{:S(2)}, u32[]{:S(2)}) collective-permute-start(bf16[32,1024]{1,0:T(8,128)(2,1)S(1)} %get-tuple-element.43), channel_id=1, source_target_pairs={{0,16},{4,20},{8,24},{12,28},{16,0},{20,4},{24,8},{28,12},{1,17},{... | collective-permute-start | bytes 196616 | tf_op jit(solution)/shard_map/ppermute | solution.py:318
  22.5 2.2 %fetch_tiles.1.refs_10_ = bf16[64,2,128,128]{3,2,1,0:T(8,128)(2,1)S(1)} custom-call(bf16[32,1024]{1,0:T(8,128)(2,1)S(1)} %get-tuple-element.36.after_ref.refs_0_, bf16[128,2,128,128]{3,2,1,0:T(8,128)(2,1)} %bitcast.7), custom_call_target="tpu_custom_call" | custom-call | tf_op jit(solution)/shard_map/fetch_tiles/pallas_call | solution.py:435
  24.7 0.0 collective-permute-done.5.refs_3_
  24.8 0.0 collective-permute-done.6.refs_4_
  24.8 0.0 collective-permute-done.7.refs_5_
  24.8 1.4 %collective-permute-done.8.refs_6_ = bf16[32,1024]{1,0:T(8,128)(2,1)S(1)} collective-permute-done((bf16[32,1024]{1,0:T(8,128)(2,1)S(1)}, bf16[32,1024]{1,0:T(8,128)(2,1)S(1)}, u32[]{:S(2)}, u32[]{:S(2)}) %collective-permute-start.8) | collective-permute-done | bytes 65568 | tf_op jit(solution)/shard_map/ppermute | solution.py:318
  26.2 0.1 collective-permute-done.9.refs_7_
  26.3 1.7 %readout.1 = f32[32,8,128]{2,1,0:T(8,128)S(1)} custom-call(bf16[32,256]{1,0:T(8,128)(2,1)S(1)} %get-tuple-element.34.select_ref, bf16[128,256]{1,0:T(8,128)(2,1)S(1)} %get-tuple-element.35.order_ref, bf16[32,1024]{1,0:T(8,128)(2,1)S(1)} %get-tuple-element.36.after_ref.refs_0_, bf16[32,1024]{1,0:T(8,128)(2,1)S(1)} %collective-permute-done.3.refs_1_, ...), custom_call_target="tpu_custom_call" | custom-call | tf_op jit(solution)/shard_map/readout/pallas_call | solution.py:447
  28.0 11.5 %all_to_all.5 = f32[32,8,128]{2,1,0:T(8,128)S(1)} all-to-all(f32[32,8,128]{2,1,0:T(8,128)S(1)} %readout.1), channel_id=1, replica_groups=mesh['tile'=8,'sec'=4] {'tile','sec'}, dimensions={0} | all-to-all | bytes 262144 | tf_op jit(solution)/shard_map/all_to_all | solution.py:466
  39.4 0.6 %reduce_sum.9 = f32[8,128]{1,0:T(8,128)} reduce(f32[32,8,128]{2,1,0:T(8,128)S(1)} %all_to_all.5, f32[]{:T(128)} %constant.0.clone.1), dimensions={0}, to_apply=%region_0.0 | reduce | flops 31744 | bytes 135172 | tf_op jit(solution)/shard_map/reduce_sum | solution.py:467
Async XLA Ops:
  3.0 4.5 %collective-permute-start.2 = (bf16[48,128]{1,0:T(8,128)(2,1)S(1)}, bf16[48,128]{1,0:T(8,128)(2,1)S(1)}, u32[]{:S(2)}, u32[]{:S(2)}) collective-permute-start(bf16[48,128]{1,0:T(8,128)(2,1)S(1)} %get-tuple-element.24.refs_0_), channel_id=1, source_target_pairs={{0,3},{1,2},{2,1},{3,0},{4,7},{5,6},{6,5},{7,4},{8,11},{9,10},{10,... | collective-permute-start | bytes 36872 | tf_op jit(solution)/shard_map/ppermute | solution.py:318
  5.4 3.7 %collective-permute-start.1 = (bf16[48,128]{1,0:T(8,128)(2,1)S(1)}, bf16[48,128]{1,0:T(8,128)(2,1)S(1)}, u32[]{:S(2)}, u32[]{:S(2)}) collective-permute-start(bf16[48,128]{1,0:T(8,128)(2,1)S(1)} %get-tuple-element.24.refs_0_), channel_id=1, source_target_pairs={{0,2},{1,3},{2,0},{3,1},{4,6},{5,7},{6,4},{7,5},{8,10},{9,11},{10,... | collective-permute-start | bytes 36872 | tf_op jit(solution)/shard_map/ppermute | solution.py:318
  6.1 3.1 %collective-permute-start = (bf16[48,128]{1,0:T(8,128)(2,1)S(1)}, bf16[48,128]{1,0:T(8,128)(2,1)S(1)}, u32[]{:S(2)}, u32[]{:S(2)}) collective-permute-start(bf16[48,128]{1,0:T(8,128)(2,1)S(1)} %get-tuple-element.24.refs_0_), channel_id=1, source_target_pairs={{0,1},{1,0},{2,3},{3,2},{4,5},{5,4},{6,7},{7,6},{8,9},{9,8},{10,11... | collective-permute-start | bytes 36872 | tf_op jit(solution)/shard_map/ppermute | solution.py:318
  10.5 10.5 %collective-permute-start.3 = (bf16[32,1024]{1,0:T(8,128)(2,1)S(1)}, bf16[32,1024]{1,0:T(8,128)(2,1)S(1)}, u32[]{:S(2)}, u32[]{:S(2)}) collective-permute-start(bf16[32,1024]{1,0:T(8,128)(2,1)S(1)} %get-tuple-element.37), channel_id=1, source_target_pairs={{0,24},{4,28},{8,16},{12,20},{16,8},{20,12},{24,0},{28,4},{1,25},{... | collective-permute-start | bytes 196616 | tf_op jit(solution)/shard_map/ppermute | solution.py:318
  14.2 6.8 %collective-permute-start.4 = (bf16[32,1024]{1,0:T(8,128)(2,1)S(1)}, bf16[32,1024]{1,0:T(8,128)(2,1)S(1)}, u32[]{:S(2)}, u32[]{:S(2)}) collective-permute-start(bf16[32,1024]{1,0:T(8,128)(2,1)S(1)} %get-tuple-element.38), channel_id=1, source_target_pairs={{0,4},{4,0},{8,12},{12,8},{16,20},{20,16},{24,28},{28,24},{1,5},{5... | collective-permute-start | bytes 196616 | tf_op jit(solution)/shard_map/ppermute | solution.py:318
  15.7 9.0 %collective-permute-start.5 = (bf16[32,1024]{1,0:T(8,128)(2,1)S(1)}, bf16[32,1024]{1,0:T(8,128)(2,1)S(1)}, u32[]{:S(2)}, u32[]{:S(2)}) collective-permute-start(bf16[32,1024]{1,0:T(8,128)(2,1)S(1)} %get-tuple-element.39), channel_id=1, source_target_pairs={{0,28},{4,24},{8,20},{12,16},{16,12},{20,8},{24,4},{28,0},{1,29},{... | collective-permute-start | bytes 196616 | tf_op jit(solution)/shard_map/ppermute | solution.py:318
  15.9 8.9 %collective-permute-start.6 = (bf16[32,1024]{1,0:T(8,128)(2,1)S(1)}, bf16[32,1024]{1,0:T(8,128)(2,1)S(1)}, u32[]{:S(2)}, u32[]{:S(2)}) collective-permute-start(bf16[32,1024]{1,0:T(8,128)(2,1)S(1)} %get-tuple-element.40), channel_id=1, source_target_pairs={{0,8},{4,12},{8,0},{12,4},{16,24},{20,28},{24,16},{28,20},{1,9},{5... | collective-permute-start | bytes 196616 | tf_op jit(solution)/shard_map/ppermute | solution.py:318
  15.9 8.9 %collective-permute-start.7 = (bf16[32,1024]{1,0:T(8,128)(2,1)S(1)}, bf16[32,1024]{1,0:T(8,128)(2,1)S(1)}, u32[]{:S(2)}, u32[]{:S(2)}) collective-permute-start(bf16[32,1024]{1,0:T(8,128)(2,1)S(1)} %get-tuple-element.41), channel_id=1, source_target_pairs={{0,20},{4,16},{8,28},{12,24},{16,4},{20,0},{24,12},{28,8},{1,21},{... | collective-permute-start | bytes 196616 | tf_op jit(solution)/shard_map/ppermute | solution.py:318
  21.0 5.2 %collective-permute-start.8 = (bf16[32,1024]{1,0:T(8,128)(2,1)S(1)}, bf16[32,1024]{1,0:T(8,128)(2,1)S(1)}, u32[]{:S(2)}, u32[]{:S(2)}) collective-permute-start(bf16[32,1024]{1,0:T(8,128)(2,1)S(1)} %get-tuple-element.42), channel_id=1, source_target_pairs={{0,12},{4,8},{8,4},{12,0},{16,28},{20,24},{24,20},{28,16},{1,13},{... | collective-permute-start | bytes 196616 | tf_op jit(solution)/shard_map/ppermute | solution.py:318
  21.0 5.2 %collective-permute-start.9 = (bf16[32,1024]{1,0:T(8,128)(2,1)S(1)}, bf16[32,1024]{1,0:T(8,128)(2,1)S(1)}, u32[]{:S(2)}, u32[]{:S(2)}) collective-permute-start(bf16[32,1024]{1,0:T(8,128)(2,1)S(1)} %get-tuple-element.43), channel_id=1, source_target_pairs={{0,16},{4,20},{8,24},{12,28},{16,0},{20,4},{24,8},{28,12},{1,17},{... | collective-permute-start | bytes 196616 | tf_op jit(solution)/shard_map/ppermute | solution.py:318

commit v6 on v5

--- a/solution.py
+++ b/solution.py
@@ -13,7 +13,8 @@
 END_ROWS = 48
 PAIRED = True
 PARTS = (48, 16, 64)
-SEQUENCE = (0, 6, 1, 7, 2, 5, 3, 4)
+SEC_SEQUENCE = (0, 3, 2, 1)
+SEQUENCE = (0, 6, 1, 7, 2, 4, 3, 5)
 BF = jnp.bfloat16
 F32 = jnp.float32
 PARAMS = pltpu.CompilerParams(vmem_limit_bytes=24 * 1024 * 1024)
@@ -80,23 +81,24 @@
 ):
     copies = start_all(
         [
+            (cable_hbm, cable_ref),
+            (v_hbm, v_ref),
             (g_hbm, g_ref),
-            (v_hbm, v_ref),
-            (cable_hbm, cable_ref),
             (e_hbm, e_ref),
             (drive_hbm, drive_ref),
             (transfer_hbm.at[pl.ds(0, PARTS[0])], early_ref),
         ],
         sems,
     )
-    for copy in copies[:5]:
-        copy.wait()
     cells, width = v_ref.shape
     steps = drive_ref.shape[0]
-    keep, source = keep_and_source(g_ref[...], e_ref[...])
+    copies[0].wait()
     cable = cable_ref[...].T
     turned_ref[...] = cable
     weights = hi_lo_weights(cable)
+    for copy in copies[1:5]:
+        copy.wait()
+    keep, source = keep_and_source(g_ref[...], e_ref[...])
     lane = iota((cells, width), 1)
 
     def with_ends(table, x, row):
@@ -201,13 +203,13 @@
 def couple_kernel(sections, block_count, *refs):
     ends_refs, refs = refs[:sections], refs[sections:]
     vloc_ref, vlast_ref, resp_ref, g_ref, e_ref, drive_ref, turned_ref, spread_ref, *refs = refs
-    final_hbm, *refs = refs
+    final_ref, *refs = refs
     out_refs, refs = refs[:block_count], refs[block_count:]
-    ends32, incoming, leak, final_ref, sem = refs
+    ends32, incoming, leak = refs
     steps, cells, width = drive_ref.shape
     mine = lax.axis_index("sec")
     for p in range(sections):
-        ends32[mine ^ p] = ends_refs[p][...].astype(F32)
+        ends32[mine ^ SEC_SEQUENCE[p]] = ends_refs[p][...].astype(F32)
 
     def rows(q):
         return ends32[:, q, :]
@@ -257,8 +259,6 @@
                 total = total + (unit[2 * j] * lefts[k - j] + unit[2 * j + 1] * rights[k - j])
             leak[k - 1, span, :] = cond * (total - rev)
         final_ref[span, :] = total
-    give = pltpu.make_async_copy(final_ref, final_hbm, sem)
-    give.start()
 
     capacity = out_refs[0].shape[0]
     for k in range(0, steps, 2):
@@ -268,16 +268,18 @@
         ).astype(BF)
         for b in range(block_count):
             out_refs[b][:, k * width : (k + 2) * width] = placed[b * capacity : (b + 1) * capacity]
-    give.wait()
-
-
-def fetch_kernel(after_ref, transfer_hbm, late_ref, sem):
-    del after_ref
-    copy = pltpu.make_async_copy(
-        transfer_hbm.at[pl.ds(PARTS[0] + PARTS[1], PARTS[2])], late_ref, sem
-    )
-    copy.start()
-    copy.wait()
+
+
+def fetch_kernel(final_ref, transfer_hbm, late_ref, final_hbm, sems):
+    copies = start_all(
+        [
+            (transfer_hbm.at[pl.ds(PARTS[0] + PARTS[1], PARTS[2])], late_ref),
+            (final_ref, final_hbm),
+        ],
+        sems,
+    )
+    for copy in copies:
+        copy.wait()
 
 
 def readout_kernel(steps, sequence, select_ref, order_ref, *refs):
@@ -398,25 +400,23 @@
 
     all_ends = exchange([ends] * sections, "sec")
     block_count = tiles if paired else 1
-    final_voltage, *outgoing = pl.pallas_call(
+    final_here, *outgoing = pl.pallas_call(
         functools.partial(couple_kernel, sections, block_count),
         out_shape=(
             jax.ShapeDtypeStruct((cells, width), F32),
         )
         + (jax.ShapeDtypeStruct((row_count // block_count, steps * width), BF),) * block_count,
         in_specs=[vmem] * (sections + 8),
-        out_specs=(hbm,) + (vmem,) * block_count,
+        out_specs=(vmem,) * (1 + block_count),
         scratch_shapes=[
             pltpu.VMEM((sections, END_ROWS, cells), F32),
             pltpu.VMEM((2 * steps, cells), F32),
             pltpu.VMEM((steps, cells, width), F32),
-            pltpu.VMEM((cells, width), F32),
-            pltpu.SemaphoreType.DMA,
         ],
         compiler_params=PARAMS,
         name="couple_sections",
     )(
-        *all_ends,
+        *[all_ends[p] for p in SEC_SEQUENCE],
         vloc,
         vlast,
         resp,
@@ -432,15 +432,18 @@
     else:
         arrived = [lax.all_to_all(outgoing[0], "tile", split_axis=0, concat_axis=0, tiled=True)]
 
-    late_tiles = pl.pallas_call(
+    late_tiles, final_voltage = pl.pallas_call(
         fetch_kernel,
-        out_shape=jax.ShapeDtypeStruct((PARTS[2],) + weights.shape[1:], BF),
+        out_shape=(
+            jax.ShapeDtypeStruct((PARTS[2],) + weights.shape[1:], BF),
+            jax.ShapeDtypeStruct((cells, width), F32),
+        ),
         in_specs=[vmem, hbm],
-        out_specs=vmem,
-        scratch_shapes=[pltpu.SemaphoreType.DMA],
+        out_specs=(vmem, hbm),
+        scratch_shapes=[pltpu.SemaphoreType.DMA((2,))],
         compiler_params=PARAMS,
         name="fetch_tiles",
-    )(outgoing[0], in_hbm(weights))
+    )(final_here, in_hbm(weights))
 
     sequence = SEQUENCE if paired else (0,)
     arrived = [arrived[p] for p in sequence]

time: 40.3 us -> 39.6 us (0.983)
  blocking collectives: 11.5 us -> 10.5 us
  waiting for transfers between devices: 3.17 us -> 4.03 us
  Pallas kernels: 8.96 us -> 8.46 us
    all_to_all x1, blocking collectives: 11.5 us -> 10.5 us  [on_device(): lax.all_to_all(partial_sum, ('tile', 'sec'), split_axis=0, concat_axis=0,...]
    ppermute x10, waiting for transfers between devices: 3.17 us -> 4.03 us  [exchange(): lax.ppermute(blocks[p], axis, [(i, i ^ p) for i in range(count)])]
    pallas_call x1, Pallas kernels: 1.39 us -> 0.95 us  [on_device(): pl.pallas_call(functools.partial(couple_kernel, sections, block_count), o...]
where the time goes in v6:
time: 39.6 us; the launch traced here: 39.4 us
  starting transfers between devices  15.1 us (38%)
  blocking collectives  10.5 us (27%)
  Pallas kernels  8.46 us (21%)
  waiting for transfers between devices  4.03 us (10%)
  between operations  0.71 us (2%)
  other arithmetic  0.63 us (2%)
    ppermute x10, starting transfers between devices, exchange(): lax.ppermute(blocks[p], axis, [(i, i ^ p) for i in range(count)])  15.1 us
    all_to_all x1, blocking collectives, on_device(): lax.all_to_all(partial_sum, ('tile', 'sec'), split_axis=0, concat_axis=0,...  10.5 us
    ppermute x10, waiting for transfers between devices, exchange(): lax.ppermute(blocks[p], axis, [(i, i ^ p) for i in range(count)])  4.03 us
    pallas_call x1, Pallas kernels, on_device(): pl.pallas_call(local_kernel, out_shape=(jax.ShapeDtypeStruct((steps - 1,...  2.26 us
    pallas_call x1, Pallas kernels, on_device(): pl.pallas_call(fetch_kernel, out_shape=(jax.ShapeDtypeStruct((PARTS[2],)...  2.23 us
    pallas_call x1, Pallas kernels, on_device(): pl.pallas_call(functools.partial(readout_kernel, steps, sequence), out_sh...  1.69 us
    pallas_call x1, Pallas kernels, on_device(): pl.pallas_call(functools.partial(prepare_kernel, tiles, paired), out_shap...  1.33 us
    pallas_call x1, Pallas kernels, on_device(): pl.pallas_call(functools.partial(couple_kernel, sections, block_count), o...  0.95 us
  transfers between devices with their start and end apart: 10, of which 3 were waited for; matrix products, arithmetic and copies ran while one was open for 0% of the time, Pallas kernels for 9%

profile of v6, /device:TPU:0, one launch (start us, length us, event | category | flops | bytes accessed | tf_op | source)
XLA Modules:
  0.0 39.4 jit_solution(1555581905524856349)
XLA Ops:
  0.6 2.3 %local_steps.1 = (f32[7,128,128]{2,1,0:T(8,128)S(1)}, f32[7,256,128]{2,1,0:T(8,128)S(1)}, bf16[48,128]{1,0:T(8,128)(2,1)S(1)}, f32[128,128]{1,0:T(8,128)S(1)}, f...) custom-call(f32[128,128]{1,0:T(8,128)} %v_hbm.1, ...), custom_call_target="tpu_custom_call" | custom-call | tf_op jit(solution)/shard_map/local_steps/pallas_call | solution.py:340
  2.9 2.4 %collective-permute-start = (bf16[48,128]{1,0:T(8,128)(2,1)S(1)}, bf16[48,128]{1,0:T(8,128)(2,1)S(1)}, u32[]{:S(2)}, u32[]{:S(2)}) collective-permute-start(bf16[48,128]{1,0:T(8,128)(2,1)S(1)} %get-tuple-element.26.refs_0_), channel_id=1, source_target_pairs={{0,3},{1,2},{2,1},{3,0},{4,7},{5,6},{6,5},{7,4},{8,11},{9,10},{10,... | collective-permute-start | bytes 36872 | tf_op jit(solution)/shard_map/ppermute | solution.py:320
  5.3 0.6 %collective-permute-start.1 = (bf16[48,128]{1,0:T(8,128)(2,1)S(1)}, bf16[48,128]{1,0:T(8,128)(2,1)S(1)}, u32[]{:S(2)}, u32[]{:S(2)}) collective-permute-start(bf16[48,128]{1,0:T(8,128)(2,1)S(1)} %get-tuple-element.26.refs_0_), channel_id=1, source_target_pairs={{0,2},{1,3},{2,0},{3,1},{4,6},{5,7},{6,4},{7,5},{8,10},{9,11},{10,... | collective-permute-start | bytes 36872 | tf_op jit(solution)/shard_map/ppermute | solution.py:320
  6.0 0.0 collective-permute-start.2
  6.0 1.3 %prepare_rows.1 = (f32[128,128]{1,0:T(8,128)S(1)}, bf16[256,128]{1,0:T(8,128)(2,1)S(1)}, bf16[128,256]{1,0:T(8,128)(2,1)S(1)}, bf16[32,256]{1,0:T(8,128)(2,1)S(1)}, bf16[16,2,128,128]{3,2,1,0:T(8,128)(2,1)S(1)}) custom-call(f32[7,128,128]{2,1,0:T(8,128)S(1)} %get-tuple-element.27.vloc_ref.refs_4_, f32[128,128]{1,0:T(8,128)S(1)} %get-tuple-element.28.g_ref.refs_7_, ...), custom_call_target="tpu_custom_call" | custom-call | tf_op jit(solution)/shard_map/prepare_rows/pallas_call | solution.py:370
  7.4 0.0 collective-permute-done.refs_1_
  7.4 1.7 %collective-permute-done.1.refs_2_ = bf16[48,128]{1,0:T(8,128)(2,1)S(1)} collective-permute-done((bf16[48,128]{1,0:T(8,128)(2,1)S(1)}, bf16[48,128]{1,0:T(8,128)(2,1)S(1)}, u32[]{:S(2)}, u32[]{:S(2)}) %collective-permute-start.1) | collective-permute-done | bytes 12320 | tf_op jit(solution)/shard_map/ppermute | solution.py:320
  9.0 0.0 collective-permute-done.2.refs_3_
  9.0 0.9 %couple_sections.1 = (f32[128,128]{1,0:T(8,128)S(1)}, bf16[32,1024]{1,0:T(8,128)(2,1)S(1)}, bf16[32,1024]{1,0:T(8,128)(2,1)S(1)}, bf16[32,1024]{1,0:T(8,128)(2,1...) custom-call(bf16[48,128]{1,0:T(8,128)(2,1)S(1)} %get-tuple-element.2, ...), custom_call_target="tpu_custom_call" | custom-call | tf_op jit(solution)/shard_map/couple_sections/pallas_call | solution.py:403
  10.0 3.7 %collective-permute-start.3 = (bf16[32,1024]{1,0:T(8,128)(2,1)S(1)}, bf16[32,1024]{1,0:T(8,128)(2,1)S(1)}, u32[]{:S(2)}, u32[]{:S(2)}) collective-permute-start(bf16[32,1024]{1,0:T(8,128)(2,1)S(1)} %get-tuple-element.40), channel_id=1, source_target_pairs={{0,24},{4,28},{8,16},{12,20},{16,8},{20,12},{24,0},{28,4},{1,25},{... | collective-permute-start | bytes 196616 | tf_op jit(solution)/shard_map/ppermute | solution.py:320
  13.7 1.5 %collective-permute-start.4 = (bf16[32,1024]{1,0:T(8,128)(2,1)S(1)}, bf16[32,1024]{1,0:T(8,128)(2,1)S(1)}, u32[]{:S(2)}, u32[]{:S(2)}) collective-permute-start(bf16[32,1024]{1,0:T(8,128)(2,1)S(1)} %get-tuple-element.41), channel_id=1, source_target_pairs={{0,4},{4,0},{8,12},{12,8},{16,20},{20,16},{24,28},{28,24},{1,5},{5... | collective-permute-start | bytes 196616 | tf_op jit(solution)/shard_map/ppermute | solution.py:320
  15.2 0.2 collective-permute-start.5
  15.4 0.0 collective-permute-start.6
  15.4 4.2 %collective-permute-start.7 = (bf16[32,1024]{1,0:T(8,128)(2,1)S(1)}, bf16[32,1024]{1,0:T(8,128)(2,1)S(1)}, u32[]{:S(2)}, u32[]{:S(2)}) collective-permute-start(bf16[32,1024]{1,0:T(8,128)(2,1)S(1)} %get-tuple-element.44), channel_id=1, source_target_pairs={{0,16},{4,20},{8,24},{12,28},{16,0},{20,4},{24,8},{28,12},{1,17},{... | collective-permute-start | bytes 196616 | tf_op jit(solution)/shard_map/ppermute | solution.py:320
  19.5 0.0 collective-permute-done.3.refs_1_
  19.5 1.0 %collective-permute-start.8 = (bf16[32,1024]{1,0:T(8,128)(2,1)S(1)}, bf16[32,1024]{1,0:T(8,128)(2,1)S(1)}, u32[]{:S(2)}, u32[]{:S(2)}) collective-permute-start(bf16[32,1024]{1,0:T(8,128)(2,1)S(1)} %get-tuple-element.45), channel_id=1, source_target_pairs={{0,12},{4,8},{8,4},{12,0},{16,28},{20,24},{24,20},{28,16},{1,13},{... | collective-permute-start | bytes 196616 | tf_op jit(solution)/shard_map/ppermute | solution.py:320
  20.5 0.0 collective-permute-done.4.refs_2_
  20.5 1.5 %collective-permute-start.9 = (bf16[32,1024]{1,0:T(8,128)(2,1)S(1)}, bf16[32,1024]{1,0:T(8,128)(2,1)S(1)}, u32[]{:S(2)}, u32[]{:S(2)}) collective-permute-start(bf16[32,1024]{1,0:T(8,128)(2,1)S(1)} %get-tuple-element.46), channel_id=1, source_target_pairs={{0,20},{4,16},{8,28},{12,24},{16,4},{20,0},{24,12},{28,8},{1,21},{... | collective-permute-start | bytes 196616 | tf_op jit(solution)/shard_map/ppermute | solution.py:320
  21.9 2.2 %fetch_tiles.1 = (bf16[64,2,128,128]{3,2,1,0:T(8,128)(2,1)S(1)}, f32[128,128]{1,0:T(8,128)}) custom-call(f32[128,128]{1,0:T(8,128)S(1)} %get-tuple-element.35.final_ref, bf16[128,2,128,128]{3,2,1,0:T(8,128)(2,1)} %bitcast.7), custom_call_target="tpu_custom_call" | custom-call | tf_op jit(solution)/shard_map/fetch_tiles/pallas_call | solution.py:435
  24.2 0.0 collective-permute-done.5.refs_3_
  24.2 0.0 collective-permute-done.6.refs_4_
  24.2 0.0 collective-permute-done.7.refs_5_
  24.2 0.8 %collective-permute-done.8.refs_6_ = bf16[32,1024]{1,0:T(8,128)(2,1)S(1)} collective-permute-done((bf16[32,1024]{1,0:T(8,128)(2,1)S(1)}, bf16[32,1024]{1,0:T(8,128)(2,1)S(1)}, u32[]{:S(2)}, u32[]{:S(2)}) %collective-permute-start.8) | collective-permute-done | bytes 65568 | tf_op jit(solution)/shard_map/ppermute | solution.py:320
  25.1 1.5 %collective-permute-done.9.refs_7_ = bf16[32,1024]{1,0:T(8,128)(2,1)S(1)} collective-permute-done((bf16[32,1024]{1,0:T(8,128)(2,1)S(1)}, bf16[32,1024]{1,0:T(8,128)(2,1)S(1)}, u32[]{:S(2)}, u32[]{:S(2)}) %collective-permute-start.9) | collective-permute-done | bytes 65568 | tf_op jit(solution)/shard_map/ppermute | solution.py:320
  26.6 1.7 %readout.1 = f32[32,8,128]{2,1,0:T(8,128)S(1)} custom-call(bf16[32,256]{1,0:T(8,128)(2,1)S(1)} %get-tuple-element.37.select_ref, bf16[128,256]{1,0:T(8,128)(2,1)S(1)} %get-tuple-element.38.order_ref, bf16[32,1024]{1,0:T(8,128)(2,1)S(1)} %get-tuple-element.39.refs_0_, bf16[32,1024]{1,0:T(8,128)(2,1)S(1)} %collective-permute-done.3.refs_1_, ...), custom_call_target="tpu_custom_call" | custom-call | tf_op jit(solution)/shard_map/readout/pallas_call | solution.py:450
  28.3 10.5 %all_to_all.5 = f32[32,8,128]{2,1,0:T(8,128)S(1)} all-to-all(f32[32,8,128]{2,1,0:T(8,128)S(1)} %readout.1), channel_id=1, replica_groups=mesh['tile'=8,'sec'=4] {'tile','sec'}, dimensions={0} | all-to-all | bytes 262144 | tf_op jit(solution)/shard_map/all_to_all | solution.py:469
  38.8 0.6 %reduce_sum.9 = f32[8,128]{1,0:T(8,128)} reduce(f32[32,8,128]{2,1,0:T(8,128)S(1)} %all_to_all.5, f32[]{:T(128)} %constant.0.clone.1), dimensions={0}, to_apply=%region_0.0 | reduce | flops 31744 | bytes 135172 | tf_op jit(solution)/shard_map/reduce_sum | solution.py:470
Async XLA Ops:
  2.9 4.5 %collective-permute-start = (bf16[48,128]{1,0:T(8,128)(2,1)S(1)}, bf16[48,128]{1,0:T(8,128)(2,1)S(1)}, u32[]{:S(2)}, u32[]{:S(2)}) collective-permute-start(bf16[48,128]{1,0:T(8,128)(2,1)S(1)} %get-tuple-element.26.refs_0_), channel_id=1, source_target_pairs={{0,3},{1,2},{2,1},{3,0},{4,7},{5,6},{6,5},{7,4},{8,11},{9,10},{10,... | collective-permute-start | bytes 36872 | tf_op jit(solution)/shard_map/ppermute | solution.py:320
  5.3 3.7 %collective-permute-start.1 = (bf16[48,128]{1,0:T(8,128)(2,1)S(1)}, bf16[48,128]{1,0:T(8,128)(2,1)S(1)}, u32[]{:S(2)}, u32[]{:S(2)}) collective-permute-start(bf16[48,128]{1,0:T(8,128)(2,1)S(1)} %get-tuple-element.26.refs_0_), channel_id=1, source_target_pairs={{0,2},{1,3},{2,0},{3,1},{4,6},{5,7},{6,4},{7,5},{8,10},{9,11},{10,... | collective-permute-start | bytes 36872 | tf_op jit(solution)/shard_map/ppermute | solution.py:320
  6.0 3.1 %collective-permute-start.2 = (bf16[48,128]{1,0:T(8,128)(2,1)S(1)}, bf16[48,128]{1,0:T(8,128)(2,1)S(1)}, u32[]{:S(2)}, u32[]{:S(2)}) collective-permute-start(bf16[48,128]{1,0:T(8,128)(2,1)S(1)} %get-tuple-element.26.refs_0_), channel_id=1, source_target_pairs={{0,1},{1,0},{2,3},{3,2},{4,5},{5,4},{6,7},{7,6},{8,9},{9,8},{10,11... | collective-permute-start | bytes 36872 | tf_op jit(solution)/shard_map/ppermute | solution.py:320
  10.0 9.5 %collective-permute-start.3 = (bf16[32,1024]{1,0:T(8,128)(2,1)S(1)}, bf16[32,1024]{1,0:T(8,128)(2,1)S(1)}, u32[]{:S(2)}, u32[]{:S(2)}) collective-permute-start(bf16[32,1024]{1,0:T(8,128)(2,1)S(1)} %get-tuple-element.40), channel_id=1, source_target_pairs={{0,24},{4,28},{8,16},{12,20},{16,8},{20,12},{24,0},{28,4},{1,25},{... | collective-permute-start | bytes 196616 | tf_op jit(solution)/shard_map/ppermute | solution.py:320
  13.7 6.8 %collective-permute-start.4 = (bf16[32,1024]{1,0:T(8,128)(2,1)S(1)}, bf16[32,1024]{1,0:T(8,128)(2,1)S(1)}, u32[]{:S(2)}, u32[]{:S(2)}) collective-permute-start(bf16[32,1024]{1,0:T(8,128)(2,1)S(1)} %get-tuple-element.41), channel_id=1, source_target_pairs={{0,4},{4,0},{8,12},{12,8},{16,20},{20,16},{24,28},{28,24},{1,5},{5... | collective-permute-start | bytes 196616 | tf_op jit(solution)/shard_map/ppermute | solution.py:320
  15.2 9.0 %collective-permute-start.5 = (bf16[32,1024]{1,0:T(8,128)(2,1)S(1)}, bf16[32,1024]{1,0:T(8,128)(2,1)S(1)}, u32[]{:S(2)}, u32[]{:S(2)}) collective-permute-start(bf16[32,1024]{1,0:T(8,128)(2,1)S(1)} %get-tuple-element.42), channel_id=1, source_target_pairs={{0,28},{4,24},{8,20},{12,16},{16,12},{20,8},{24,4},{28,0},{1,29},{... | collective-permute-start | bytes 196616 | tf_op jit(solution)/shard_map/ppermute | solution.py:320
  15.4 8.8 %collective-permute-start.6 = (bf16[32,1024]{1,0:T(8,128)(2,1)S(1)}, bf16[32,1024]{1,0:T(8,128)(2,1)S(1)}, u32[]{:S(2)}, u32[]{:S(2)}) collective-permute-start(bf16[32,1024]{1,0:T(8,128)(2,1)S(1)} %get-tuple-element.43), channel_id=1, source_target_pairs={{0,8},{4,12},{8,0},{12,4},{16,24},{20,28},{24,16},{28,20},{1,9},{5... | collective-permute-start | bytes 196616 | tf_op jit(solution)/shard_map/ppermute | solution.py:320
  15.4 8.8 %collective-permute-start.7 = (bf16[32,1024]{1,0:T(8,128)(2,1)S(1)}, bf16[32,1024]{1,0:T(8,128)(2,1)S(1)}, u32[]{:S(2)}, u32[]{:S(2)}) collective-permute-start(bf16[32,1024]{1,0:T(8,128)(2,1)S(1)} %get-tuple-element.44), channel_id=1, source_target_pairs={{0,16},{4,20},{8,24},{12,28},{16,0},{20,4},{24,8},{28,12},{1,17},{... | collective-permute-start | bytes 196616 | tf_op jit(solution)/shard_map/ppermute | solution.py:320
  19.5 5.5 %collective-permute-start.8 = (bf16[32,1024]{1,0:T(8,128)(2,1)S(1)}, bf16[32,1024]{1,0:T(8,128)(2,1)S(1)}, u32[]{:S(2)}, u32[]{:S(2)}) collective-permute-start(bf16[32,1024]{1,0:T(8,128)(2,1)S(1)} %get-tuple-element.45), channel_id=1, source_target_pairs={{0,12},{4,8},{8,4},{12,0},{16,28},{20,24},{24,20},{28,16},{1,13},{... | collective-permute-start | bytes 196616 | tf_op jit(solution)/shard_map/ppermute | solution.py:320
  20.5 6.1 %collective-permute-start.9 = (bf16[32,1024]{1,0:T(8,128)(2,1)S(1)}, bf16[32,1024]{1,0:T(8,128)(2,1)S(1)}, u32[]{:S(2)}, u32[]{:S(2)}) collective-permute-start(bf16[32,1024]{1,0:T(8,128)(2,1)S(1)} %get-tuple-element.46), channel_id=1, source_target_pairs={{0,20},{4,16},{8,28},{12,24},{16,4},{20,0},{24,12},{28,8},{1,21},{... | collective-permute-start | bytes 196616 | tf_op jit(solution)/shard_map/ppermute | solution.py:320

commit v7 on v6

--- a/solution.py
+++ b/solution.py
@@ -13,7 +13,7 @@
 END_ROWS = 48
 PAIRED = True
 PARTS = (48, 16, 64)
-SEC_SEQUENCE = (0, 3, 2, 1)
+SEC_SEQUENCE = (0, 1, 2, 3)
 SEQUENCE = (0, 6, 1, 7, 2, 4, 3, 5)
 BF = jnp.bfloat16
 F32 = jnp.float32
@@ -283,7 +283,7 @@
 
 
 def readout_kernel(steps, sequence, select_ref, order_ref, *refs):
-    *block_refs, early_ref, middle_ref, late_ref, out_ref, slots, reach = refs
+    *block_refs, early_ref, middle_ref, late_ref, out_ref, slots, reach, sums = refs
     held = [(ref, at) for ref in (early_ref, middle_ref, late_ref) for at in range(ref.shape[0])]
     block_refs = [block_refs[sequence.index(p)] for p in range(len(block_refs))]
     slot_count = order_ref.shape[0]
@@ -306,7 +306,8 @@
         both = jnp.dot(
             select_ref[...], jnp.concatenate([hi, lo], axis=1), preferred_element_type=F32
         )
-        out_ref[:, k, :] = both[:, :contacts] + both[:, contacts:]
+        sums[:, k, :] = both[:, :contacts] + both[:, contacts:]
+    out_ref[...] = sums[...].astype(BF)
 
 
 def in_hbm(x):
@@ -449,12 +450,13 @@
     arrived = [arrived[p] for p in sequence]
     partial_sum = pl.pallas_call(
         functools.partial(readout_kernel, steps, sequence),
-        out_shape=jax.ShapeDtypeStruct((contact_tiles, steps, contact_width), F32),
+        out_shape=jax.ShapeDtypeStruct((contact_tiles, steps, contact_width), BF),
         in_specs=[vmem] * (len(arrived) + 5),
         out_specs=vmem,
         scratch_shapes=[
             pltpu.VMEM((slot_count * steps, width), F32),
             pltpu.VMEM((kinds * slot_count * steps, contact_width), F32),
+            pltpu.VMEM((contact_tiles, steps, contact_width), F32),
         ],
         compiler_params=PARAMS,
         name="readout",
@@ -467,7 +469,7 @@
         partial_sum = partial_sum.reshape(contact_tiles, steps, parts, share)
         partial_sum = partial_sum.transpose(0, 2, 1, 3).reshape(devices, steps, share)
     shares = lax.all_to_all(partial_sum, ("tile", "sec"), split_axis=0, concat_axis=0, tiled=True)
-    return final_voltage, jnp.sum(shares, axis=0)
+    return final_voltage, jnp.sum(shares.astype(F32), axis=0)
 
 
 def solution(mesh):

time: 39.6 us -> 38.8 us (0.980)
  blocking collectives: 10.5 us -> 9.69 us
    all_to_all x1, blocking collectives: 10.5 us -> 9.69 us  [on_device(): lax.all_to_all(partial_sum, ('tile', 'sec'), split_axis=0, concat_axis=0,...]
where the time goes in v7:
time: 38.8 us; the launch traced here: 38.6 us
  starting transfers between devices  15.1 us (39%)
  blocking collectives  9.69 us (25%)
  Pallas kernels  8.48 us (22%)
  waiting for transfers between devices  4.02 us (10%)
  between operations  0.71 us (2%)
  other arithmetic  0.63 us (2%)
    ppermute x10, starting transfers between devices, exchange(): lax.ppermute(blocks[p], axis, [(i, i ^ p) for i in range(count)])  15.1 us
    all_to_all x1, blocking collectives, on_device(): lax.all_to_all(partial_sum, ('tile', 'sec'), split_axis=0, concat_axis=0,...  9.69 us
    ppermute x10, waiting for transfers between devices, exchange(): lax.ppermute(blocks[p], axis, [(i, i ^ p) for i in range(count)])  4.02 us
    pallas_call x1, Pallas kernels, on_device(): pl.pallas_call(local_kernel, out_shape=(jax.ShapeDtypeStruct((steps - 1,...  2.26 us
    pallas_call x1, Pallas kernels, on_device(): pl.pallas_call(fetch_kernel, out_shape=(jax.ShapeDtypeStruct((PARTS[2],)...  2.23 us
    pallas_call x1, Pallas kernels, on_device(): pl.pallas_call(functools.partial(readout_kernel, steps, sequence), out_sh...  1.71 us
    pallas_call x1, Pallas kernels, on_device(): pl.pallas_call(functools.partial(prepare_kernel, tiles, paired), out_shap...  1.33 us
    pallas_call x1, Pallas kernels, on_device(): pl.pallas_call(functools.partial(couple_kernel, sections, block_count), o...  0.95 us
  transfers between devices with their start and end apart: 10, of which 3 were waited for; matrix products, arithmetic and copies ran while one was open for 0% of the time, Pallas kernels for 9%

profile of v7, /device:TPU:0, one launch (start us, length us, event | category | flops | bytes accessed | tf_op | source)
XLA Modules:
  0.0 38.6 jit_solution(5546460112973667502)
XLA Ops:
  0.6 2.3 %local_steps.1 = (f32[7,128,128]{2,1,0:T(8,128)S(1)}, f32[7,256,128]{2,1,0:T(8,128)S(1)}, bf16[48,128]{1,0:T(8,128)(2,1)S(1)}, f32[128,128]{1,0:T(8,128)S(1)}, f...) custom-call(f32[128,128]{1,0:T(8,128)} %v_hbm.1, ...), custom_call_target="tpu_custom_call" | custom-call | tf_op jit(solution)/shard_map/local_steps/pallas_call | solution.py:341
  2.9 2.4 %collective-permute-start.2 = (bf16[48,128]{1,0:T(8,128)(2,1)S(1)}, bf16[48,128]{1,0:T(8,128)(2,1)S(1)}, u32[]{:S(2)}, u32[]{:S(2)}) collective-permute-start(bf16[48,128]{1,0:T(8,128)(2,1)S(1)} %get-tuple-element.26.refs_0_), channel_id=1, source_target_pairs={{0,3},{1,2},{2,1},{3,0},{4,7},{5,6},{6,5},{7,4},{8,11},{9,10},{10,... | collective-permute-start | bytes 36872 | tf_op jit(solution)/shard_map/ppermute | solution.py:321
  5.3 0.6 %collective-permute-start.1 = (bf16[48,128]{1,0:T(8,128)(2,1)S(1)}, bf16[48,128]{1,0:T(8,128)(2,1)S(1)}, u32[]{:S(2)}, u32[]{:S(2)}) collective-permute-start(bf16[48,128]{1,0:T(8,128)(2,1)S(1)} %get-tuple-element.26.refs_0_), channel_id=1, source_target_pairs={{0,2},{1,3},{2,0},{3,1},{4,6},{5,7},{6,4},{7,5},{8,10},{9,11},{10,... | collective-permute-start | bytes 36872 | tf_op jit(solution)/shard_map/ppermute | solution.py:321
  6.0 0.0 collective-permute-start
  6.0 1.3 %prepare_rows.1 = (f32[128,128]{1,0:T(8,128)S(1)}, bf16[256,128]{1,0:T(8,128)(2,1)S(1)}, bf16[128,256]{1,0:T(8,128)(2,1)S(1)}, bf16[32,256]{1,0:T(8,128)(2,1)S(1)}, bf16[16,2,128,128]{3,2,1,0:T(8,128)(2,1)S(1)}) custom-call(f32[7,128,128]{2,1,0:T(8,128)S(1)} %get-tuple-element.27.vloc_ref.refs_4_, f32[128,128]{1,0:T(8,128)S(1)} %get-tuple-element.28.g_ref.refs_7_, ...), custom_call_target="tpu_custom_call" | custom-call | tf_op jit(solution)/shard_map/prepare_rows/pallas_call | solution.py:371
  7.4 0.0 collective-permute-done.2.refs_3_
  7.4 1.7 %collective-permute-done.1.refs_2_ = bf16[48,128]{1,0:T(8,128)(2,1)S(1)} collective-permute-done((bf16[48,128]{1,0:T(8,128)(2,1)S(1)}, bf16[48,128]{1,0:T(8,128)(2,1)S(1)}, u32[]{:S(2)}, u32[]{:S(2)}) %collective-permute-start.1) | collective-permute-done | bytes 12320 | tf_op jit(solution)/shard_map/ppermute | solution.py:321
  9.0 0.0 collective-permute-done.refs_1_
  9.0 1.0 %couple_sections.1 = (f32[128,128]{1,0:T(8,128)S(1)}, bf16[32,1024]{1,0:T(8,128)(2,1)S(1)}, bf16[32,1024]{1,0:T(8,128)(2,1)S(1)}, bf16[32,1024]{1,0:T(8,128)(2,1...) custom-call(bf16[48,128]{1,0:T(8,128)(2,1)S(1)} %get-tuple-element.2, ...), custom_call_target="tpu_custom_call" | custom-call | tf_op jit(solution)/shard_map/couple_sections/pallas_call | solution.py:404
  10.0 3.7 %collective-permute-start.3 = (bf16[32,1024]{1,0:T(8,128)(2,1)S(1)}, bf16[32,1024]{1,0:T(8,128)(2,1)S(1)}, u32[]{:S(2)}, u32[]{:S(2)}) collective-permute-start(bf16[32,1024]{1,0:T(8,128)(2,1)S(1)} %get-tuple-element.40), channel_id=1, source_target_pairs={{0,24},{4,28},{8,16},{12,20},{16,8},{20,12},{24,0},{28,4},{1,25},{... | collective-permute-start | bytes 196616 | tf_op jit(solution)/shard_map/ppermute | solution.py:321
  13.7 1.5 %collective-permute-start.4 = (bf16[32,1024]{1,0:T(8,128)(2,1)S(1)}, bf16[32,1024]{1,0:T(8,128)(2,1)S(1)}, u32[]{:S(2)}, u32[]{:S(2)}) collective-permute-start(bf16[32,1024]{1,0:T(8,128)(2,1)S(1)} %get-tuple-element.41), channel_id=1, source_target_pairs={{0,4},{4,0},{8,12},{12,8},{16,20},{20,16},{24,28},{28,24},{1,5},{5... | collective-permute-start | bytes 196616 | tf_op jit(solution)/shard_map/ppermute | solution.py:321
  15.2 0.2 collective-permute-start.5
  15.4 0.0 collective-permute-start.6
  15.4 4.2 %collective-permute-start.7 = (bf16[32,1024]{1,0:T(8,128)(2,1)S(1)}, bf16[32,1024]{1,0:T(8,128)(2,1)S(1)}, u32[]{:S(2)}, u32[]{:S(2)}) collective-permute-start(bf16[32,1024]{1,0:T(8,128)(2,1)S(1)} %get-tuple-element.44), channel_id=1, source_target_pairs={{0,16},{4,20},{8,24},{12,28},{16,0},{20,4},{24,8},{28,12},{1,17},{... | collective-permute-start | bytes 196616 | tf_op jit(solution)/shard_map/ppermute | solution.py:321
  19.5 0.0 collective-permute-done.3.refs_1_
  19.5 1.0 %collective-permute-start.8 = (bf16[32,1024]{1,0:T(8,128)(2,1)S(1)}, bf16[32,1024]{1,0:T(8,128)(2,1)S(1)}, u32[]{:S(2)}, u32[]{:S(2)}) collective-permute-start(bf16[32,1024]{1,0:T(8,128)(2,1)S(1)} %get-tuple-element.45), channel_id=1, source_target_pairs={{0,12},{4,8},{8,4},{12,0},{16,28},{20,24},{24,20},{28,16},{1,13},{... | collective-permute-start | bytes 196616 | tf_op jit(solution)/shard_map/ppermute | solution.py:321
  20.5 0.0 collective-permute-done.4.refs_2_
  20.5 1.5 %collective-permute-start.9 = (bf16[32,1024]{1,0:T(8,128)(2,1)S(1)}, bf16[32,1024]{1,0:T(8,128)(2,1)S(1)}, u32[]{:S(2)}, u32[]{:S(2)}) collective-permute-start(bf16[32,1024]{1,0:T(8,128)(2,1)S(1)} %get-tuple-element.46), channel_id=1, source_target_pairs={{0,20},{4,16},{8,28},{12,24},{16,4},{20,0},{24,12},{28,8},{1,21},{... | collective-permute-start | bytes 196616 | tf_op jit(solution)/shard_map/ppermute | solution.py:321
  21.9 2.2 %fetch_tiles.1 = (bf16[64,2,128,128]{3,2,1,0:T(8,128)(2,1)S(1)}, f32[128,128]{1,0:T(8,128)}) custom-call(f32[128,128]{1,0:T(8,128)S(1)} %get-tuple-element.35.final_ref, bf16[128,2,128,128]{3,2,1,0:T(8,128)(2,1)} %bitcast.7), custom_call_target="tpu_custom_call" | custom-call | tf_op jit(solution)/shard_map/fetch_tiles/pallas_call | solution.py:436
  24.2 0.0 collective-permute-done.5.refs_3_
  24.2 0.0 collective-permute-done.6.refs_4_
  24.2 0.0 collective-permute-done.7.refs_5_
  24.2 0.8 %collective-permute-done.8.refs_6_ = bf16[32,1024]{1,0:T(8,128)(2,1)S(1)} collective-permute-done((bf16[32,1024]{1,0:T(8,128)(2,1)S(1)}, bf16[32,1024]{1,0:T(8,128)(2,1)S(1)}, u32[]{:S(2)}, u32[]{:S(2)}) %collective-permute-start.8) | collective-permute-done | bytes 65568 | tf_op jit(solution)/shard_map/ppermute | solution.py:321
  25.1 1.5 %collective-permute-done.9.refs_7_ = bf16[32,1024]{1,0:T(8,128)(2,1)S(1)} collective-permute-done((bf16[32,1024]{1,0:T(8,128)(2,1)S(1)}, bf16[32,1024]{1,0:T(8,128)(2,1)S(1)}, u32[]{:S(2)}, u32[]{:S(2)}) %collective-permute-start.9) | collective-permute-done | bytes 65568 | tf_op jit(solution)/shard_map/ppermute | solution.py:321
  26.5 1.7 %readout.1 = bf16[32,8,128]{2,1,0:T(8,128)(2,1)S(1)} custom-call(bf16[32,256]{1,0:T(8,128)(2,1)S(1)} %get-tuple-element.37.select_ref, bf16[128,256]{1,0:T(8,128)(2,1)S(1)} %get-tuple-element.38.order_ref, bf16[32,1024]{1,0:T(8,128)(2,1)S(1)} %get-tuple-element.39.refs_0_, bf16[32,1024]{1,0:T(8,128)(2,1)S(1)} %collective-permute-done.3.refs_1_, ...), custom_call_target="tpu_custom_call" | custom-call | tf_op jit(solution)/shard_map/readout/pallas_call | solution.py:451
  28.3 9.7 %all_to_all.5 = bf16[32,8,128]{2,1,0:T(8,128)(2,1)S(1)} all-to-all(bf16[32,8,128]{2,1,0:T(8,128)(2,1)S(1)} %readout.1), channel_id=1, replica_groups=mesh['tile'=8,'sec'=4] {'tile','sec'}, dimensions={0} | all-to-all | bytes 131072 | tf_op jit(solution)/shard_map/all_to_all | solution.py:471
  37.9 0.6 %convert_reduce_fusion = f32[8,128]{1,0:T(8,128)} fusion(bf16[32,8,128]{2,1,0:T(8,128)(2,1)S(1)} %all_to_all.5), kind=kLoop, calls=%fused_computation | loop fusion | flops 64512 | bytes 69632 | tf_op jit(solution)/shard_map/reduce_sum | solution.py:472
Async XLA Ops:
  2.9 4.5 %collective-permute-start.2 = (bf16[48,128]{1,0:T(8,128)(2,1)S(1)}, bf16[48,128]{1,0:T(8,128)(2,1)S(1)}, u32[]{:S(2)}, u32[]{:S(2)}) collective-permute-start(bf16[48,128]{1,0:T(8,128)(2,1)S(1)} %get-tuple-element.26.refs_0_), channel_id=1, source_target_pairs={{0,3},{1,2},{2,1},{3,0},{4,7},{5,6},{6,5},{7,4},{8,11},{9,10},{10,... | collective-permute-start | bytes 36872 | tf_op jit(solution)/shard_map/ppermute | solution.py:321
  5.3 3.7 %collective-permute-start.1 = (bf16[48,128]{1,0:T(8,128)(2,1)S(1)}, bf16[48,128]{1,0:T(8,128)(2,1)S(1)}, u32[]{:S(2)}, u32[]{:S(2)}) collective-permute-start(bf16[48,128]{1,0:T(8,128)(2,1)S(1)} %get-tuple-element.26.refs_0_), channel_id=1, source_target_pairs={{0,2},{1,3},{2,0},{3,1},{4,6},{5,7},{6,4},{7,5},{8,10},{9,11},{10,... | collective-permute-start | bytes 36872 | tf_op jit(solution)/shard_map/ppermute | solution.py:321
  6.0 3.1 %collective-permute-start = (bf16[48,128]{1,0:T(8,128)(2,1)S(1)}, bf16[48,128]{1,0:T(8,128)(2,1)S(1)}, u32[]{:S(2)}, u32[]{:S(2)}) collective-permute-start(bf16[48,128]{1,0:T(8,128)(2,1)S(1)} %get-tuple-element.26.refs_0_), channel_id=1, source_target_pairs={{0,1},{1,0},{2,3},{3,2},{4,5},{5,4},{6,7},{7,6},{8,9},{9,8},{10,11... | collective-permute-start | bytes 36872 | tf_op jit(solution)/shard_map/ppermute | solution.py:321
  10.0 9.5 %collective-permute-start.3 = (bf16[32,1024]{1,0:T(8,128)(2,1)S(1)}, bf16[32,1024]{1,0:T(8,128)(2,1)S(1)}, u32[]{:S(2)}, u32[]{:S(2)}) collective-permute-start(bf16[32,1024]{1,0:T(8,128)(2,1)S(1)} %get-tuple-element.40), channel_id=1, source_target_pairs={{0,24},{4,28},{8,16},{12,20},{16,8},{20,12},{24,0},{28,4},{1,25},{... | collective-permute-start | bytes 196616 | tf_op jit(solution)/shard_map/ppermute | solution.py:321
  13.7 6.8 %collective-permute-start.4 = (bf16[32,1024]{1,0:T(8,128)(2,1)S(1)}, bf16[32,1024]{1,0:T(8,128)(2,1)S(1)}, u32[]{:S(2)}, u32[]{:S(2)}) collective-permute-start(bf16[32,1024]{1,0:T(8,128)(2,1)S(1)} %get-tuple-element.41), channel_id=1, source_target_pairs={{0,4},{4,0},{8,12},{12,8},{16,20},{20,16},{24,28},{28,24},{1,5},{5... | collective-permute-start | bytes 196616 | tf_op jit(solution)/shard_map/ppermute | solution.py:321
  15.2 9.0 %collective-permute-start.5 = (bf16[32,1024]{1,0:T(8,128)(2,1)S(1)}, bf16[32,1024]{1,0:T(8,128)(2,1)S(1)}, u32[]{:S(2)}, u32[]{:S(2)}) collective-permute-start(bf16[32,1024]{1,0:T(8,128)(2,1)S(1)} %get-tuple-element.42), channel_id=1, source_target_pairs={{0,28},{4,24},{8,20},{12,16},{16,12},{20,8},{24,4},{28,0},{1,29},{... | collective-permute-start | bytes 196616 | tf_op jit(solution)/shard_map/ppermute | solution.py:321
  15.4 8.8 %collective-permute-start.6 = (bf16[32,1024]{1,0:T(8,128)(2,1)S(1)}, bf16[32,1024]{1,0:T(8,128)(2,1)S(1)}, u32[]{:S(2)}, u32[]{:S(2)}) collective-permute-start(bf16[32,1024]{1,0:T(8,128)(2,1)S(1)} %get-tuple-element.43), channel_id=1, source_target_pairs={{0,8},{4,12},{8,0},{12,4},{16,24},{20,28},{24,16},{28,20},{1,9},{5... | collective-permute-start | bytes 196616 | tf_op jit(solution)/shard_map/ppermute | solution.py:321
  15.4 8.8 %collective-permute-start.7 = (bf16[32,1024]{1,0:T(8,128)(2,1)S(1)}, bf16[32,1024]{1,0:T(8,128)(2,1)S(1)}, u32[]{:S(2)}, u32[]{:S(2)}) collective-permute-start(bf16[32,1024]{1,0:T(8,128)(2,1)S(1)} %get-tuple-element.44), channel_id=1, source_target_pairs={{0,16},{4,20},{8,24},{12,28},{16,0},{20,4},{24,8},{28,12},{1,17},{... | collective-permute-start | bytes 196616 | tf_op jit(solution)/shard_map/ppermute | solution.py:321
  19.5 5.5 %collective-permute-start.8 = (bf16[32,1024]{1,0:T(8,128)(2,1)S(1)}, bf16[32,1024]{1,0:T(8,128)(2,1)S(1)}, u32[]{:S(2)}, u32[]{:S(2)}) collective-permute-start(bf16[32,1024]{1,0:T(8,128)(2,1)S(1)} %get-tuple-element.45), channel_id=1, source_target_pairs={{0,12},{4,8},{8,4},{12,0},{16,28},{20,24},{24,20},{28,16},{1,13},{... | collective-permute-start | bytes 196616 | tf_op jit(solution)/shard_map/ppermute | solution.py:321
  20.5 6.1 %collective-permute-start.9 = (bf16[32,1024]{1,0:T(8,128)(2,1)S(1)}, bf16[32,1024]{1,0:T(8,128)(2,1)S(1)}, u32[]{:S(2)}, u32[]{:S(2)}) collective-permute-start(bf16[32,1024]{1,0:T(8,128)(2,1)S(1)} %get-tuple-element.46), channel_id=1, source_target_pairs={{0,20},{4,16},{8,28},{12,24},{16,4},{20,0},{24,12},{28,8},{1,21},{... | collective-permute-start | bytes 196616 | tf_op jit(solution)/shard_map/ppermute | solution.py:321

commit v8 on v7

--- a/solution.py
+++ b/solution.py
@@ -14,7 +14,7 @@
 PAIRED = True
 PARTS = (48, 16, 64)
 SEC_SEQUENCE = (0, 1, 2, 3)
-SEQUENCE = (0, 6, 1, 7, 2, 4, 3, 5)
+SEQUENCE = (0, 6, 1, 7, 5, 2, 4, 3)
 BF = jnp.bfloat16
 F32 = jnp.float32
 PARAMS = pltpu.CompilerParams(vmem_limit_bytes=24 * 1024 * 1024)
@@ -116,8 +116,8 @@
         left = solve(left * keep, weights)
         right = solve(right * keep, weights)
         vloc_ref[k] = voltage
-        resp_ref[k, :cells] = left
-        resp_ref[k, cells:] = right
+        resp_ref[k, :cells] = left.astype(BF)
+        resp_ref[k, cells:] = right.astype(BF)
         table = with_ends(table, voltage, 2 * (k + 1))
         if k < steps - 2:
             table = with_ends(table, left, left_row + 2 * (k + 1))
@@ -238,15 +238,15 @@
         )
     by_cell = incoming[...].T
 
-    block = 8
-    lag_left = jnp.broadcast_to(TIME_STEP * AXIAL * turned_ref[0:1, :], (block, width))
-    lag_right = jnp.broadcast_to(
-        TIME_STEP * AXIAL * turned_ref[width - 1 : width, :], (block, width)
-    )
+    block = 16
+    lag_left = jnp.broadcast_to(TIME_STEP * AXIAL * turned_ref[0:1, :], (block, width)).astype(BF)
+    lag_right = TIME_STEP * AXIAL * turned_ref[width - 1 : width, :]
+    lag_right = jnp.broadcast_to(lag_right, (block, width)).astype(BF)
     for c in range(0, cells, block):
         span = slice(c, c + block)
         unit = [
-            jnp.broadcast_to(by_cell[span, q : q + 1], (block, width)) for q in range(2 * steps)
+            jnp.broadcast_to(by_cell[span, q : q + 1], (block, width)).astype(BF)
+            for q in range(2 * steps)
         ]
         lefts = [None, lag_left] + [resp_ref[l, span, :] for l in range(steps - 1)]
         rights = [None, lag_right] + [
@@ -255,8 +255,10 @@
         cond, rev = g_ref[span, :], e_ref[span, :]
         for k in range(1, steps + 1):
             total = vloc_ref[k - 1, span, :] if k < steps else vlast_ref[span, :]
-            for j in range(k):
-                total = total + (unit[2 * j] * lefts[k - j] + unit[2 * j + 1] * rights[k - j])
+            inflow = [
+                unit[2 * j] * lefts[k - j] + unit[2 * j + 1] * rights[k - j] for j in range(k)
+            ]
+            total = total + sum(inflow[1:], inflow[0]).astype(F32)
             leak[k - 1, span, :] = cond * (total - rev)
         final_ref[span, :] = total
 
@@ -342,7 +344,7 @@
         local_kernel,
         out_shape=(
             jax.ShapeDtypeStruct((steps - 1, cells, width), F32),
-            jax.ShapeDtypeStruct((steps - 1, 2 * cells, width), F32),
+            jax.ShapeDtypeStruct((steps - 1, 2 * cells, width), BF),
             jax.ShapeDtypeStruct((END_ROWS, cells), BF),
             jax.ShapeDtypeStruct((cells, width), F32),
             jax.ShapeDtypeStruct((cells, width), F32),

time: 38.8 us -> 38.7 us (level)
  transfers between devices with their start and end apart: 10 -> 10, of which waited for: 3 -> 4; matrix products, arithmetic and copies ran while one was open for 0% -> 0% of each run, Pallas kernels for 9% -> 9%
where the time goes in v8:
time: 38.7 us; the launch traced here: 38.5 us
  starting transfers between devices  15.2 us (39%)
  blocking collectives  9.61 us (25%)
  Pallas kernels  8.3 us (21%)
  waiting for transfers between devices  4.08 us (11%)
  between operations  0.69 us (2%)
  other arithmetic  0.63 us (2%)
    ppermute x10, starting transfers between devices, exchange(): lax.ppermute(blocks[p], axis, [(i, i ^ p) for i in range(count)])  15.2 us
    all_to_all x1, blocking collectives, on_device(): lax.all_to_all(partial_sum, ('tile', 'sec'), split_axis=0, concat_axis=0,...  9.61 us
    ppermute x10, waiting for transfers between devices, exchange(): lax.ppermute(blocks[p], axis, [(i, i ^ p) for i in range(count)])  4.08 us
    pallas_call x1, Pallas kernels, on_device(): pl.pallas_call(local_kernel, out_shape=(jax.ShapeDtypeStruct((steps - 1,...  2.25 us
    pallas_call x1, Pallas kernels, on_device(): pl.pallas_call(fetch_kernel, out_shape=(jax.ShapeDtypeStruct((PARTS[2],)...  2.23 us
    pallas_call x1, Pallas kernels, on_device(): pl.pallas_call(functools.partial(readout_kernel, steps, sequence), out_sh...  1.71 us
    pallas_call x1, Pallas kernels, on_device(): pl.pallas_call(functools.partial(prepare_kernel, tiles, paired), out_shap...  1.32 us
    pallas_call x1, Pallas kernels, on_device(): pl.pallas_call(functools.partial(couple_kernel, sections, block_count), o...  0.79 us
  transfers between devices with their start and end apart: 10, of which 4 were waited for; matrix products, arithmetic and copies ran while one was open for 0% of the time, Pallas kernels for 9%

profile of v8, /device:TPU:0, one launch (start us, length us, event | category | flops | bytes accessed | tf_op | source)
XLA Modules:
  0.0 38.5 jit_solution(10548110535430550039)
XLA Ops:
  0.6 2.2 %local_steps.1 = (f32[7,128,128]{2,1,0:T(8,128)S(1)}, bf16[7,256,128]{2,1,0:T(8,128)(2,1)S(1)}, bf16[48,128]{1,0:T(8,128)(2,1)S(1)}, f32[128,128]{1,0:T(8,128)S(...) custom-call(f32[128,128]{1,0:T(8,128)} %v_hbm.1, ...), custom_call_target="tpu_custom_call" | custom-call | tf_op jit(solution)/shard_map/local_steps/pallas_call | solution.py:343
  2.9 2.4 %collective-permute-start.2 = (bf16[48,128]{1,0:T(8,128)(2,1)S(1)}, bf16[48,128]{1,0:T(8,128)(2,1)S(1)}, u32[]{:S(2)}, u32[]{:S(2)}) collective-permute-start(bf16[48,128]{1,0:T(8,128)(2,1)S(1)} %get-tuple-element.26.refs_0_), channel_id=1, source_target_pairs={{0,3},{1,2},{2,1},{3,0},{4,7},{5,6},{6,5},{7,4},{8,11},{9,10},{10,... | collective-permute-start | bytes 36872 | tf_op jit(solution)/shard_map/ppermute | solution.py:323
  5.3 0.6 %collective-permute-start.1 = (bf16[48,128]{1,0:T(8,128)(2,1)S(1)}, bf16[48,128]{1,0:T(8,128)(2,1)S(1)}, u32[]{:S(2)}, u32[]{:S(2)}) collective-permute-start(bf16[48,128]{1,0:T(8,128)(2,1)S(1)} %get-tuple-element.26.refs_0_), channel_id=1, source_target_pairs={{0,2},{1,3},{2,0},{3,1},{4,6},{5,7},{6,4},{7,5},{8,10},{9,11},{10,... | collective-permute-start | bytes 36872 | tf_op jit(solution)/shard_map/ppermute | solution.py:323
  6.0 0.0 collective-permute-start
  6.0 1.3 %prepare_rows.1 = (f32[128,128]{1,0:T(8,128)S(1)}, bf16[256,128]{1,0:T(8,128)(2,1)S(1)}, bf16[128,256]{1,0:T(8,128)(2,1)S(1)}, bf16[32,256]{1,0:T(8,128)(2,1)S(1)}, bf16[16,2,128,128]{3,2,1,0:T(8,128)(2,1)S(1)}) custom-call(f32[7,128,128]{2,1,0:T(8,128)S(1)} %get-tuple-element.27.vloc_ref.refs_4_, f32[128,128]{1,0:T(8,128)S(1)} %get-tuple-element.28.g_ref.refs_7_, ...), custom_call_target="tpu_custom_call" | custom-call | tf_op jit(solution)/shard_map/prepare_rows/pallas_call | solution.py:373
  7.3 0.0 collective-permute-done.2.refs_3_
  7.4 1.7 %collective-permute-done.1.refs_2_ = bf16[48,128]{1,0:T(8,128)(2,1)S(1)} collective-permute-done((bf16[48,128]{1,0:T(8,128)(2,1)S(1)}, bf16[48,128]{1,0:T(8,128)(2,1)S(1)}, u32[]{:S(2)}, u32[]{:S(2)}) %collective-permute-start.1) | collective-permute-done | bytes 12320 | tf_op jit(solution)/shard_map/ppermute | solution.py:323
  9.0 0.0 collective-permute-done.refs_1_
  9.0 0.8 %couple_sections.1 = (f32[128,128]{1,0:T(8,128)S(1)}, bf16[32,1024]{1,0:T(8,128)(2,1)S(1)}, bf16[32,1024]{1,0:T(8,128)(2,1)S(1)}, bf16[32,1024]{1,0:T(8,128)(2,1...) custom-call(bf16[48,128]{1,0:T(8,128)(2,1)S(1)} %get-tuple-element.2, ...), custom_call_target="tpu_custom_call" | custom-call | tf_op jit(solution)/shard_map/couple_sections/pallas_call | solution.py:406
  9.8 3.7 %collective-permute-start.3 = (bf16[32,1024]{1,0:T(8,128)(2,1)S(1)}, bf16[32,1024]{1,0:T(8,128)(2,1)S(1)}, u32[]{:S(2)}, u32[]{:S(2)}) collective-permute-start(bf16[32,1024]{1,0:T(8,128)(2,1)S(1)} %get-tuple-element.40), channel_id=1, source_target_pairs={{0,24},{4,28},{8,16},{12,20},{16,8},{20,12},{24,0},{28,4},{1,25},{... | collective-permute-start | bytes 196616 | tf_op jit(solution)/shard_map/ppermute | solution.py:323
  13.5 1.5 %collective-permute-start.4 = (bf16[32,1024]{1,0:T(8,128)(2,1)S(1)}, bf16[32,1024]{1,0:T(8,128)(2,1)S(1)}, u32[]{:S(2)}, u32[]{:S(2)}) collective-permute-start(bf16[32,1024]{1,0:T(8,128)(2,1)S(1)} %get-tuple-element.41), channel_id=1, source_target_pairs={{0,4},{4,0},{8,12},{12,8},{16,20},{20,16},{24,28},{28,24},{1,5},{5... | collective-permute-start | bytes 196616 | tf_op jit(solution)/shard_map/ppermute | solution.py:323
  15.0 0.2 collective-permute-start.5
  15.2 1.7 %collective-permute-start.6 = (bf16[32,1024]{1,0:T(8,128)(2,1)S(1)}, bf16[32,1024]{1,0:T(8,128)(2,1)S(1)}, u32[]{:S(2)}, u32[]{:S(2)}) collective-permute-start(bf16[32,1024]{1,0:T(8,128)(2,1)S(1)} %get-tuple-element.43), channel_id=1, source_target_pairs={{0,20},{4,16},{8,28},{12,24},{16,4},{20,0},{24,12},{28,8},{1,21},{... | collective-permute-start | bytes 196616 | tf_op jit(solution)/shard_map/ppermute | solution.py:323
  16.9 3.4 %collective-permute-start.7 = (bf16[32,1024]{1,0:T(8,128)(2,1)S(1)}, bf16[32,1024]{1,0:T(8,128)(2,1)S(1)}, u32[]{:S(2)}, u32[]{:S(2)}) collective-permute-start(bf16[32,1024]{1,0:T(8,128)(2,1)S(1)} %get-tuple-element.44), channel_id=1, source_target_pairs={{0,8},{4,12},{8,0},{12,4},{16,24},{20,28},{24,16},{28,20},{1,9},{5... | collective-permute-start | bytes 196616 | tf_op jit(solution)/shard_map/ppermute | solution.py:323
  20.3 0.0 collective-permute-done.3.refs_1_
  20.3 0.6 %collective-permute-start.8 = (bf16[32,1024]{1,0:T(8,128)(2,1)S(1)}, bf16[32,1024]{1,0:T(8,128)(2,1)S(1)}, u32[]{:S(2)}, u32[]{:S(2)}) collective-permute-start(bf16[32,1024]{1,0:T(8,128)(2,1)S(1)} %get-tuple-element.45), channel_id=1, source_target_pairs={{0,16},{4,20},{8,24},{12,28},{16,0},{20,4},{24,8},{28,12},{1,17},{... | collective-permute-start | bytes 196616 | tf_op jit(solution)/shard_map/ppermute | solution.py:323
  20.9 0.0 collective-permute-done.4.refs_2_
  20.9 1.0 %collective-permute-start.9 = (bf16[32,1024]{1,0:T(8,128)(2,1)S(1)}, bf16[32,1024]{1,0:T(8,128)(2,1)S(1)}, u32[]{:S(2)}, u32[]{:S(2)}) collective-permute-start(bf16[32,1024]{1,0:T(8,128)(2,1)S(1)} %get-tuple-element.46), channel_id=1, source_target_pairs={{0,12},{4,8},{8,4},{12,0},{16,28},{20,24},{24,20},{28,16},{1,13},{... | collective-permute-start | bytes 196616 | tf_op jit(solution)/shard_map/ppermute | solution.py:323
  21.9 2.2 %fetch_tiles.1 = (bf16[64,2,128,128]{3,2,1,0:T(8,128)(2,1)S(1)}, f32[128,128]{1,0:T(8,128)}) custom-call(f32[128,128]{1,0:T(8,128)S(1)} %get-tuple-element.35.final_ref, bf16[128,2,128,128]{3,2,1,0:T(8,128)(2,1)} %bitcast.7), custom_call_target="tpu_custom_call" | custom-call | tf_op jit(solution)/shard_map/fetch_tiles/pallas_call | solution.py:438
  24.1 0.0 collective-permute-done.5.refs_3_
  24.1 0.2 collective-permute-done.6.refs_4_
  24.4 0.0 collective-permute-done.7.refs_5_
  24.4 1.2 %collective-permute-done.8.refs_6_ = bf16[32,1024]{1,0:T(8,128)(2,1)S(1)} collective-permute-done((bf16[32,1024]{1,0:T(8,128)(2,1)S(1)}, bf16[32,1024]{1,0:T(8,128)(2,1)S(1)}, u32[]{:S(2)}, u32[]{:S(2)}) %collective-permute-start.8) | collective-permute-done | bytes 65568 | tf_op jit(solution)/shard_map/ppermute | solution.py:323
  25.6 0.9 %collective-permute-done.9.refs_7_ = bf16[32,1024]{1,0:T(8,128)(2,1)S(1)} collective-permute-done((bf16[32,1024]{1,0:T(8,128)(2,1)S(1)}, bf16[32,1024]{1,0:T(8,128)(2,1)S(1)}, u32[]{:S(2)}, u32[]{:S(2)}) %collective-permute-start.9) | collective-permute-done | bytes 65568 | tf_op jit(solution)/shard_map/ppermute | solution.py:323
  26.5 1.7 %readout.1 = bf16[32,8,128]{2,1,0:T(8,128)(2,1)S(1)} custom-call(bf16[32,256]{1,0:T(8,128)(2,1)S(1)} %get-tuple-element.37.select_ref, bf16[128,256]{1,0:T(8,128)(2,1)S(1)} %get-tuple-element.38.order_ref, bf16[32,1024]{1,0:T(8,128)(2,1)S(1)} %get-tuple-element.39.refs_0_, bf16[32,1024]{1,0:T(8,128)(2,1)S(1)} %collective-permute-done.3.refs_1_, ...), custom_call_target="tpu_custom_call" | custom-call | tf_op jit(solution)/shard_map/readout/pallas_call | solution.py:453
  28.2 9.6 %all_to_all.5 = bf16[32,8,128]{2,1,0:T(8,128)(2,1)S(1)} all-to-all(bf16[32,8,128]{2,1,0:T(8,128)(2,1)S(1)} %readout.1), channel_id=1, replica_groups=mesh['tile'=8,'sec'=4] {'tile','sec'}, dimensions={0} | all-to-all | bytes 131072 | tf_op jit(solution)/shard_map/all_to_all | solution.py:473
  37.9 0.6 %convert_reduce_fusion = f32[8,128]{1,0:T(8,128)} fusion(bf16[32,8,128]{2,1,0:T(8,128)(2,1)S(1)} %all_to_all.5), kind=kLoop, calls=%fused_computation | loop fusion | flops 64512 | bytes 69632 | tf_op jit(solution)/shard_map/reduce_sum | solution.py:474
Async XLA Ops:
  2.9 4.5 %collective-permute-start.2 = (bf16[48,128]{1,0:T(8,128)(2,1)S(1)}, bf16[48,128]{1,0:T(8,128)(2,1)S(1)}, u32[]{:S(2)}, u32[]{:S(2)}) collective-permute-start(bf16[48,128]{1,0:T(8,128)(2,1)S(1)} %get-tuple-element.26.refs_0_), channel_id=1, source_target_pairs={{0,3},{1,2},{2,1},{3,0},{4,7},{5,6},{6,5},{7,4},{8,11},{9,10},{10,... | collective-permute-start | bytes 36872 | tf_op jit(solution)/shard_map/ppermute | solution.py:323
  5.3 3.7 %collective-permute-start.1 = (bf16[48,128]{1,0:T(8,128)(2,1)S(1)}, bf16[48,128]{1,0:T(8,128)(2,1)S(1)}, u32[]{:S(2)}, u32[]{:S(2)}) collective-permute-start(bf16[48,128]{1,0:T(8,128)(2,1)S(1)} %get-tuple-element.26.refs_0_), channel_id=1, source_target_pairs={{0,2},{1,3},{2,0},{3,1},{4,6},{5,7},{6,4},{7,5},{8,10},{9,11},{10,... | collective-permute-start | bytes 36872 | tf_op jit(solution)/shard_map/ppermute | solution.py:323
  6.0 3.1 %collective-permute-start = (bf16[48,128]{1,0:T(8,128)(2,1)S(1)}, bf16[48,128]{1,0:T(8,128)(2,1)S(1)}, u32[]{:S(2)}, u32[]{:S(2)}) collective-permute-start(bf16[48,128]{1,0:T(8,128)(2,1)S(1)} %get-tuple-element.26.refs_0_), channel_id=1, source_target_pairs={{0,1},{1,0},{2,3},{3,2},{4,5},{5,4},{6,7},{7,6},{8,9},{9,8},{10,11... | collective-permute-start | bytes 36872 | tf_op jit(solution)/shard_map/ppermute | solution.py:323
  9.8 10.5 %collective-permute-start.3 = (bf16[32,1024]{1,0:T(8,128)(2,1)S(1)}, bf16[32,1024]{1,0:T(8,128)(2,1)S(1)}, u32[]{:S(2)}, u32[]{:S(2)}) collective-permute-start(bf16[32,1024]{1,0:T(8,128)(2,1)S(1)} %get-tuple-element.40), channel_id=1, source_target_pairs={{0,24},{4,28},{8,16},{12,20},{16,8},{20,12},{24,0},{28,4},{1,25},{... | collective-permute-start | bytes 196616 | tf_op jit(solution)/shard_map/ppermute | solution.py:323
  13.5 7.4 %collective-permute-start.4 = (bf16[32,1024]{1,0:T(8,128)(2,1)S(1)}, bf16[32,1024]{1,0:T(8,128)(2,1)S(1)}, u32[]{:S(2)}, u32[]{:S(2)}) collective-permute-start(bf16[32,1024]{1,0:T(8,128)(2,1)S(1)} %get-tuple-element.41), channel_id=1, source_target_pairs={{0,4},{4,0},{8,12},{12,8},{16,20},{20,16},{24,28},{28,24},{1,5},{5... | collective-permute-start | bytes 196616 | tf_op jit(solution)/shard_map/ppermute | solution.py:323
  15.0 9.1 %collective-permute-start.5 = (bf16[32,1024]{1,0:T(8,128)(2,1)S(1)}, bf16[32,1024]{1,0:T(8,128)(2,1)S(1)}, u32[]{:S(2)}, u32[]{:S(2)}) collective-permute-start(bf16[32,1024]{1,0:T(8,128)(2,1)S(1)} %get-tuple-element.42), channel_id=1, source_target_pairs={{0,28},{4,24},{8,20},{12,16},{16,12},{20,8},{24,4},{28,0},{1,29},{... | collective-permute-start | bytes 196616 | tf_op jit(solution)/shard_map/ppermute | solution.py:323
  15.2 9.2 %collective-permute-start.6 = (bf16[32,1024]{1,0:T(8,128)(2,1)S(1)}, bf16[32,1024]{1,0:T(8,128)(2,1)S(1)}, u32[]{:S(2)}, u32[]{:S(2)}) collective-permute-start(bf16[32,1024]{1,0:T(8,128)(2,1)S(1)} %get-tuple-element.43), channel_id=1, source_target_pairs={{0,20},{4,16},{8,28},{12,24},{16,4},{20,0},{24,12},{28,8},{1,21},{... | collective-permute-start | bytes 196616 | tf_op jit(solution)/shard_map/ppermute | solution.py:323
  16.9 7.5 %collective-permute-start.7 = (bf16[32,1024]{1,0:T(8,128)(2,1)S(1)}, bf16[32,1024]{1,0:T(8,128)(2,1)S(1)}, u32[]{:S(2)}, u32[]{:S(2)}) collective-permute-start(bf16[32,1024]{1,0:T(8,128)(2,1)S(1)} %get-tuple-element.44), channel_id=1, source_target_pairs={{0,8},{4,12},{8,0},{12,4},{16,24},{20,28},{24,16},{28,20},{1,9},{5... | collective-permute-start | bytes 196616 | tf_op jit(solution)/shard_map/ppermute | solution.py:323
  20.3 5.3 %collective-permute-start.8 = (bf16[32,1024]{1,0:T(8,128)(2,1)S(1)}, bf16[32,1024]{1,0:T(8,128)(2,1)S(1)}, u32[]{:S(2)}, u32[]{:S(2)}) collective-permute-start(bf16[32,1024]{1,0:T(8,128)(2,1)S(1)} %get-tuple-element.45), channel_id=1, source_target_pairs={{0,16},{4,20},{8,24},{12,28},{16,0},{20,4},{24,8},{28,12},{1,17},{... | collective-permute-start | bytes 196616 | tf_op jit(solution)/shard_map/ppermute | solution.py:323
  20.9 5.7 %collective-permute-start.9 = (bf16[32,1024]{1,0:T(8,128)(2,1)S(1)}, bf16[32,1024]{1,0:T(8,128)(2,1)S(1)}, u32[]{:S(2)}, u32[]{:S(2)}) collective-permute-start(bf16[32,1024]{1,0:T(8,128)(2,1)S(1)} %get-tuple-element.46), channel_id=1, source_target_pairs={{0,12},{4,8},{8,4},{12,0},{16,28},{20,24},{24,20},{28,16},{1,13},{... | collective-permute-start | bytes 196616 | tf_op jit(solution)/shard_map/ppermute | solution.py:323

commit v9 on v8

--- a/solution.py
+++ b/solution.py
@@ -236,7 +236,7 @@
         incoming[pl.ds(2 * j + 1, 1), :] = jnp.sum(
             jnp.where(own, from_right[j], 0.0), axis=0, keepdims=True
         )
-    by_cell = incoming[...].T
+    by_cell = incoming[...].T.astype(BF)
 
     block = 16
     lag_left = jnp.broadcast_to(TIME_STEP * AXIAL * turned_ref[0:1, :], (block, width)).astype(BF)
@@ -245,7 +245,7 @@
     for c in range(0, cells, block):
         span = slice(c, c + block)
         unit = [
-            jnp.broadcast_to(by_cell[span, q : q + 1], (block, width)).astype(BF)
+            jnp.broadcast_to(by_cell[span, q : q + 1], (block, width))
             for q in range(2 * steps)
         ]
         lefts = [None, lag_left] + [resp_ref[l, span, :] for l in range(steps - 1)]

time: 38.7 us -> 38.6 us (level)
  no operation moved by 1% of the time
where the time goes in v9:
time: 38.6 us; the launch traced here: 38.4 us
  starting transfers between devices  15.2 us (39%)
  blocking collectives  9.62 us (25%)
  Pallas kernels  8.25 us (21%)
  waiting for transfers between devices  4.07 us (11%)
  between operations  0.69 us (2%)
  other arithmetic  0.63 us (2%)
    ppermute x10, starting transfers between devices, exchange(): lax.ppermute(blocks[p], axis, [(i, i ^ p) for i in range(count)])  15.2 us
    all_to_all x1, blocking collectives, on_device(): lax.all_to_all(partial_sum, ('tile', 'sec'), split_axis=0, concat_axis=0,...  9.62 us
    ppermute x10, waiting for transfers between devices, exchange(): lax.ppermute(blocks[p], axis, [(i, i ^ p) for i in range(count)])  4.07 us
    pallas_call x1, Pallas kernels, on_device(): pl.pallas_call(local_kernel, out_shape=(jax.ShapeDtypeStruct((steps - 1,...  2.25 us
    pallas_call x1, Pallas kernels, on_device(): pl.pallas_call(fetch_kernel, out_shape=(jax.ShapeDtypeStruct((PARTS[2],)...  2.23 us
    pallas_call x1, Pallas kernels, on_device(): pl.pallas_call(functools.partial(readout_kernel, steps, sequence), out_sh...  1.71 us
    pallas_call x1, Pallas kernels, on_device(): pl.pallas_call(functools.partial(prepare_kernel, tiles, paired), out_shap...  1.32 us
  transfers between devices with their start and end apart: 10, of which 4 were waited for; matrix products, arithmetic and copies ran while one was open for 0% of the time, Pallas kernels for 9%

profile of v9, /device:TPU:0, one launch (start us, length us, event | category | flops | bytes accessed | tf_op | source)
XLA Modules:
  0.0 38.4 jit_solution(3535714036284868923)
XLA Ops:
  0.6 2.2 %local_steps.1 = (f32[7,128,128]{2,1,0:T(8,128)S(1)}, bf16[7,256,128]{2,1,0:T(8,128)(2,1)S(1)}, bf16[48,128]{1,0:T(8,128)(2,1)S(1)}, f32[128,128]{1,0:T(8,128)S(...) custom-call(f32[128,128]{1,0:T(8,128)} %v_hbm.1, ...), custom_call_target="tpu_custom_call" | custom-call | tf_op jit(solution)/shard_map/local_steps/pallas_call | solution.py:343
  2.9 2.4 %collective-permute-start.2 = (bf16[48,128]{1,0:T(8,128)(2,1)S(1)}, bf16[48,128]{1,0:T(8,128)(2,1)S(1)}, u32[]{:S(2)}, u32[]{:S(2)}) collective-permute-start(bf16[48,128]{1,0:T(8,128)(2,1)S(1)} %get-tuple-element.26.refs_0_), channel_id=1, source_target_pairs={{0,3},{1,2},{2,1},{3,0},{4,7},{5,6},{6,5},{7,4},{8,11},{9,10},{10,... | collective-permute-start | bytes 36872 | tf_op jit(solution)/shard_map/ppermute | solution.py:323
  5.3 0.6 %collective-permute-start.1 = (bf16[48,128]{1,0:T(8,128)(2,1)S(1)}, bf16[48,128]{1,0:T(8,128)(2,1)S(1)}, u32[]{:S(2)}, u32[]{:S(2)}) collective-permute-start(bf16[48,128]{1,0:T(8,128)(2,1)S(1)} %get-tuple-element.26.refs_0_), channel_id=1, source_target_pairs={{0,2},{1,3},{2,0},{3,1},{4,6},{5,7},{6,4},{7,5},{8,10},{9,11},{10,... | collective-permute-start | bytes 36872 | tf_op jit(solution)/shard_map/ppermute | solution.py:323
  6.0 0.0 collective-permute-start
  6.0 1.3 %prepare_rows.1 = (f32[128,128]{1,0:T(8,128)S(1)}, bf16[256,128]{1,0:T(8,128)(2,1)S(1)}, bf16[128,256]{1,0:T(8,128)(2,1)S(1)}, bf16[32,256]{1,0:T(8,128)(2,1)S(1)}, bf16[16,2,128,128]{3,2,1,0:T(8,128)(2,1)S(1)}) custom-call(f32[7,128,128]{2,1,0:T(8,128)S(1)} %get-tuple-element.27.vloc_ref.refs_4_, f32[128,128]{1,0:T(8,128)S(1)} %get-tuple-element.28.g_ref.refs_7_, ...), custom_call_target="tpu_custom_call" | custom-call | tf_op jit(solution)/shard_map/prepare_rows/pallas_call | solution.py:373
  7.3 0.0 collective-permute-done.2.refs_3_
  7.4 1.7 %collective-permute-done.1.refs_2_ = bf16[48,128]{1,0:T(8,128)(2,1)S(1)} collective-permute-done((bf16[48,128]{1,0:T(8,128)(2,1)S(1)}, bf16[48,128]{1,0:T(8,128)(2,1)S(1)}, u32[]{:S(2)}, u32[]{:S(2)}) %collective-permute-start.1) | collective-permute-done | bytes 12320 | tf_op jit(solution)/shard_map/ppermute | solution.py:323
  9.0 0.0 collective-permute-done.refs_1_
  9.0 0.7 %couple_sections.1 = (f32[128,128]{1,0:T(8,128)S(1)}, bf16[32,1024]{1,0:T(8,128)(2,1)S(1)}, bf16[32,1024]{1,0:T(8,128)(2,1)S(1)}, bf16[32,1024]{1,0:T(8,128)(2,1...) custom-call(bf16[48,128]{1,0:T(8,128)(2,1)S(1)} %get-tuple-element.2, ...), custom_call_target="tpu_custom_call" | custom-call | tf_op jit(solution)/shard_map/couple_sections/pallas_call | solution.py:406
  9.8 3.7 %collective-permute-start.3 = (bf16[32,1024]{1,0:T(8,128)(2,1)S(1)}, bf16[32,1024]{1,0:T(8,128)(2,1)S(1)}, u32[]{:S(2)}, u32[]{:S(2)}) collective-permute-start(bf16[32,1024]{1,0:T(8,128)(2,1)S(1)} %get-tuple-element.40), channel_id=1, source_target_pairs={{0,24},{4,28},{8,16},{12,20},{16,8},{20,12},{24,0},{28,4},{1,25},{... | collective-permute-start | bytes 196616 | tf_op jit(solution)/shard_map/ppermute | solution.py:323
  13.5 1.5 %collective-permute-start.4 = (bf16[32,1024]{1,0:T(8,128)(2,1)S(1)}, bf16[32,1024]{1,0:T(8,128)(2,1)S(1)}, u32[]{:S(2)}, u32[]{:S(2)}) collective-permute-start(bf16[32,1024]{1,0:T(8,128)(2,1)S(1)} %get-tuple-element.41), channel_id=1, source_target_pairs={{0,4},{4,0},{8,12},{12,8},{16,20},{20,16},{24,28},{28,24},{1,5},{5... | collective-permute-start | bytes 196616 | tf_op jit(solution)/shard_map/ppermute | solution.py:323
  15.0 0.2 collective-permute-start.5
  15.1 1.7 %collective-permute-start.6 = (bf16[32,1024]{1,0:T(8,128)(2,1)S(1)}, bf16[32,1024]{1,0:T(8,128)(2,1)S(1)}, u32[]{:S(2)}, u32[]{:S(2)}) collective-permute-start(bf16[32,1024]{1,0:T(8,128)(2,1)S(1)} %get-tuple-element.43), channel_id=1, source_target_pairs={{0,20},{4,16},{8,28},{12,24},{16,4},{20,0},{24,12},{28,8},{1,21},{... | collective-permute-start | bytes 196616 | tf_op jit(solution)/shard_map/ppermute | solution.py:323
  16.9 3.4 %collective-permute-start.7 = (bf16[32,1024]{1,0:T(8,128)(2,1)S(1)}, bf16[32,1024]{1,0:T(8,128)(2,1)S(1)}, u32[]{:S(2)}, u32[]{:S(2)}) collective-permute-start(bf16[32,1024]{1,0:T(8,128)(2,1)S(1)} %get-tuple-element.44), channel_id=1, source_target_pairs={{0,8},{4,12},{8,0},{12,4},{16,24},{20,28},{24,16},{28,20},{1,9},{5... | collective-permute-start | bytes 196616 | tf_op jit(solution)/shard_map/ppermute | solution.py:323
  20.3 0.0 collective-permute-done.3.refs_1_
  20.3 0.6 %collective-permute-start.8 = (bf16[32,1024]{1,0:T(8,128)(2,1)S(1)}, bf16[32,1024]{1,0:T(8,128)(2,1)S(1)}, u32[]{:S(2)}, u32[]{:S(2)}) collective-permute-start(bf16[32,1024]{1,0:T(8,128)(2,1)S(1)} %get-tuple-element.45), channel_id=1, source_target_pairs={{0,16},{4,20},{8,24},{12,28},{16,0},{20,4},{24,8},{28,12},{1,17},{... | collective-permute-start | bytes 196616 | tf_op jit(solution)/shard_map/ppermute | solution.py:323
  20.8 0.0 collective-permute-done.4.refs_2_
  20.8 1.0 %collective-permute-start.9 = (bf16[32,1024]{1,0:T(8,128)(2,1)S(1)}, bf16[32,1024]{1,0:T(8,128)(2,1)S(1)}, u32[]{:S(2)}, u32[]{:S(2)}) collective-permute-start(bf16[32,1024]{1,0:T(8,128)(2,1)S(1)} %get-tuple-element.46), channel_id=1, source_target_pairs={{0,12},{4,8},{8,4},{12,0},{16,28},{20,24},{24,20},{28,16},{1,13},{... | collective-permute-start | bytes 196616 | tf_op jit(solution)/shard_map/ppermute | solution.py:323
  21.8 2.2 %fetch_tiles.1 = (bf16[64,2,128,128]{3,2,1,0:T(8,128)(2,1)S(1)}, f32[128,128]{1,0:T(8,128)}) custom-call(f32[128,128]{1,0:T(8,128)S(1)} %get-tuple-element.35.final_ref, bf16[128,2,128,128]{3,2,1,0:T(8,128)(2,1)} %bitcast.7), custom_call_target="tpu_custom_call" | custom-call | tf_op jit(solution)/shard_map/fetch_tiles/pallas_call | solution.py:438
  24.1 0.0 collective-permute-done.5.refs_3_
  24.1 0.2 collective-permute-done.6.refs_4_
  24.3 0.0 collective-permute-done.7.refs_5_
  24.3 1.2 %collective-permute-done.8.refs_6_ = bf16[32,1024]{1,0:T(8,128)(2,1)S(1)} collective-permute-done((bf16[32,1024]{1,0:T(8,128)(2,1)S(1)}, bf16[32,1024]{1,0:T(8,128)(2,1)S(1)}, u32[]{:S(2)}, u32[]{:S(2)}) %collective-permute-start.8) | collective-permute-done | bytes 65568 | tf_op jit(solution)/shard_map/ppermute | solution.py:323
  25.6 0.9 %collective-permute-done.9.refs_7_ = bf16[32,1024]{1,0:T(8,128)(2,1)S(1)} collective-permute-done((bf16[32,1024]{1,0:T(8,128)(2,1)S(1)}, bf16[32,1024]{1,0:T(8,128)(2,1)S(1)}, u32[]{:S(2)}, u32[]{:S(2)}) %collective-permute-start.9) | collective-permute-done | bytes 65568 | tf_op jit(solution)/shard_map/ppermute | solution.py:323
  26.5 1.7 %readout.1 = bf16[32,8,128]{2,1,0:T(8,128)(2,1)S(1)} custom-call(bf16[32,256]{1,0:T(8,128)(2,1)S(1)} %get-tuple-element.37.select_ref, bf16[128,256]{1,0:T(8,128)(2,1)S(1)} %get-tuple-element.38.order_ref, bf16[32,1024]{1,0:T(8,128)(2,1)S(1)} %get-tuple-element.39.refs_0_, bf16[32,1024]{1,0:T(8,128)(2,1)S(1)} %collective-permute-done.3.refs_1_, ...), custom_call_target="tpu_custom_call" | custom-call | tf_op jit(solution)/shard_map/readout/pallas_call | solution.py:453
  28.2 9.6 %all_to_all.5 = bf16[32,8,128]{2,1,0:T(8,128)(2,1)S(1)} all-to-all(bf16[32,8,128]{2,1,0:T(8,128)(2,1)S(1)} %readout.1), channel_id=1, replica_groups=mesh['tile'=8,'sec'=4] {'tile','sec'}, dimensions={0} | all-to-all | bytes 131072 | tf_op jit(solution)/shard_map/all_to_all | solution.py:473
  37.8 0.6 %convert_reduce_fusion = f32[8,128]{1,0:T(8,128)} fusion(bf16[32,8,128]{2,1,0:T(8,128)(2,1)S(1)} %all_to_all.5), kind=kLoop, calls=%fused_computation | loop fusion | flops 64512 | bytes 69632 | tf_op jit(solution)/shard_map/reduce_sum | solution.py:474
Async XLA Ops:
  2.9 4.5 %collective-permute-start.2 = (bf16[48,128]{1,0:T(8,128)(2,1)S(1)}, bf16[48,128]{1,0:T(8,128)(2,1)S(1)}, u32[]{:S(2)}, u32[]{:S(2)}) collective-permute-start(bf16[48,128]{1,0:T(8,128)(2,1)S(1)} %get-tuple-element.26.refs_0_), channel_id=1, source_target_pairs={{0,3},{1,2},{2,1},{3,0},{4,7},{5,6},{6,5},{7,4},{8,11},{9,10},{10,... | collective-permute-start | bytes 36872 | tf_op jit(solution)/shard_map/ppermute | solution.py:323
  5.3 3.7 %collective-permute-start.1 = (bf16[48,128]{1,0:T(8,128)(2,1)S(1)}, bf16[48,128]{1,0:T(8,128)(2,1)S(1)}, u32[]{:S(2)}, u32[]{:S(2)}) collective-permute-start(bf16[48,128]{1,0:T(8,128)(2,1)S(1)} %get-tuple-element.26.refs_0_), channel_id=1, source_target_pairs={{0,2},{1,3},{2,0},{3,1},{4,6},{5,7},{6,4},{7,5},{8,10},{9,11},{10,... | collective-permute-start | bytes 36872 | tf_op jit(solution)/shard_map/ppermute | solution.py:323
  6.0 3.1 %collective-permute-start = (bf16[48,128]{1,0:T(8,128)(2,1)S(1)}, bf16[48,128]{1,0:T(8,128)(2,1)S(1)}, u32[]{:S(2)}, u32[]{:S(2)}) collective-permute-start(bf16[48,128]{1,0:T(8,128)(2,1)S(1)} %get-tuple-element.26.refs_0_), channel_id=1, source_target_pairs={{0,1},{1,0},{2,3},{3,2},{4,5},{5,4},{6,7},{7,6},{8,9},{9,8},{10,11... | collective-permute-start | bytes 36872 | tf_op jit(solution)/shard_map/ppermute | solution.py:323
  9.8 10.5 %collective-permute-start.3 = (bf16[32,1024]{1,0:T(8,128)(2,1)S(1)}, bf16[32,1024]{1,0:T(8,128)(2,1)S(1)}, u32[]{:S(2)}, u32[]{:S(2)}) collective-permute-start(bf16[32,1024]{1,0:T(8,128)(2,1)S(1)} %get-tuple-element.40), channel_id=1, source_target_pairs={{0,24},{4,28},{8,16},{12,20},{16,8},{20,12},{24,0},{28,4},{1,25},{... | collective-permute-start | bytes 196616 | tf_op jit(solution)/shard_map/ppermute | solution.py:323
  13.5 7.4 %collective-permute-start.4 = (bf16[32,1024]{1,0:T(8,128)(2,1)S(1)}, bf16[32,1024]{1,0:T(8,128)(2,1)S(1)}, u32[]{:S(2)}, u32[]{:S(2)}) collective-permute-start(bf16[32,1024]{1,0:T(8,128)(2,1)S(1)} %get-tuple-element.41), channel_id=1, source_target_pairs={{0,4},{4,0},{8,12},{12,8},{16,20},{20,16},{24,28},{28,24},{1,5},{5... | collective-permute-start | bytes 196616 | tf_op jit(solution)/shard_map/ppermute | solution.py:323
  15.0 9.1 %collective-permute-start.5 = (bf16[32,1024]{1,0:T(8,128)(2,1)S(1)}, bf16[32,1024]{1,0:T(8,128)(2,1)S(1)}, u32[]{:S(2)}, u32[]{:S(2)}) collective-permute-start(bf16[32,1024]{1,0:T(8,128)(2,1)S(1)} %get-tuple-element.42), channel_id=1, source_target_pairs={{0,28},{4,24},{8,20},{12,16},{16,12},{20,8},{24,4},{28,0},{1,29},{... | collective-permute-start | bytes 196616 | tf_op jit(solution)/shard_map/ppermute | solution.py:323
  15.1 9.2 %collective-permute-start.6 = (bf16[32,1024]{1,0:T(8,128)(2,1)S(1)}, bf16[32,1024]{1,0:T(8,128)(2,1)S(1)}, u32[]{:S(2)}, u32[]{:S(2)}) collective-permute-start(bf16[32,1024]{1,0:T(8,128)(2,1)S(1)} %get-tuple-element.43), channel_id=1, source_target_pairs={{0,20},{4,16},{8,28},{12,24},{16,4},{20,0},{24,12},{28,8},{1,21},{... | collective-permute-start | bytes 196616 | tf_op jit(solution)/shard_map/ppermute | solution.py:323
  16.9 7.5 %collective-permute-start.7 = (bf16[32,1024]{1,0:T(8,128)(2,1)S(1)}, bf16[32,1024]{1,0:T(8,128)(2,1)S(1)}, u32[]{:S(2)}, u32[]{:S(2)}) collective-permute-start(bf16[32,1024]{1,0:T(8,128)(2,1)S(1)} %get-tuple-element.44), channel_id=1, source_target_pairs={{0,8},{4,12},{8,0},{12,4},{16,24},{20,28},{24,16},{28,20},{1,9},{5... | collective-permute-start | bytes 196616 | tf_op jit(solution)/shard_map/ppermute | solution.py:323
  20.3 5.3 %collective-permute-start.8 = (bf16[32,1024]{1,0:T(8,128)(2,1)S(1)}, bf16[32,1024]{1,0:T(8,128)(2,1)S(1)}, u32[]{:S(2)}, u32[]{:S(2)}) collective-permute-start(bf16[32,1024]{1,0:T(8,128)(2,1)S(1)} %get-tuple-element.45), channel_id=1, source_target_pairs={{0,16},{4,20},{8,24},{12,28},{16,0},{20,4},{24,8},{28,12},{1,17},{... | collective-permute-start | bytes 196616 | tf_op jit(solution)/shard_map/ppermute | solution.py:323
  20.8 5.6 %collective-permute-start.9 = (bf16[32,1024]{1,0:T(8,128)(2,1)S(1)}, bf16[32,1024]{1,0:T(8,128)(2,1)S(1)}, u32[]{:S(2)}, u32[]{:S(2)}) collective-permute-start(bf16[32,1024]{1,0:T(8,128)(2,1)S(1)} %get-tuple-element.46), channel_id=1, source_target_pairs={{0,12},{4,8},{8,4},{12,0},{16,28},{20,24},{24,20},{28,16},{1,13},{... | collective-permute-start | bytes 196616 | tf_op jit(solution)/shard_map/ppermute | solution.py:323

commit v10 on v9

--- a/solution.py
+++ b/solution.py
@@ -82,9 +82,9 @@
     copies = start_all(
         [
             (cable_hbm, cable_ref),
-            (v_hbm, v_ref),
             (g_hbm, g_ref),
             (e_hbm, e_ref),
+            (v_hbm, v_ref),
             (drive_hbm, drive_ref),
             (transfer_hbm.at[pl.ds(0, PARTS[0])], early_ref),
         ],
@@ -96,25 +96,29 @@
     cable = cable_ref[...].T
     turned_ref[...] = cable
     weights = hi_lo_weights(cable)
-    for copy in copies[1:5]:
+    for copy in copies[1:3]:
         copy.wait()
     keep, source = keep_and_source(g_ref[...], e_ref[...])
+    left = jnp.broadcast_to(TIME_STEP * AXIAL * cable[0:1, :], (cells, width))
+    right = jnp.broadcast_to(TIME_STEP * AXIAL * cable[width - 1 : width, :], (cells, width))
+    next_sides = solve(left * keep, weights), solve(right * keep, weights)
+    for copy in copies[3:5]:
+        copy.wait()
     lane = iota((cells, width), 1)
 
     def with_ends(table, x, row):
         return jnp.where((lane >= row) & (lane < row + 2), pltpu.roll(x, row + 1, 1), table)
 
     voltage = v_ref[...]
-    left = jnp.broadcast_to(TIME_STEP * AXIAL * cable[0:1, :], (cells, width))
-    right = jnp.broadcast_to(TIME_STEP * AXIAL * cable[width - 1 : width, :], (cells, width))
     left_row, right_row = 2 * steps, 4 * steps
     table = with_ends(jnp.zeros((cells, width), F32), voltage, 0)
     table = with_ends(with_ends(table, left, left_row), right, right_row)
     for k in range(steps - 1):
         rhs = voltage * keep + source + TIME_STEP * drive_ref[k].astype(F32)
         voltage = solve(rhs, weights)
-        left = solve(left * keep, weights)
-        right = solve(right * keep, weights)
+        left, right = next_sides
+        if k < steps - 2:
+            next_sides = solve(left * keep, weights), solve(right * keep, weights)
         vloc_ref[k] = voltage
         resp_ref[k, :cells] = left.astype(BF)
         resp_ref[k, cells:] = right.astype(BF)

time: 38.6 us -> 38.6 us (level)
  no operation moved by 1% of the time
where the time goes in v10:
time: 38.6 us; the launch traced here: 38.4 us
  starting transfers between devices  15.2 us (39%)
  blocking collectives  9.53 us (25%)
  Pallas kernels  8.3 us (22%)
  waiting for transfers between devices  4.08 us (11%)
  between operations  0.69 us (2%)
  other arithmetic  0.63 us (2%)
    ppermute x10, starting transfers between devices, exchange(): lax.ppermute(blocks[p], axis, [(i, i ^ p) for i in range(count)])  15.2 us
    all_to_all x1, blocking collectives, on_device(): lax.all_to_all(partial_sum, ('tile', 'sec'), split_axis=0, concat_axis=0,...  9.53 us
    ppermute x10, waiting for transfers between devices, exchange(): lax.ppermute(blocks[p], axis, [(i, i ^ p) for i in range(count)])  4.08 us
    pallas_call x1, Pallas kernels, on_device(): pl.pallas_call(local_kernel, out_shape=(jax.ShapeDtypeStruct((steps - 1,...  2.29 us
    pallas_call x1, Pallas kernels, on_device(): pl.pallas_call(fetch_kernel, out_shape=(jax.ShapeDtypeStruct((PARTS[2],)...  2.23 us
    pallas_call x1, Pallas kernels, on_device(): pl.pallas_call(functools.partial(readout_kernel, steps, sequence), out_sh...  1.71 us
    pallas_call x1, Pallas kernels, on_device(): pl.pallas_call(functools.partial(prepare_kernel, tiles, paired), out_shap...  1.32 us
  transfers between devices with their start and end apart: 10, of which 4 were waited for; matrix products, arithmetic and copies ran while one was open for 0% of the time, Pallas kernels for 9%

profile of v10, /device:TPU:0, one launch (start us, length us, event | category | flops | bytes accessed | tf_op | source)
XLA Modules:
  0.0 38.4 jit_solution(3643563171000281094)
XLA Ops:
  0.6 2.3 %local_steps.1 = (f32[7,128,128]{2,1,0:T(8,128)S(1)}, bf16[7,256,128]{2,1,0:T(8,128)(2,1)S(1)}, bf16[48,128]{1,0:T(8,128)(2,1)S(1)}, f32[128,128]{1,0:T(8,128)S(...) custom-call(f32[128,128]{1,0:T(8,128)} %v_hbm.1, ...), custom_call_target="tpu_custom_call" | custom-call | tf_op jit(solution)/shard_map/local_steps/pallas_call | solution.py:347
  2.9 2.4 %collective-permute-start.2 = (bf16[48,128]{1,0:T(8,128)(2,1)S(1)}, bf16[48,128]{1,0:T(8,128)(2,1)S(1)}, u32[]{:S(2)}, u32[]{:S(2)}) collective-permute-start(bf16[48,128]{1,0:T(8,128)(2,1)S(1)} %get-tuple-element.26.refs_0_), channel_id=1, source_target_pairs={{0,3},{1,2},{2,1},{3,0},{4,7},{5,6},{6,5},{7,4},{8,11},{9,10},{10,... | collective-permute-start | bytes 36872 | tf_op jit(solution)/shard_map/ppermute | solution.py:327
  5.4 0.6 %collective-permute-start.1 = (bf16[48,128]{1,0:T(8,128)(2,1)S(1)}, bf16[48,128]{1,0:T(8,128)(2,1)S(1)}, u32[]{:S(2)}, u32[]{:S(2)}) collective-permute-start(bf16[48,128]{1,0:T(8,128)(2,1)S(1)} %get-tuple-element.26.refs_0_), channel_id=1, source_target_pairs={{0,2},{1,3},{2,0},{3,1},{4,6},{5,7},{6,4},{7,5},{8,10},{9,11},{10,... | collective-permute-start | bytes 36872 | tf_op jit(solution)/shard_map/ppermute | solution.py:327
  6.0 0.0 collective-permute-start
  6.0 1.3 %prepare_rows.1 = (f32[128,128]{1,0:T(8,128)S(1)}, bf16[256,128]{1,0:T(8,128)(2,1)S(1)}, bf16[128,256]{1,0:T(8,128)(2,1)S(1)}, bf16[32,256]{1,0:T(8,128)(2,1)S(1)}, bf16[16,2,128,128]{3,2,1,0:T(8,128)(2,1)S(1)}) custom-call(f32[7,128,128]{2,1,0:T(8,128)S(1)} %get-tuple-element.27.vloc_ref.refs_4_, f32[128,128]{1,0:T(8,128)S(1)} %get-tuple-element.28.g_ref.refs_7_, ...), custom_call_target="tpu_custom_call" | custom-call | tf_op jit(solution)/shard_map/prepare_rows/pallas_call | solution.py:377
  7.4 0.0 collective-permute-done.2.refs_3_
  7.4 1.7 %collective-permute-done.1.refs_2_ = bf16[48,128]{1,0:T(8,128)(2,1)S(1)} collective-permute-done((bf16[48,128]{1,0:T(8,128)(2,1)S(1)}, bf16[48,128]{1,0:T(8,128)(2,1)S(1)}, u32[]{:S(2)}, u32[]{:S(2)}) %collective-permute-start.1) | collective-permute-done | bytes 12320 | tf_op jit(solution)/shard_map/ppermute | solution.py:327
  9.1 0.0 collective-permute-done.refs_1_
  9.1 0.7 %couple_sections.1 = (f32[128,128]{1,0:T(8,128)S(1)}, bf16[32,1024]{1,0:T(8,128)(2,1)S(1)}, bf16[32,1024]{1,0:T(8,128)(2,1)S(1)}, bf16[32,1024]{1,0:T(8,128)(2,1...) custom-call(bf16[48,128]{1,0:T(8,128)(2,1)S(1)} %get-tuple-element.2, ...), custom_call_target="tpu_custom_call" | custom-call | tf_op jit(solution)/shard_map/couple_sections/pallas_call | solution.py:410
  9.8 3.7 %collective-permute-start.3 = (bf16[32,1024]{1,0:T(8,128)(2,1)S(1)}, bf16[32,1024]{1,0:T(8,128)(2,1)S(1)}, u32[]{:S(2)}, u32[]{:S(2)}) collective-permute-start(bf16[32,1024]{1,0:T(8,128)(2,1)S(1)} %get-tuple-element.40), channel_id=1, source_target_pairs={{0,24},{4,28},{8,16},{12,20},{16,8},{20,12},{24,0},{28,4},{1,25},{... | collective-permute-start | bytes 196616 | tf_op jit(solution)/shard_map/ppermute | solution.py:327
  13.5 1.5 %collective-permute-start.4 = (bf16[32,1024]{1,0:T(8,128)(2,1)S(1)}, bf16[32,1024]{1,0:T(8,128)(2,1)S(1)}, u32[]{:S(2)}, u32[]{:S(2)}) collective-permute-start(bf16[32,1024]{1,0:T(8,128)(2,1)S(1)} %get-tuple-element.41), channel_id=1, source_target_pairs={{0,4},{4,0},{8,12},{12,8},{16,20},{20,16},{24,28},{28,24},{1,5},{5... | collective-permute-start | bytes 196616 | tf_op jit(solution)/shard_map/ppermute | solution.py:327
  15.0 0.2 collective-permute-start.5
  15.2 1.7 %collective-permute-start.6 = (bf16[32,1024]{1,0:T(8,128)(2,1)S(1)}, bf16[32,1024]{1,0:T(8,128)(2,1)S(1)}, u32[]{:S(2)}, u32[]{:S(2)}) collective-permute-start(bf16[32,1024]{1,0:T(8,128)(2,1)S(1)} %get-tuple-element.43), channel_id=1, source_target_pairs={{0,20},{4,16},{8,28},{12,24},{16,4},{20,0},{24,12},{28,8},{1,21},{... | collective-permute-start | bytes 196616 | tf_op jit(solution)/shard_map/ppermute | solution.py:327
  16.9 3.4 %collective-permute-start.7 = (bf16[32,1024]{1,0:T(8,128)(2,1)S(1)}, bf16[32,1024]{1,0:T(8,128)(2,1)S(1)}, u32[]{:S(2)}, u32[]{:S(2)}) collective-permute-start(bf16[32,1024]{1,0:T(8,128)(2,1)S(1)} %get-tuple-element.44), channel_id=1, source_target_pairs={{0,8},{4,12},{8,0},{12,4},{16,24},{20,28},{24,16},{28,20},{1,9},{5... | collective-permute-start | bytes 196616 | tf_op jit(solution)/shard_map/ppermute | solution.py:327
  20.3 0.0 collective-permute-done.3.refs_1_
  20.3 0.6 %collective-permute-start.8 = (bf16[32,1024]{1,0:T(8,128)(2,1)S(1)}, bf16[32,1024]{1,0:T(8,128)(2,1)S(1)}, u32[]{:S(2)}, u32[]{:S(2)}) collective-permute-start(bf16[32,1024]{1,0:T(8,128)(2,1)S(1)} %get-tuple-element.45), channel_id=1, source_target_pairs={{0,16},{4,20},{8,24},{12,28},{16,0},{20,4},{24,8},{28,12},{1,17},{... | collective-permute-start | bytes 196616 | tf_op jit(solution)/shard_map/ppermute | solution.py:327
  20.9 0.0 collective-permute-done.4.refs_2_
  20.9 1.0 %collective-permute-start.9 = (bf16[32,1024]{1,0:T(8,128)(2,1)S(1)}, bf16[32,1024]{1,0:T(8,128)(2,1)S(1)}, u32[]{:S(2)}, u32[]{:S(2)}) collective-permute-start(bf16[32,1024]{1,0:T(8,128)(2,1)S(1)} %get-tuple-element.46), channel_id=1, source_target_pairs={{0,12},{4,8},{8,4},{12,0},{16,28},{20,24},{24,20},{28,16},{1,13},{... | collective-permute-start | bytes 196616 | tf_op jit(solution)/shard_map/ppermute | solution.py:327
  21.9 2.2 %fetch_tiles.1 = (bf16[64,2,128,128]{3,2,1,0:T(8,128)(2,1)S(1)}, f32[128,128]{1,0:T(8,128)}) custom-call(f32[128,128]{1,0:T(8,128)S(1)} %get-tuple-element.35.final_ref, bf16[128,2,128,128]{3,2,1,0:T(8,128)(2,1)} %bitcast.7), custom_call_target="tpu_custom_call" | custom-call | tf_op jit(solution)/shard_map/fetch_tiles/pallas_call | solution.py:442
  24.1 0.0 collective-permute-done.5.refs_3_
  24.1 0.2 collective-permute-done.6.refs_4_
  24.4 0.0 collective-permute-done.7.refs_5_
  24.4 1.2 %collective-permute-done.8.refs_6_ = bf16[32,1024]{1,0:T(8,128)(2,1)S(1)} collective-permute-done((bf16[32,1024]{1,0:T(8,128)(2,1)S(1)}, bf16[32,1024]{1,0:T(8,128)(2,1)S(1)}, u32[]{:S(2)}, u32[]{:S(2)}) %collective-permute-start.8) | collective-permute-done | bytes 65568 | tf_op jit(solution)/shard_map/ppermute | solution.py:327
  25.6 0.9 %collective-permute-done.9.refs_7_ = bf16[32,1024]{1,0:T(8,128)(2,1)S(1)} collective-permute-done((bf16[32,1024]{1,0:T(8,128)(2,1)S(1)}, bf16[32,1024]{1,0:T(8,128)(2,1)S(1)}, u32[]{:S(2)}, u32[]{:S(2)}) %collective-permute-start.9) | collective-permute-done | bytes 65568 | tf_op jit(solution)/shard_map/ppermute | solution.py:327
  26.5 1.7 %readout.1 = bf16[32,8,128]{2,1,0:T(8,128)(2,1)S(1)} custom-call(bf16[32,256]{1,0:T(8,128)(2,1)S(1)} %get-tuple-element.37.select_ref, bf16[128,256]{1,0:T(8,128)(2,1)S(1)} %get-tuple-element.38.order_ref, bf16[32,1024]{1,0:T(8,128)(2,1)S(1)} %get-tuple-element.39.refs_0_, bf16[32,1024]{1,0:T(8,128)(2,1)S(1)} %collective-permute-done.3.refs_1_, ...), custom_call_target="tpu_custom_call" | custom-call | tf_op jit(solution)/shard_map/readout/pallas_call | solution.py:457
  28.2 9.5 %all_to_all.5 = bf16[32,8,128]{2,1,0:T(8,128)(2,1)S(1)} all-to-all(bf16[32,8,128]{2,1,0:T(8,128)(2,1)S(1)} %readout.1), channel_id=1, replica_groups=mesh['tile'=8,'sec'=4] {'tile','sec'}, dimensions={0} | all-to-all | bytes 131072 | tf_op jit(solution)/shard_map/all_to_all | solution.py:477
  37.8 0.6 %convert_reduce_fusion = f32[8,128]{1,0:T(8,128)} fusion(bf16[32,8,128]{2,1,0:T(8,128)(2,1)S(1)} %all_to_all.5), kind=kLoop, calls=%fused_computation | loop fusion | flops 64512 | bytes 69632 | tf_op jit(solution)/shard_map/reduce_sum | solution.py:478
Async XLA Ops:
  2.9 4.5 %collective-permute-start.2 = (bf16[48,128]{1,0:T(8,128)(2,1)S(1)}, bf16[48,128]{1,0:T(8,128)(2,1)S(1)}, u32[]{:S(2)}, u32[]{:S(2)}) collective-permute-start(bf16[48,128]{1,0:T(8,128)(2,1)S(1)} %get-tuple-element.26.refs_0_), channel_id=1, source_target_pairs={{0,3},{1,2},{2,1},{3,0},{4,7},{5,6},{6,5},{7,4},{8,11},{9,10},{10,... | collective-permute-start | bytes 36872 | tf_op jit(solution)/shard_map/ppermute | solution.py:327
  5.4 3.7 %collective-permute-start.1 = (bf16[48,128]{1,0:T(8,128)(2,1)S(1)}, bf16[48,128]{1,0:T(8,128)(2,1)S(1)}, u32[]{:S(2)}, u32[]{:S(2)}) collective-permute-start(bf16[48,128]{1,0:T(8,128)(2,1)S(1)} %get-tuple-element.26.refs_0_), channel_id=1, source_target_pairs={{0,2},{1,3},{2,0},{3,1},{4,6},{5,7},{6,4},{7,5},{8,10},{9,11},{10,... | collective-permute-start | bytes 36872 | tf_op jit(solution)/shard_map/ppermute | solution.py:327
  6.0 3.1 %collective-permute-start = (bf16[48,128]{1,0:T(8,128)(2,1)S(1)}, bf16[48,128]{1,0:T(8,128)(2,1)S(1)}, u32[]{:S(2)}, u32[]{:S(2)}) collective-permute-start(bf16[48,128]{1,0:T(8,128)(2,1)S(1)} %get-tuple-element.26.refs_0_), channel_id=1, source_target_pairs={{0,1},{1,0},{2,3},{3,2},{4,5},{5,4},{6,7},{7,6},{8,9},{9,8},{10,11... | collective-permute-start | bytes 36872 | tf_op jit(solution)/shard_map/ppermute | solution.py:327
  9.8 10.5 %collective-permute-start.3 = (bf16[32,1024]{1,0:T(8,128)(2,1)S(1)}, bf16[32,1024]{1,0:T(8,128)(2,1)S(1)}, u32[]{:S(2)}, u32[]{:S(2)}) collective-permute-start(bf16[32,1024]{1,0:T(8,128)(2,1)S(1)} %get-tuple-element.40), channel_id=1, source_target_pairs={{0,24},{4,28},{8,16},{12,20},{16,8},{20,12},{24,0},{28,4},{1,25},{... | collective-permute-start | bytes 196616 | tf_op jit(solution)/shard_map/ppermute | solution.py:327
  13.5 7.4 %collective-permute-start.4 = (bf16[32,1024]{1,0:T(8,128)(2,1)S(1)}, bf16[32,1024]{1,0:T(8,128)(2,1)S(1)}, u32[]{:S(2)}, u32[]{:S(2)}) collective-permute-start(bf16[32,1024]{1,0:T(8,128)(2,1)S(1)} %get-tuple-element.41), channel_id=1, source_target_pairs={{0,4},{4,0},{8,12},{12,8},{16,20},{20,16},{24,28},{28,24},{1,5},{5... | collective-permute-start | bytes 196616 | tf_op jit(solution)/shard_map/ppermute | solution.py:327
  15.0 9.1 %collective-permute-start.5 = (bf16[32,1024]{1,0:T(8,128)(2,1)S(1)}, bf16[32,1024]{1,0:T(8,128)(2,1)S(1)}, u32[]{:S(2)}, u32[]{:S(2)}) collective-permute-start(bf16[32,1024]{1,0:T(8,128)(2,1)S(1)} %get-tuple-element.42), channel_id=1, source_target_pairs={{0,28},{4,24},{8,20},{12,16},{16,12},{20,8},{24,4},{28,0},{1,29},{... | collective-permute-start | bytes 196616 | tf_op jit(solution)/shard_map/ppermute | solution.py:327
  15.2 9.2 %collective-permute-start.6 = (bf16[32,1024]{1,0:T(8,128)(2,1)S(1)}, bf16[32,1024]{1,0:T(8,128)(2,1)S(1)}, u32[]{:S(2)}, u32[]{:S(2)}) collective-permute-start(bf16[32,1024]{1,0:T(8,128)(2,1)S(1)} %get-tuple-element.43), channel_id=1, source_target_pairs={{0,20},{4,16},{8,28},{12,24},{16,4},{20,0},{24,12},{28,8},{1,21},{... | collective-permute-start | bytes 196616 | tf_op jit(solution)/shard_map/ppermute | solution.py:327
  16.9 7.4 %collective-permute-start.7 = (bf16[32,1024]{1,0:T(8,128)(2,1)S(1)}, bf16[32,1024]{1,0:T(8,128)(2,1)S(1)}, u32[]{:S(2)}, u32[]{:S(2)}) collective-permute-start(bf16[32,1024]{1,0:T(8,128)(2,1)S(1)} %get-tuple-element.44), channel_id=1, source_target_pairs={{0,8},{4,12},{8,0},{12,4},{16,24},{20,28},{24,16},{28,20},{1,9},{5... | collective-permute-start | bytes 196616 | tf_op jit(solution)/shard_map/ppermute | solution.py:327
  20.3 5.3 %collective-permute-start.8 = (bf16[32,1024]{1,0:T(8,128)(2,1)S(1)}, bf16[32,1024]{1,0:T(8,128)(2,1)S(1)}, u32[]{:S(2)}, u32[]{:S(2)}) collective-permute-start(bf16[32,1024]{1,0:T(8,128)(2,1)S(1)} %get-tuple-element.45), channel_id=1, source_target_pairs={{0,16},{4,20},{8,24},{12,28},{16,0},{20,4},{24,8},{28,12},{1,17},{... | collective-permute-start | bytes 196616 | tf_op jit(solution)/shard_map/ppermute | solution.py:327
  20.9 5.7 %collective-permute-start.9 = (bf16[32,1024]{1,0:T(8,128)(2,1)S(1)}, bf16[32,1024]{1,0:T(8,128)(2,1)S(1)}, u32[]{:S(2)}, u32[]{:S(2)}) collective-permute-start(bf16[32,1024]{1,0:T(8,128)(2,1)S(1)} %get-tuple-element.46), channel_id=1, source_target_pairs={{0,12},{4,8},{8,4},{12,0},{16,28},{20,24},{24,20},{28,16},{1,13},{... | collective-permute-start | bytes 196616 | tf_op jit(solution)/shard_map/ppermute | solution.py:327

commit v11 on v9

--- a/solution.py
+++ b/solution.py
@@ -14,7 +14,7 @@
 PAIRED = True
 PARTS = (48, 16, 64)
 SEC_SEQUENCE = (0, 1, 2, 3)
-SEQUENCE = (0, 6, 1, 7, 5, 2, 4, 3)
+SEQUENCE = (0, 6, 3, 7, 5, 2, 4, 1)
 BF = jnp.bfloat16
 F32 = jnp.float32
 PARAMS = pltpu.CompilerParams(vmem_limit_bytes=24 * 1024 * 1024)

time: 38.6 us -> 38.6 us (level)
  starting transfers between devices: 15.2 us -> 14.2 us
  blocking collectives: 9.62 us -> 10.1 us
  waiting for transfers between devices: 4.07 us -> 4.49 us
    ppermute x10, starting transfers between devices: 15.2 us -> 14.2 us  [exchange(): lax.ppermute(blocks[p], axis, [(i, i ^ p) for i in range(count)])]
    all_to_all x1, blocking collectives: 9.62 us -> 10.1 us  [on_device(): lax.all_to_all(partial_sum, ('tile', 'sec'), split_axis=0, concat_axis=0,...]
    ppermute x10, waiting for transfers between devices: 4.07 us -> 4.49 us  [exchange(): lax.ppermute(blocks[p], axis, [(i, i ^ p) for i in range(count)])]
  transfers between devices with their start and end apart: 10 -> 10, of which waited for: 4 -> 2; matrix products, arithmetic and copies ran while one was open for 0% -> 0% of each run, Pallas kernels for 9% -> 9%
where the time goes in v11:
time: 38.6 us; the launch traced here: 38.4 us
  starting transfers between devices  14.2 us (37%)
  blocking collectives  10.1 us (26%)
  Pallas kernels  8.26 us (21%)
  waiting for transfers between devices  4.49 us (12%)
  between operations  0.69 us (2%)
  other arithmetic  0.63 us (2%)
    ppermute x10, starting transfers between devices, exchange(): lax.ppermute(blocks[p], axis, [(i, i ^ p) for i in range(count)])  14.2 us
    all_to_all x1, blocking collectives, on_device(): lax.all_to_all(partial_sum, ('tile', 'sec'), split_axis=0, concat_axis=0,...  10.1 us
    ppermute x10, waiting for transfers between devices, exchange(): lax.ppermute(blocks[p], axis, [(i, i ^ p) for i in range(count)])  4.49 us
    pallas_call x1, Pallas kernels, on_device(): pl.pallas_call(local_kernel, out_shape=(jax.ShapeDtypeStruct((steps - 1,...  2.25 us
    pallas_call x1, Pallas kernels, on_device(): pl.pallas_call(fetch_kernel, out_shape=(jax.ShapeDtypeStruct((PARTS[2],)...  2.23 us
    pallas_call x1, Pallas kernels, on_device(): pl.pallas_call(functools.partial(readout_kernel, steps, sequence), out_sh...  1.71 us
    pallas_call x1, Pallas kernels, on_device(): pl.pallas_call(functools.partial(prepare_kernel, tiles, paired), out_shap...  1.32 us
  transfers between devices with their start and end apart: 10, of which 2 were waited for; matrix products, arithmetic and copies ran while one was open for 0% of the time, Pallas kernels for 9%

profile of v11, /device:TPU:0, one launch (start us, length us, event | category | flops | bytes accessed | tf_op | source)
XLA Modules:
  0.0 38.4 jit_solution(1719120384172130288)
XLA Ops:
  0.6 2.2 %local_steps.1 = (f32[7,128,128]{2,1,0:T(8,128)S(1)}, bf16[7,256,128]{2,1,0:T(8,128)(2,1)S(1)}, bf16[48,128]{1,0:T(8,128)(2,1)S(1)}, f32[128,128]{1,0:T(8,128)S(...) custom-call(f32[128,128]{1,0:T(8,128)} %v_hbm.1, ...), custom_call_target="tpu_custom_call" | custom-call | tf_op jit(solution)/shard_map/local_steps/pallas_call | solution.py:343
  2.9 2.4 %collective-permute-start.2 = (bf16[48,128]{1,0:T(8,128)(2,1)S(1)}, bf16[48,128]{1,0:T(8,128)(2,1)S(1)}, u32[]{:S(2)}, u32[]{:S(2)}) collective-permute-start(bf16[48,128]{1,0:T(8,128)(2,1)S(1)} %get-tuple-element.26.refs_0_), channel_id=1, source_target_pairs={{0,3},{1,2},{2,1},{3,0},{4,7},{5,6},{6,5},{7,4},{8,11},{9,10},{10,... | collective-permute-start | bytes 36872 | tf_op jit(solution)/shard_map/ppermute | solution.py:323
  5.3 0.6 %collective-permute-start.1 = (bf16[48,128]{1,0:T(8,128)(2,1)S(1)}, bf16[48,128]{1,0:T(8,128)(2,1)S(1)}, u32[]{:S(2)}, u32[]{:S(2)}) collective-permute-start(bf16[48,128]{1,0:T(8,128)(2,1)S(1)} %get-tuple-element.26.refs_0_), channel_id=1, source_target_pairs={{0,2},{1,3},{2,0},{3,1},{4,6},{5,7},{6,4},{7,5},{8,10},{9,11},{10,... | collective-permute-start | bytes 36872 | tf_op jit(solution)/shard_map/ppermute | solution.py:323
  6.0 0.0 collective-permute-start
  6.0 1.3 %prepare_rows.1 = (f32[128,128]{1,0:T(8,128)S(1)}, bf16[256,128]{1,0:T(8,128)(2,1)S(1)}, bf16[128,256]{1,0:T(8,128)(2,1)S(1)}, bf16[32,256]{1,0:T(8,128)(2,1)S(1)}, bf16[16,2,128,128]{3,2,1,0:T(8,128)(2,1)S(1)}) custom-call(f32[7,128,128]{2,1,0:T(8,128)S(1)} %get-tuple-element.27.vloc_ref.refs_4_, f32[128,128]{1,0:T(8,128)S(1)} %get-tuple-element.28.g_ref.refs_7_, ...), custom_call_target="tpu_custom_call" | custom-call | tf_op jit(solution)/shard_map/prepare_rows/pallas_call | solution.py:373
  7.3 0.0 collective-permute-done.2.refs_3_
  7.4 1.7 %collective-permute-done.1.refs_2_ = bf16[48,128]{1,0:T(8,128)(2,1)S(1)} collective-permute-done((bf16[48,128]{1,0:T(8,128)(2,1)S(1)}, bf16[48,128]{1,0:T(8,128)(2,1)S(1)}, u32[]{:S(2)}, u32[]{:S(2)}) %collective-permute-start.1) | collective-permute-done | bytes 12320 | tf_op jit(solution)/shard_map/ppermute | solution.py:323
  9.0 0.0 collective-permute-done.refs_1_
  9.0 0.7 %couple_sections.1 = (f32[128,128]{1,0:T(8,128)S(1)}, bf16[32,1024]{1,0:T(8,128)(2,1)S(1)}, bf16[32,1024]{1,0:T(8,128)(2,1)S(1)}, bf16[32,1024]{1,0:T(8,128)(2,1...) custom-call(bf16[48,128]{1,0:T(8,128)(2,1)S(1)} %get-tuple-element.2, ...), custom_call_target="tpu_custom_call" | custom-call | tf_op jit(solution)/shard_map/couple_sections/pallas_call | solution.py:406
  9.8 3.7 %collective-permute-start.3 = (bf16[32,1024]{1,0:T(8,128)(2,1)S(1)}, bf16[32,1024]{1,0:T(8,128)(2,1)S(1)}, u32[]{:S(2)}, u32[]{:S(2)}) collective-permute-start(bf16[32,1024]{1,0:T(8,128)(2,1)S(1)} %get-tuple-element.40), channel_id=1, source_target_pairs={{0,24},{4,28},{8,16},{12,20},{16,8},{20,12},{24,0},{28,4},{1,25},{... | collective-permute-start | bytes 196616 | tf_op jit(solution)/shard_map/ppermute | solution.py:323
  13.5 0.5 %collective-permute-start.4 = (bf16[32,1024]{1,0:T(8,128)(2,1)S(1)}, bf16[32,1024]{1,0:T(8,128)(2,1)S(1)}, u32[]{:S(2)}, u32[]{:S(2)}) collective-permute-start(bf16[32,1024]{1,0:T(8,128)(2,1)S(1)} %get-tuple-element.41), channel_id=1, source_target_pairs={{0,12},{4,8},{8,4},{12,0},{16,28},{20,24},{24,20},{28,16},{1,13},{... | collective-permute-start | bytes 196616 | tf_op jit(solution)/shard_map/ppermute | solution.py:323
  14.0 1.3 %collective-permute-start.5 = (bf16[32,1024]{1,0:T(8,128)(2,1)S(1)}, bf16[32,1024]{1,0:T(8,128)(2,1)S(1)}, u32[]{:S(2)}, u32[]{:S(2)}) collective-permute-start(bf16[32,1024]{1,0:T(8,128)(2,1)S(1)} %get-tuple-element.42), channel_id=1, source_target_pairs={{0,28},{4,24},{8,20},{12,16},{16,12},{20,8},{24,4},{28,0},{1,29},{... | collective-permute-start | bytes 196616 | tf_op jit(solution)/shard_map/ppermute | solution.py:323
  15.2 3.5 %collective-permute-start.6 = (bf16[32,1024]{1,0:T(8,128)(2,1)S(1)}, bf16[32,1024]{1,0:T(8,128)(2,1)S(1)}, u32[]{:S(2)}, u32[]{:S(2)}) collective-permute-start(bf16[32,1024]{1,0:T(8,128)(2,1)S(1)} %get-tuple-element.43), channel_id=1, source_target_pairs={{0,20},{4,16},{8,28},{12,24},{16,4},{20,0},{24,12},{28,8},{1,21},{... | collective-permute-start | bytes 196616 | tf_op jit(solution)/shard_map/ppermute | solution.py:323
  18.8 0.4 %collective-permute-start.7 = (bf16[32,1024]{1,0:T(8,128)(2,1)S(1)}, bf16[32,1024]{1,0:T(8,128)(2,1)S(1)}, u32[]{:S(2)}, u32[]{:S(2)}) collective-permute-start(bf16[32,1024]{1,0:T(8,128)(2,1)S(1)} %get-tuple-element.44), channel_id=1, source_target_pairs={{0,8},{4,12},{8,0},{12,4},{16,24},{20,28},{24,16},{28,20},{1,9},{5... | collective-permute-start | bytes 196616 | tf_op jit(solution)/shard_map/ppermute | solution.py:323
  19.2 0.0 collective-permute-done.3.refs_1_
  19.2 0.3 collective-permute-start.8
  19.6 0.0 collective-permute-done.4.refs_2_
  19.6 1.3 %collective-permute-start.9 = (bf16[32,1024]{1,0:T(8,128)(2,1)S(1)}, bf16[32,1024]{1,0:T(8,128)(2,1)S(1)}, u32[]{:S(2)}, u32[]{:S(2)}) collective-permute-start(bf16[32,1024]{1,0:T(8,128)(2,1)S(1)} %get-tuple-element.46), channel_id=1, source_target_pairs={{0,4},{4,0},{8,12},{12,8},{16,20},{20,16},{24,28},{28,24},{1,5},{5... | collective-permute-start | bytes 196616 | tf_op jit(solution)/shard_map/ppermute | solution.py:323
  20.9 2.2 %fetch_tiles.1 = (bf16[64,2,128,128]{3,2,1,0:T(8,128)(2,1)S(1)}, f32[128,128]{1,0:T(8,128)}) custom-call(f32[128,128]{1,0:T(8,128)S(1)} %get-tuple-element.35.final_ref, bf16[128,2,128,128]{3,2,1,0:T(8,128)(2,1)} %bitcast.7), custom_call_target="tpu_custom_call" | custom-call | tf_op jit(solution)/shard_map/fetch_tiles/pallas_call | solution.py:438
  23.1 0.0 collective-permute-done.5.refs_3_
  23.2 2.8 %collective-permute-done.6.refs_4_ = bf16[32,1024]{1,0:T(8,128)(2,1)S(1)} collective-permute-done((bf16[32,1024]{1,0:T(8,128)(2,1)S(1)}, bf16[32,1024]{1,0:T(8,128)(2,1)S(1)}, u32[]{:S(2)}, u32[]{:S(2)}) %collective-permute-start.6) | collective-permute-done | bytes 65568 | tf_op jit(solution)/shard_map/ppermute | solution.py:323
  26.0 0.0 collective-permute-done.7.refs_5_
  26.0 0.0 collective-permute-done.8.refs_6_
  26.0 0.0 collective-permute-done.9.refs_7_
  26.0 1.7 %readout.1 = bf16[32,8,128]{2,1,0:T(8,128)(2,1)S(1)} custom-call(bf16[32,256]{1,0:T(8,128)(2,1)S(1)} %get-tuple-element.37.select_ref, bf16[128,256]{1,0:T(8,128)(2,1)S(1)} %get-tuple-element.38.order_ref, bf16[32,1024]{1,0:T(8,128)(2,1)S(1)} %get-tuple-element.39.refs_0_, bf16[32,1024]{1,0:T(8,128)(2,1)S(1)} %collective-permute-done.3.refs_1_, ...), custom_call_target="tpu_custom_call" | custom-call | tf_op jit(solution)/shard_map/readout/pallas_call | solution.py:453
  27.7 10.1 %all_to_all.5 = bf16[32,8,128]{2,1,0:T(8,128)(2,1)S(1)} all-to-all(bf16[32,8,128]{2,1,0:T(8,128)(2,1)S(1)} %readout.1), channel_id=1, replica_groups=mesh['tile'=8,'sec'=4] {'tile','sec'}, dimensions={0} | all-to-all | bytes 131072 | tf_op jit(solution)/shard_map/all_to_all | solution.py:473
  37.8 0.6 %convert_reduce_fusion = f32[8,128]{1,0:T(8,128)} fusion(bf16[32,8,128]{2,1,0:T(8,128)(2,1)S(1)} %all_to_all.5), kind=kLoop, calls=%fused_computation | loop fusion | flops 64512 | bytes 69632 | tf_op jit(solution)/shard_map/reduce_sum | solution.py:474
Async XLA Ops:
  2.9 4.5 %collective-permute-start.2 = (bf16[48,128]{1,0:T(8,128)(2,1)S(1)}, bf16[48,128]{1,0:T(8,128)(2,1)S(1)}, u32[]{:S(2)}, u32[]{:S(2)}) collective-permute-start(bf16[48,128]{1,0:T(8,128)(2,1)S(1)} %get-tuple-element.26.refs_0_), channel_id=1, source_target_pairs={{0,3},{1,2},{2,1},{3,0},{4,7},{5,6},{6,5},{7,4},{8,11},{9,10},{10,... | collective-permute-start | bytes 36872 | tf_op jit(solution)/shard_map/ppermute | solution.py:323
  5.3 3.7 %collective-permute-start.1 = (bf16[48,128]{1,0:T(8,128)(2,1)S(1)}, bf16[48,128]{1,0:T(8,128)(2,1)S(1)}, u32[]{:S(2)}, u32[]{:S(2)}) collective-permute-start(bf16[48,128]{1,0:T(8,128)(2,1)S(1)} %get-tuple-element.26.refs_0_), channel_id=1, source_target_pairs={{0,2},{1,3},{2,0},{3,1},{4,6},{5,7},{6,4},{7,5},{8,10},{9,11},{10,... | collective-permute-start | bytes 36872 | tf_op jit(solution)/shard_map/ppermute | solution.py:323
  6.0 3.1 %collective-permute-start = (bf16[48,128]{1,0:T(8,128)(2,1)S(1)}, bf16[48,128]{1,0:T(8,128)(2,1)S(1)}, u32[]{:S(2)}, u32[]{:S(2)}) collective-permute-start(bf16[48,128]{1,0:T(8,128)(2,1)S(1)} %get-tuple-element.26.refs_0_), channel_id=1, source_target_pairs={{0,1},{1,0},{2,3},{3,2},{4,5},{5,4},{6,7},{7,6},{8,9},{9,8},{10,11... | collective-permute-start | bytes 36872 | tf_op jit(solution)/shard_map/ppermute | solution.py:323
  9.8 9.5 %collective-permute-start.3 = (bf16[32,1024]{1,0:T(8,128)(2,1)S(1)}, bf16[32,1024]{1,0:T(8,128)(2,1)S(1)}, u32[]{:S(2)}, u32[]{:S(2)}) collective-permute-start(bf16[32,1024]{1,0:T(8,128)(2,1)S(1)} %get-tuple-element.40), channel_id=1, source_target_pairs={{0,24},{4,28},{8,16},{12,20},{16,8},{20,12},{24,0},{28,4},{1,25},{... | collective-permute-start | bytes 196616 | tf_op jit(solution)/shard_map/ppermute | solution.py:323
  13.5 6.1 %collective-permute-start.4 = (bf16[32,1024]{1,0:T(8,128)(2,1)S(1)}, bf16[32,1024]{1,0:T(8,128)(2,1)S(1)}, u32[]{:S(2)}, u32[]{:S(2)}) collective-permute-start(bf16[32,1024]{1,0:T(8,128)(2,1)S(1)} %get-tuple-element.41), channel_id=1, source_target_pairs={{0,12},{4,8},{8,4},{12,0},{16,28},{20,24},{24,20},{28,16},{1,13},{... | collective-permute-start | bytes 196616 | tf_op jit(solution)/shard_map/ppermute | solution.py:323
  14.0 9.2 %collective-permute-start.5 = (bf16[32,1024]{1,0:T(8,128)(2,1)S(1)}, bf16[32,1024]{1,0:T(8,128)(2,1)S(1)}, u32[]{:S(2)}, u32[]{:S(2)}) collective-permute-start(bf16[32,1024]{1,0:T(8,128)(2,1)S(1)} %get-tuple-element.42), channel_id=1, source_target_pairs={{0,28},{4,24},{8,20},{12,16},{16,12},{20,8},{24,4},{28,0},{1,29},{... | collective-permute-start | bytes 196616 | tf_op jit(solution)/shard_map/ppermute | solution.py:323
  15.2 10.7 %collective-permute-start.6 = (bf16[32,1024]{1,0:T(8,128)(2,1)S(1)}, bf16[32,1024]{1,0:T(8,128)(2,1)S(1)}, u32[]{:S(2)}, u32[]{:S(2)}) collective-permute-start(bf16[32,1024]{1,0:T(8,128)(2,1)S(1)} %get-tuple-element.43), channel_id=1, source_target_pairs={{0,20},{4,16},{8,28},{12,24},{16,4},{20,0},{24,12},{28,8},{1,21},{... | collective-permute-start | bytes 196616 | tf_op jit(solution)/shard_map/ppermute | solution.py:323
  18.8 7.2 %collective-permute-start.7 = (bf16[32,1024]{1,0:T(8,128)(2,1)S(1)}, bf16[32,1024]{1,0:T(8,128)(2,1)S(1)}, u32[]{:S(2)}, u32[]{:S(2)}) collective-permute-start(bf16[32,1024]{1,0:T(8,128)(2,1)S(1)} %get-tuple-element.44), channel_id=1, source_target_pairs={{0,8},{4,12},{8,0},{12,4},{16,24},{20,28},{24,16},{28,20},{1,9},{5... | collective-permute-start | bytes 196616 | tf_op jit(solution)/shard_map/ppermute | solution.py:323
  19.2 6.7 %collective-permute-start.8 = (bf16[32,1024]{1,0:T(8,128)(2,1)S(1)}, bf16[32,1024]{1,0:T(8,128)(2,1)S(1)}, u32[]{:S(2)}, u32[]{:S(2)}) collective-permute-start(bf16[32,1024]{1,0:T(8,128)(2,1)S(1)} %get-tuple-element.45), channel_id=1, source_target_pairs={{0,16},{4,20},{8,24},{12,28},{16,0},{20,4},{24,8},{28,12},{1,17},{... | collective-permute-start | bytes 196616 | tf_op jit(solution)/shard_map/ppermute | solution.py:323
  19.6 6.4 %collective-permute-start.9 = (bf16[32,1024]{1,0:T(8,128)(2,1)S(1)}, bf16[32,1024]{1,0:T(8,128)(2,1)S(1)}, u32[]{:S(2)}, u32[]{:S(2)}) collective-permute-start(bf16[32,1024]{1,0:T(8,128)(2,1)S(1)} %get-tuple-element.46), channel_id=1, source_target_pairs={{0,4},{4,0},{8,12},{12,8},{16,20},{20,16},{24,28},{28,24},{1,5},{5... | collective-permute-start | bytes 196616 | tf_op jit(solution)/shard_map/ppermute | solution.py:323
